TPU v7x, 32 devices: a whole 2x2x4 slice. The times are simulated.
32 devices in a mesh: rep: 2 (over y), grp: 4 (over z), tp: 4 (over x, core).
Axes of the slice: x: 2, y: 2, z: 4, core: 2. Of those that a mesh axis runs over, the one named last changes fastest.
Arguments:
- activations: bfloat16 [6, 32, 20, 8192], P('rep', 'grp', None, 'tp'), parts along dimension 0, may hold values from -6 to 6
- cotangent: bfloat16 [6, 32, 20, 8192], P('rep', 'grp', None, 'tp'), parts along dimension 0, may hold values from -6 to 6
- frozen_weight_matrix: bfloat16 [8192, 8192], P('tp'), may hold values from -0.0625 to 0.0625
- adapter_down_weights: bfloat16 [64, 8192, 128], P(('rep', 'grp'), 'tp'), parts along dimension 0, may hold values from -0.5 to 0.5
- adapter_up_weights: bfloat16 [64, 128, 8192], P(('rep', 'grp'), None, 'tp'), parts along dimension 0, may hold values from -0.0625 to 0.0625
- window_adapter: int32 [6, 32], P('rep', 'grp'), parts along dimension 0, may hold values from 0 to 31, as said below
- window_live_rows: int32 [6, 32], P('rep', 'grp'), parts along dimension 0, may hold values from 1 to 20, as said below
- rank_per_adapter: int32 [64], P('rep'), parts along dimension 0, may hold values from 16 to 128, as said below
- slot_per_adapter: int32 [64], P('rep'), parts along dimension 0, may hold values from 0 to 31, as said below
Outputs:
- input_grad: bfloat16 [6, 32, 20, 8192], P('rep', 'grp', None, 'tp'), parts along dimension 0
- grad_down: bfloat16 [64, 8192, 128], P(('rep', 'grp'), 'tp'), parts along dimension 0
- grad_up: bfloat16 [64, 128, 8192], P(('rep', 'grp'), None, 'tp'), parts along dimension 0
There are 2 independent parts, one for each index of `rep`. A program takes and returns all parts, laid end to end along the dimension named above; an argument that names none is the same for every part. Nothing has to cross between parts.
Inputs may be any that keep to these rules, and one draw needn't show every extreme that they name: `window_adapter`: in each microstep, at most 2 of one group's 8 windows name adapters whose slots lie in one owner group's block of 8 slots (owner = slot_per_adapter[a] // 8); in every microstep some owner group gets exactly 2 windows from every group. `window_live_rows`: the first of each group's 8 windows in a microstep has all rows live. `rank_per_adapter`: each rank is 128 divided by 8, 4, 2 or 1, and each of these values is held by a quarter of the 32 adapters. `slot_per_adapter`: A permutation of the 32 slots.
All inputs are finite; a program needn't handle non-finite values. Where the computation divides by a largest or mean magnitude, that divisor is 1e-20 or more.
Results may differ from a plain program's by a relative error of at most 0.0051.
Values may be sent and summed in bfloat16 or wider, within the bound.
No kernel may reach another device: no remote copies, remote signals or barrier semaphores. Data moves between devices by JAX's collectives and lax.ppermute only.
A program may use at most 192 MiB of HBM per device.

v0:
```python
import jax
import jax.numpy as jnp
from jax import lax
from jax.sharding import PartitionSpec as P

WINDOWS_PER_OWNER = 2


grad_limit = 4.0


def fold_columns(frozen_weight_matrix, gathered):
    return lax.dot_general(
        gathered, frozen_weight_matrix, (((1,), (1,)), ((), ())), preferred_element_type=jnp.float32
    )


def lowrank_product(
    acts_items, masked_items, slot_picks, lane_scale, down_adapter_matrix, up_adapter_matrix
):
    down_sel = jnp.einsum(
        "ne,ewr->nwr", slot_picks, down_adapter_matrix, preferred_element_type=jnp.float32
    ).astype(jnp.bfloat16)
    up_sel = jnp.einsum(
        "ne,erw->nrw", slot_picks, up_adapter_matrix, preferred_element_type=jnp.float32
    ).astype(jnp.bfloat16)
    down_part = jnp.einsum("npw,nwr->npr", acts_items, down_sel, preferred_element_type=jnp.float32)
    up_part = jnp.einsum("npw,nrw->npr", masked_items, up_sel, preferred_element_type=jnp.float32)
    down_gradient_total, up_gradient_total = lax.psum((down_part, up_part), "tp")
    lifted = (down_gradient_total * lane_scale[:, None, :]).astype(jnp.bfloat16)
    lowered_program = (up_gradient_total * lane_scale[:, None, :]).astype(jnp.bfloat16)
    item_count, token_row_count, feature_width = acts_items.shape
    table_slot_count = slot_picks.shape[1]
    rank_limit_value = lane_scale.shape[1]
    spread_lift = (lifted[:, :, None, :] * slot_picks[:, None, :, None]).reshape(
        item_count * token_row_count, table_slot_count * rank_limit_value
    )
    spread_low = (lowered_program[:, :, None, :] * slot_picks[:, None, :, None]).reshape(
        item_count * token_row_count, table_slot_count * rank_limit_value
    )
    contract = (((0,), (0,)), ((), ()))
    up_gradient_step = lax.dot_general(
        spread_lift,
        masked_items.reshape(item_count * token_row_count, feature_width),
        contract,
        preferred_element_type=jnp.float32,
    )
    down_gradient_step = lax.dot_general(
        acts_items.reshape(item_count * token_row_count, feature_width),
        spread_low,
        contract,
        preferred_element_type=jnp.float32,
    )
    adapter_result = jnp.einsum(
        "npr,nwr->npw", lowered_program, down_sel, preferred_element_type=jnp.float32
    ).astype(jnp.bfloat16)
    return (down_gradient_step, up_gradient_step, adapter_result)


def local(
    activations,
    cotangent,
    frozen_weight_matrix,
    adapter_down_weights,
    adapter_up_weights,
    window_adapter,
    window_live_rows,
    rank_per_adapter,
    slot_per_adapter,
):
    micro_iterations, window_count, token_row_count, feature_width = activations.shape
    owner_group_count = lax.axis_size("grp")
    table_slot_count = adapter_down_weights.shape[0]
    rank_limit_value = adapter_down_weights.shape[2]
    adapters = slot_per_adapter.shape[0]
    live_rows = (jnp.arange(token_row_count)[None, None, :] < window_live_rows[:, :, None]).astype(
        jnp.bfloat16
    )
    masked = cotangent * live_rows[:, :, :, None]
    flat_masked = masked.reshape(micro_iterations * window_count * token_row_count, feature_width)
    frozen_weight_gradient = fold_columns(
        frozen_weight_matrix, lax.all_gather(flat_masked, "tp", axis=1, tiled=True)
    )
    chosen = window_adapter[:, :, None] == jnp.arange(adapters)[None, None, :]
    slot_of = jnp.sum(jnp.where(chosen, slot_per_adapter[None, None, :], 0), axis=2)
    rank_of = jnp.sum(jnp.where(chosen, rank_per_adapter[None, None, :], 0), axis=2)
    scale_of = rank_limit_value // 8 / rank_of.astype(jnp.float32)
    lanes = jnp.where(
        jnp.arange(rank_limit_value)[None, None, :] < rank_of[:, :, None], scale_of[:, :, None], 0.0
    )
    owner_group = slot_of // table_slot_count
    local_slot = slot_of % table_slot_count
    same_owner = owner_group[:, :, None] == owner_group[:, None, :]
    earlier = jnp.arange(window_count)[None, :] < jnp.arange(window_count)[:, None]
    before = jnp.sum(jnp.logical_and(same_owner, earlier[None, :, :]).astype(jnp.int32), axis=2)
    target = owner_group * WINDOWS_PER_OWNER + before
    placing = (
        jnp.arange(owner_group_count * WINDOWS_PER_OWNER)[None, :, None] == target[:, None, :]
    ).astype(jnp.bfloat16)
    local_pick = (local_slot[:, :, None] == jnp.arange(table_slot_count)[None, None, :]).astype(
        jnp.bfloat16
    )

    def pack_rows(values):
        return jnp.einsum(
            "msj,mjf->smf", placing, values, preferred_element_type=jnp.float32
        ).astype(jnp.bfloat16)

    send_acts = pack_rows(
        activations.reshape(micro_iterations, window_count, token_row_count * feature_width)
    ).reshape(
        owner_group_count, WINDOWS_PER_OWNER, micro_iterations, token_row_count, feature_width
    )
    send_masked = pack_rows(
        masked.reshape(micro_iterations, window_count, token_row_count * feature_width)
    ).reshape(
        owner_group_count, WINDOWS_PER_OWNER, micro_iterations, token_row_count, feature_width
    )
    send_picks = pack_rows(local_pick).reshape(
        owner_group_count, WINDOWS_PER_OWNER, micro_iterations, table_slot_count
    )
    send_lanes = pack_rows(lanes.astype(jnp.bfloat16)).reshape(
        owner_group_count, WINDOWS_PER_OWNER, micro_iterations, rank_limit_value
    )
    down_acc = jnp.zeros((feature_width, table_slot_count * rank_limit_value), jnp.float32)
    up_acc = jnp.zeros((table_slot_count * rank_limit_value, feature_width), jnp.float32)
    returns = []
    item_count = owner_group_count * WINDOWS_PER_OWNER
    for micro_step in range(micro_iterations):
        arrived = (
            lax.all_to_all(
                send_acts[:, :, micro_step], "grp", split_axis=0, concat_axis=0, tiled=True
            ),
            lax.all_to_all(
                send_masked[:, :, micro_step], "grp", split_axis=0, concat_axis=0, tiled=True
            ),
            lax.all_to_all(
                send_picks[:, :, micro_step], "grp", split_axis=0, concat_axis=0, tiled=True
            ),
            lax.all_to_all(
                send_lanes[:, :, micro_step], "grp", split_axis=0, concat_axis=0, tiled=True
            ),
        )
        down_gradient_step, up_gradient_step, adapter_result = lowrank_product(
            arrived[0].reshape(item_count, token_row_count, feature_width),
            arrived[1].reshape(item_count, token_row_count, feature_width),
            arrived[2].reshape(item_count, table_slot_count),
            arrived[3].reshape(item_count, rank_limit_value).astype(jnp.float32),
            adapter_down_weights,
            adapter_up_weights,
        )
        down_acc = down_acc + down_gradient_step
        up_acc = up_acc + up_gradient_step
        returns.append(
            lax.all_to_all(
                adapter_result.reshape(
                    owner_group_count, WINDOWS_PER_OWNER, token_row_count, feature_width
                ),
                "grp",
                split_axis=0,
                concat_axis=0,
                tiled=True,
            )
        )
    returned = jnp.stack(returns, axis=2)
    adapter_backward = jnp.einsum(
        "msj,smf->mjf",
        placing,
        returned.reshape(
            owner_group_count * WINDOWS_PER_OWNER, micro_iterations, token_row_count * feature_width
        ),
        preferred_element_type=jnp.float32,
    )
    adapter_backward = adapter_backward.reshape(
        micro_iterations, window_count, token_row_count, feature_width
    )
    grad_down = down_acc.reshape(feature_width, table_slot_count, rank_limit_value).transpose(
        1, 0, 2
    )
    grad_up = up_acc.reshape(table_slot_count, rank_limit_value, feature_width)
    input_grad = (
        frozen_weight_gradient.reshape(
            micro_iterations, window_count, token_row_count, feature_width
        )
        + adapter_backward
    ).astype(jnp.bfloat16)
    largest = jnp.maximum(jnp.max(jnp.abs(grad_down)), jnp.max(jnp.abs(grad_up)))
    highest = lax.pmax(largest, ("grp", "tp"))
    factor = grad_limit / jnp.maximum(highest, grad_limit)
    return (
        input_grad,
        (grad_down * factor).astype(jnp.bfloat16),
        (grad_up * factor).astype(jnp.bfloat16),
    )


def solution(mesh):
    return jax.shard_map(
        local,
        mesh=mesh,
        in_specs=(
            P("rep", "grp", None, "tp"),
            P("rep", "grp", None, "tp"),
            P("tp", None),
            P(("rep", "grp"), "tp", None),
            P(("rep", "grp"), None, "tp"),
            P("rep", "grp"),
            P("rep", "grp"),
            P("rep"),
            P("rep"),
        ),
        out_specs=(
            P("rep", "grp", None, "tp"),
            P(("rep", "grp"), "tp", None),
            P(("rep", "grp"), None, "tp"),
        ),
        check_vma=False,
    )
```

profile of v0, /device:TPU:0, one launch (start us, length us, event | category | flops | bytes accessed | tf_op | source)
XLA Modules:
  0.0 373.9 jit_solution(12376099641673036163)
XLA Ops:
  9.9 6.3 %all-to-all-start.9 = ((bf16[4,2,8]{2,1,0:T(2,128)(2,1)}), bf16[4,2,8]{2,1,0:T(2,128)(2,1)S(1)}, u32[]{:S(2)}, u32[]{:S(2)}) async-start(bf16[4,2,8]{2,1,0:T(2,128)(2,1)} %get-tuple-element.30), calls=%async_computation.9 | async-start | bytes 4096 | tf_op jit(solution)/shard_map/all_to_all | solution.py:137
  16.9 3.0 broadcast_multiply_fusion
  21.7 3.3 all-to-all-start.5
  25.1 3.5 fusion
  28.5 4.3 %reshape.277 = bf16[4,2,3,20,2048]{4,3,1,0,2:T(8,128)(2,1)} reshape(bf16[8,3,40960]{2,0,1:T(8,128)(2,1)} %fusion) | data formatting | bytes 3932160 | tf_op jit(solution)/shard_map/reshape | solution.py:116
  32.8 5.1 %all-to-all-start.1 = ((bf16[4,2,8]{2,1,0:T(2,128)(2,1)}), bf16[4,2,8]{2,1,0:T(2,128)(2,1)S(1)}, u32[]{:S(2)}, u32[]{:S(2)}) async-start(bf16[4,2,8]{2,1,0:T(2,128)(2,1)} %get-tuple-element.29), calls=%async_computation.1 | async-start | bytes 4096 | tf_op jit(solution)/shard_map/all_to_all | solution.py:137
  43.3 4.2 %all-to-all-start.8 = ((bf16[4,2,20,2048]{3,1,2,0:T(2,128)(2,1)}), bf16[4,2,20,2048]{3,1,2,0:T(2,128)(2,1)}, u32[]{:S(2)}, u32[]{:S(2)}) async-start(bf16[4,2,20,2048]{3,1,2,0:T(2,128)(2,1)} %copy.105), calls=%async_computation.8 | async-start | bytes 1310720 | tf_op jit(solution)/shard_map/all_to_all | solution.py:134
  49.0 13.7 %all-to-all-done.8 = bf16[4,2,20,2048]{3,1,2,0:T(2,128)(2,1)} async-done(((bf16[4,2,20,2048]{3,1,2,0:T(2,128)(2,1)}), bf16[4,2,20,2048]{3,1,2,0:T(2,128)(2,1)}, u32[]{:S(2)}, u32[]{:S(2)}) %all-to-all-start.8) | async-done | bytes 655392 | tf_op jit(solution)/shard_map/all_to_all | solution.py:134
  62.7 3.5 all-to-all-start.4
  69.7 4.3 %reshape.291 = bf16[4,2,3,20,2048]{4,3,1,0,2:T(8,128)(2,1)} reshape(bf16[8,3,40960]{2,0,1:T(8,128)(2,1)} %fusion.1) | data formatting | bytes 3932160 | tf_op jit(solution)/shard_map/reshape | solution.py:111
  73.9 8.0 %all-to-all-done.4 = bf16[4,2,20,2048]{3,1,2,0:T(2,128)(2,1)S(1)} async-done(((bf16[4,2,20,2048]{3,1,2,0:T(2,128)(2,1)}), bf16[4,2,20,2048]{3,1,2,0:T(2,128)(2,1)S(1)}, u32[]{:S(2)}, u32[]{:S(2)}) %all-to-all-start.4) | async-done | bytes 655392 | tf_op jit(solution)/shard_map/all_to_all | solution.py:134
  81.9 3.8 %all-to-all-start = ((bf16[4,2,20,2048]{3,1,2,0:T(2,128)(2,1)}), bf16[4,2,20,2048]{3,1,2,0:T(2,128)(2,1)S(1)}, u32[]{:S(2)}, u32[]{:S(2)}) async-start(bf16[4,2,20,2048]{3,1,2,0:T(2,128)(2,1)} %copy.88), calls=%async_computation | async-start | bytes 1310720 | tf_op jit(solution)/shard_map/all_to_all | solution.py:134
  92.2 4.9 %convolution_convert_fusion.3 = bf16[8,128,2048]{2,0,1:T(8,128)(2,1)} fusion(bf16[8,8,1]{1,0,2:T(8,128)(2,1)S(1)} %bitcast.151, bf16[8,128,2048]{2,1,0:T(8,128)(2,1)S(1)} %copy-done.2), kind=kOutput, calls=%fused_computation.19 | convolution fusion | flops 35651584 | bytes 8388736 | tf_op jit(solution)/shard_map/ne,erw->nrw/dot_general | solution.py:24
  97.2 4.9 %convolution_convert_fusion.4 = bf16[8,128,2048]{2,0,1:T(8,128)(2,1)} fusion(bf16[8,8,1]{1,0,2:T(8,128)(2,1)S(1)} %bitcast.154, bf16[8,128,2048]{2,1,0:T(8,128)(2,1)S(1)} %copy-done.2), kind=kOutput, calls=%fused_computation.20 | convolution fusion | flops 35651584 | bytes 8388736 | tf_op jit(solution)/shard_map/ne,erw->nrw/dot_general | solution.py:24
  102.2 5.3 %all-to-all-start.12 = ((bf16[4,2,20,2048]{3,1,2,0:T(2,128)(2,1)}), bf16[4,2,20,2048]{3,1,2,0:T(2,128)(2,1)S(1)}, u32[]{:S(2)}, u32[]{:S(2)}) async-start(bf16[4,2,20,2048]{3,1,2,0:T(2,128)(2,1)} %copy.115), calls=%async_computation.12 | async-start | bytes 1310720 | tf_op jit(solution)/shard_map/all_to_all | solution.py:131
  107.5 6.9 %fusion.30 = bf16[8,2048,128]{2,0,1:T(8,128)(2,1)} fusion(bf16[8,8,1]{1,0,2:T(8,128)(2,1)S(1)} %bitcast.155, bf16[8,2048,128]{2,1,0:T(8,128)(2,1)} %param.12), kind=kOutput, calls=%fused_computation.42 | convolution fusion | flops 35651584 | bytes 8388736 | tf_op jit(solution)/shard_map/ne,ewr->nwr/dot_general | solution.py:21
  114.4 4.5 %fusion.33 = bf16[8,2048,128]{2,0,1:T(8,128)(2,1)} fusion(bf16[8,8,1]{1,0,2:T(8,128)(2,1)S(1)} %bitcast.152, bf16[8,2048,128]{2,1,0:T(8,128)(2,1)S(1)} %copy-done.4), kind=kOutput, calls=%fused_computation.43 | convolution fusion | flops 35651584 | bytes 8388736 | tf_op jit(solution)/shard_map/ne,ewr->nwr/dot_general | solution.py:21
  118.9 4.9 %convolution_convert_fusion.2 = bf16[8,128,2048]{2,0,1:T(8,128)(2,1)} fusion(bf16[8,8,1]{1,0,2:T(8,128)(2,1)S(1)} %bitcast.148, bf16[8,128,2048]{2,1,0:T(8,128)(2,1)S(1)} %copy-done.3), kind=kOutput, calls=%fused_computation.18 | convolution fusion | flops 35651584 | bytes 8388736 | tf_op jit(solution)/shard_map/ne,erw->nrw/dot_general | solution.py:24
  124.7 5.7 %all-to-all-start.13 = ((bf16[4,2,20,2048]{3,1,2,0:T(2,128)(2,1)}), bf16[4,2,20,2048]{3,1,2,0:T(2,128)(2,1)}, u32[]{:S(2)}, u32[]{:S(2)}) async-start(bf16[4,2,20,2048]{3,1,2,0:T(2,128)(2,1)} %copy.117), calls=%async_computation.13 | async-start | bytes 1310720 | tf_op jit(solution)/shard_map/all_to_all | solution.py:131
  130.4 6.9 %fusion.36 = bf16[8,2048,128]{2,0,1:T(8,128)(2,1)} fusion(bf16[8,8,1]{1,0,2:T(8,128)(2,1)S(1)} %bitcast.149, bf16[8,2048,128]{2,1,0:T(8,128)(2,1)} %param.12), kind=kOutput, calls=%fused_computation.44 | convolution fusion | flops 35651584 | bytes 8388736 | tf_op jit(solution)/shard_map/ne,ewr->nwr/dot_general | solution.py:21
  139.7 3.2 fusion.3
  142.9 3.1 fusion.5
  146.1 5.1 %all-to-all-start.14 = ((bf16[4,2,20,2048]{3,1,2,0:T(2,128)(2,1)}), bf16[4,2,20,2048]{3,1,2,0:T(2,128)(2,1)}, u32[]{:S(2)}, u32[]{:S(2)}) async-start(bf16[4,2,20,2048]{3,1,2,0:T(2,128)(2,1)} %copy.119), calls=%async_computation.14 | async-start | bytes 1310720 | tf_op jit(solution)/shard_map/all_to_all | solution.py:131
  152.8 5.6 %fusion.7 = f32[8,20,128]{2,1,0:T(8,128)} fusion(bf16[8,20,2048]{2,1,0:T(8,128)(2,1)S(1)} %bitcast.138, bf16[8,128,2048]{2,0,1:T(8,128)(2,1)} %convolution_convert_fusion.4), kind=kOutput, calls=%fused_computation.16 | convolution fusion | flops 83886080 | bytes 4931584 | tf_op jit(solution)/shard_map/npw,nrw->npr/dot_general | solution.py:28
  162.6 3.8 %all-to-all-done.14 = bf16[4,2,20,2048]{3,1,2,0:T(2,128)(2,1)} async-done(((bf16[4,2,20,2048]{3,1,2,0:T(2,128)(2,1)}), bf16[4,2,20,2048]{3,1,2,0:T(2,128)(2,1)}, u32[]{:S(2)}, u32[]{:S(2)}) %all-to-all-start.14) | async-done | bytes 655392 | tf_op jit(solution)/shard_map/all_to_all | solution.py:131
  168.6 4.3 %fusion.9 = f32[8,20,128]{2,1,0:T(8,128)} fusion(bf16[8,20,2048]{2,1,0:T(8,128)(2,1)S(1)} %bitcast.141, bf16[8,2048,128]{2,0,1:T(8,128)(2,1)} %fusion.36), kind=kOutput, calls=%fused_computation.21 | convolution fusion | flops 83886080 | bytes 4931584 | tf_op jit(solution)/shard_map/npw,nwr->npr/dot_general | solution.py:27
  175.5 4.0 %reshape.274 = bf16[480,2048]{1,0:T(8,128)(2,1)} reshape(bf16[3,8,20,2048]{3,2,1,0:T(8,128)(2,1)} %copy.87) | data formatting | bytes 3932160 | tf_op jit(solution)/shard_map/reshape | solution.py:80
  180.3 8.1 %all_to_all.75 = bf16[4,2,128]{2,1,0:T(2,128)(2,1)S(1)} all-to-all(bf16[4,2,128]{2,1,0:T(2,128)(2,1)S(1)} %get-tuple-element.27), channel_id=1, replica_groups=mesh['rep'=2,'grp'=4,'tp'=4] {'grp'}, dimensions={0} | all-to-all | bytes 4096 | tf_op jit(solution)/shard_map/all_to_all | solution.py:140
  188.4 7.9 %all_to_all.76 = bf16[4,2,128]{2,1,0:T(2,128)(2,1)S(1)} all-to-all(bf16[4,2,128]{2,1,0:T(2,128)(2,1)S(1)} %get-tuple-element.28), channel_id=1, replica_groups=mesh['rep'=2,'grp'=4,'tp'=4] {'grp'}, dimensions={0} | all-to-all | bytes 4096 | tf_op jit(solution)/shard_map/all_to_all | solution.py:140
  196.3 3.2 all-to-all-start.2
  200.7 4.3 %all-to-all-done.2 = bf16[4,2,128]{2,1,0:T(2,128)(2,1)S(1)} async-done(((bf16[4,2,128]{2,1,0:T(2,128)(2,1)}), bf16[4,2,128]{2,1,0:T(2,128)(2,1)S(1)}, u32[]{:S(2)}, u32[]{:S(2)}) %all-to-all-start.2) | async-done | bytes 2080 | tf_op jit(solution)/shard_map/all_to_all | solution.py:140
  212.5 4.7 %fusion.45 = bf16[8,20,2048]{2,1,0:T(8,128)(2,1)S(1)} fusion(bf16[8,20,128]{2,1,0:T(8,128)(2,1)S(1)} %get-tuple-element.33, bf16[8,2048,128]{2,0,1:T(8,128)(2,1)} %fusion.36), kind=kOutput, calls=%fused_computation.47 | convolution fusion | flops 84213760 | bytes 4890624 | tf_op jit(solution)/shard_map/npr,nwr->npw/dot_general | solution.py:54
  218.8 3.7 all-to-all-start.11
  223.7 4.5 %fusion.42 = bf16[8,20,2048]{2,1,0:T(8,128)(2,1)S(1)} fusion(bf16[8,20,128]{2,1,0:T(8,128)(2,1)S(1)} %get-tuple-element.50, bf16[8,2048,128]{2,0,1:T(8,128)(2,1)} %fusion.33), kind=kOutput, calls=%fused_computation.46 | convolution fusion | flops 84213760 | bytes 4890624 | tf_op jit(solution)/shard_map/npr,nwr->npw/dot_general | solution.py:54
  230.9 4.6 %fusion.60 = f32[1024,2048]{1,0:T(8,128)} fusion(bf16[160,2048]{1,0:T(8,128)(2,1)S(1)} %copy-done.16, bf16[20,8,8,128]{3,2,1,0:T(8,128)(2,1)S(1)} %bitcast.142), kind=kOutput, calls=%fused_computation.69 | convolution fusion | flops 671088640 | bytes 9371648 | tf_op jit(solution)/shard_map/dot_general | solution.py:42
  235.5 4.6 %fusion.57 = f32[1024,2048]{1,0:T(8,128)} fusion(bf16[160,2048]{1,0:T(8,128)(2,1)S(1)} %reshape_reshape.22, bf16[20,8,8,128]{3,2,1,0:T(8,128)(2,1)S(1)} %bitcast.143), kind=kOutput, calls=%fused_computation.66 | convolution fusion | flops 671088640 | bytes 9371648 | tf_op jit(solution)/shard_map/dot_general | solution.py:42
  241.8 5.7 %abs_reduce_fusion.1 = (f32[]{:T(128)}, f32[2048,1024]{0,1:T(8,128)}) fusion(bf16[160,2048]{1,0:T(8,128)(2,1)S(1)} %copy-done.15, bf16[20,8,8,128]{3,2,1,0:T(8,128)(2,1)S(1)} %bitcast.147, f32[2048,1024]{0,1:T(8,128)S(1)} %fusion.68, f32[2048,1024]{0,1:T(8,128)S(1)} %fusion.65), kind=kOutput, calls=%fused_computation.8 | convolution fusion | flops 679477248 | bytes 26148868 | tf_op jit(solution)/shard_map/dot_general | solution.py:48
  247.5 5.1 %all-to-all-start.7 = ((bf16[4,2,20,2048]{3,1,2,0:T(2,128)(2,1)}), bf16[4,2,20,2048]{3,1,2,0:T(2,128)(2,1)S(1)}, u32[]{:S(2)}, u32[]{:S(2)}) async-start(bf16[4,2,20,2048]{3,1,2,0:T(2,128)(2,1)} %copy.103), calls=%async_computation.7 | async-start | bytes 1310720 | tf_op jit(solution)/shard_map/all_to_all | solution.py:155
  252.6 11.1 %abs_reduce_fusion = (f32[]{:T(128)}, f32[1024,2048]{1,0:T(8,128)}) fusion(bf16[160,2048]{1,0:T(8,128)(2,1)S(1)} %reshape_reshape.23, bf16[20,8,8,128]{3,2,1,0:T(8,128)(2,1)S(1)} %bitcast.146, f32[1024,2048]{1,0:T(8,128)} %fusion.60, f32[1024,2048]{1,0:T(8,128)} %fusion.57), kind=kOutput, calls=%fused_computation.6 | convolution fusion | flops 679477248 | bytes 26148868 | tf_op jit(solution)/shard_map/dot_general | solution.py:42
  264.9 30.4 %pmax.7 = f32[]{:T(128)} all-reduce(f32[]{:T(128)S(6)} %max.8), channel_id=1, replica_groups=mesh['rep'=2,'grp'=4,'tp'=4] {'grp','tp'}, use_global_device_ids=true, to_apply=%region_11.12 | all-reduce | flops 1 | bytes 8 | tf_op jit(solution)/shard_map/pmax | solution.py:188
  295.3 4.5 %fusion.39 = bf16[8,20,2048]{2,1,0:T(8,128)(2,1)S(1)} fusion(bf16[8,20,128]{2,1,0:T(8,128)(2,1)S(1)} %get-tuple-element.37, bf16[8,2048,128]{2,0,1:T(8,128)(2,1)} %fusion.30), kind=kOutput, calls=%fused_computation.45 | convolution fusion | flops 84213760 | bytes 4890624 | tf_op jit(solution)/shard_map/npr,nwr->npw/dot_general | solution.py:54
  302.0 3.5 all-to-all-start.3
  305.5 6.6 %multiply_convert_fusion.1 = bf16[2048,1024]{0,1:T(8,128)(2,1)} fusion(f32[2048,1024]{0,1:T(8,128)} %get-tuple-element.47, f32[]{:T(128)S(6)} %div.27), kind=kLoop, calls=%fused_computation.5 | loop fusion | flops 4194304 | bytes 12582916 | tf_op jit(solution)/shard_map/convert_element_type | solution.py:192
  312.1 6.4 %copy.130 = bf16[2048,8,128]{2,0,1:T(8,128)(2,1)} copy(bf16[2048,8,128]{0,2,1:T(8,128)(2,1)} %bitcast.130) | data formatting | bytes 8388608 | tf_op jit(solution)/shard_map/convert_element_type | solution.py:192
  318.5 6.6 %multiply_convert_fusion = bf16[1024,2048]{1,0:T(8,128)(2,1)} fusion(f32[1024,2048]{1,0:T(8,128)} %get-tuple-element.49, f32[]{:T(128)S(6)} %div.27), kind=kLoop, calls=%fused_computation.4 | loop fusion | flops 4194304 | bytes 12582916 | tf_op jit(solution)/shard_map/convert_element_type | solution.py:193
  329.8 23.6 %fusion.84 = f32[480,2048]{1,0:T(8,128)} fusion(bf16[480,8192]{1,0:T(8,128)(2,1)} %all-gather.2.cloned.1.call-done, bf16[2048,8192]{1,0:T(8,128)(2,1)} %param.11), kind=kOutput, calls=%fused_computation.130 | convolution fusion | flops 16106127360 | bytes 45350912 | tf_op jit(solution)/shard_map/dot_general | solution.py:13
  353.4 5.1 %reshape.275 = f32[3,8,20,2048]{3,2,1,0:T(8,128)} reshape(f32[480,2048]{1,0:T(8,128)} %fusion.84) | data formatting | bytes 7864320 | tf_op jit(solution)/shard_map/reshape | solution.py:182
  358.5 6.0 %fusion.2 = bf16[3,8,20,2048]{3,2,1,0:T(8,128)(2,1)S(1)} fusion(f32[3,8,20,2048]{3,2,1,0:T(8,128)} %reshape.275, f32[3,8,20,2048]{3,1,2,0:T(8,128)} %bitcast.128), kind=kLoop, calls=%fused_computation.11 | loop fusion | flops 1966080 | bytes 9830400 | tf_op jit(solution)/shard_map/convert_element_type | solution.py:186
  (138 shorter events, 61.1 us)
Async XLA Ops:
  7.2 60.6 %copy-start = (bf16[3,8,20,2048]{3,1,2,0:T(8,128)(2,1)S(1)}, bf16[3,8,20,2048]{3,1,2,0:T(8,128)(2,1)}, u32[]{:S(2)}) copy-start(bf16[3,8,20,2048]{3,1,2,0:T(8,128)(2,1)} %param.9) | copy-start | bytes 5898244
  9.1 170.5 %copy-start.23 = (s32[3,8]{1,0:T(4,128)}, s32[3,8]{1,0:T(4,128)S(1)}, u32[]{:S(2)}) copy-start(s32[3,8]{1,0:T(4,128)S(1)} %multiply_add_fusion) | copy-start | bytes 292
  9.9 11.8 %all-to-all-start.9 = ((bf16[4,2,8]{2,1,0:T(2,128)(2,1)}), bf16[4,2,8]{2,1,0:T(2,128)(2,1)S(1)}, u32[]{:S(2)}, u32[]{:S(2)}) async-start(bf16[4,2,8]{2,1,0:T(2,128)(2,1)} %get-tuple-element.30), calls=%async_computation.9 | async-start | bytes 4096 | tf_op jit(solution)/shard_map/all_to_all | solution.py:137
  21.7 108.7 %copy-start.25 = (bf16[4,2,8]{2,1,0:T(2,128)(2,1)}, bf16[4,2,8]{2,1,0:T(2,128)(2,1)S(1)}, u32[]{:S(2)}) copy-start(bf16[4,2,8]{2,1,0:T(2,128)(2,1)S(1)} %all-to-all-done.9) | copy-start | bytes 388
  21.7 11.1 %all-to-all-start.5 = ((bf16[4,2,8]{2,1,0:T(2,128)(2,1)}), bf16[4,2,8]{2,1,0:T(2,128)(2,1)S(1)}, u32[]{:S(2)}, u32[]{:S(2)}) async-start(bf16[4,2,8]{2,1,0:T(2,128)(2,1)} %get-tuple-element.31), calls=%async_computation.5 | async-start | bytes 4096 | tf_op jit(solution)/shard_map/all_to_all | solution.py:137
  32.8 81.5 %copy-start.27 = (bf16[4,2,8]{2,1,0:T(2,128)(2,1)}, bf16[4,2,8]{2,1,0:T(2,128)(2,1)S(1)}, u32[]{:S(2)}) copy-start(bf16[4,2,8]{2,1,0:T(2,128)(2,1)S(1)} %all-to-all-done.5) | copy-start | bytes 388
  32.8 10.5 %all-to-all-start.1 = ((bf16[4,2,8]{2,1,0:T(2,128)(2,1)}), bf16[4,2,8]{2,1,0:T(2,128)(2,1)S(1)}, u32[]{:S(2)}, u32[]{:S(2)}) async-start(bf16[4,2,8]{2,1,0:T(2,128)(2,1)} %get-tuple-element.29), calls=%async_computation.1 | async-start | bytes 4096 | tf_op jit(solution)/shard_map/all_to_all | solution.py:137
  43.3 64.2 %copy-start.29 = (bf16[4,2,8]{2,1,0:T(2,128)(2,1)}, bf16[4,2,8]{2,1,0:T(2,128)(2,1)S(1)}, u32[]{:S(2)}) copy-start(bf16[4,2,8]{2,1,0:T(2,128)(2,1)S(1)} %all-to-all-done.1) | copy-start | bytes 388
  43.3 19.4 %all-to-all-start.8 = ((bf16[4,2,20,2048]{3,1,2,0:T(2,128)(2,1)}), bf16[4,2,20,2048]{3,1,2,0:T(2,128)(2,1)}, u32[]{:S(2)}, u32[]{:S(2)}) async-start(bf16[4,2,20,2048]{3,1,2,0:T(2,128)(2,1)} %copy.105), calls=%async_computation.8 | async-start | bytes 1310720 | tf_op jit(solution)/shard_map/all_to_all | solution.py:134
  62.7 19.2 %all-to-all-start.4 = ((bf16[4,2,20,2048]{3,1,2,0:T(2,128)(2,1)}), bf16[4,2,20,2048]{3,1,2,0:T(2,128)(2,1)S(1)}, u32[]{:S(2)}, u32[]{:S(2)}) async-start(bf16[4,2,20,2048]{3,1,2,0:T(2,128)(2,1)} %copy.97), calls=%async_computation.4 | async-start | bytes 1310720 | tf_op jit(solution)/shard_map/all_to_all | solution.py:134
  81.9 8.8 %copy-start.17 = (bf16[4,2,20,2048]{3,1,2,0:T(2,128)(2,1)}, bf16[4,2,20,2048]{3,1,2,0:T(2,128)(2,1)S(1)}, u32[]{:S(2)}) copy-start(bf16[4,2,20,2048]{3,1,2,0:T(2,128)(2,1)S(1)} %all-to-all-done.4) | copy-start | bytes 1966084
  81.9 20.3 %all-to-all-start = ((bf16[4,2,20,2048]{3,1,2,0:T(2,128)(2,1)}), bf16[4,2,20,2048]{3,1,2,0:T(2,128)(2,1)S(1)}, u32[]{:S(2)}, u32[]{:S(2)}) async-start(bf16[4,2,20,2048]{3,1,2,0:T(2,128)(2,1)} %copy.88), calls=%async_computation | async-start | bytes 1310720 | tf_op jit(solution)/shard_map/all_to_all | solution.py:134
  85.7 6.6 %copy-start.2 = (bf16[8,128,2048]{2,1,0:T(8,128)(2,1)S(1)}, bf16[8,128,2048]{2,1,0:T(8,128)(2,1)}, u32[]{:S(2)}) copy-start(bf16[8,128,2048]{2,1,0:T(8,128)(2,1)} %param.13) | copy-start | bytes 12582916
  102.2 12.2 %copy-start.19 = (bf16[4,2,20,2048]{3,1,2,0:T(2,128)(2,1)}, bf16[4,2,20,2048]{3,1,2,0:T(2,128)(2,1)S(1)}, u32[]{:S(2)}) copy-start(bf16[4,2,20,2048]{3,1,2,0:T(2,128)(2,1)S(1)} %all-to-all-done) | copy-start | bytes 1966084
  102.2 21.7 %all-to-all-start.12 = ((bf16[4,2,20,2048]{3,1,2,0:T(2,128)(2,1)}), bf16[4,2,20,2048]{3,1,2,0:T(2,128)(2,1)S(1)}, u32[]{:S(2)}, u32[]{:S(2)}) async-start(bf16[4,2,20,2048]{3,1,2,0:T(2,128)(2,1)} %copy.115), calls=%async_computation.12 | async-start | bytes 1310720 | tf_op jit(solution)/shard_map/all_to_all | solution.py:131
  107.5 6.9 %copy-start.4 = (bf16[8,2048,128]{2,1,0:T(8,128)(2,1)S(1)}, bf16[8,2048,128]{2,1,0:T(8,128)(2,1)}, u32[]{:S(2)}) copy-start(bf16[8,2048,128]{2,1,0:T(8,128)(2,1)} %param.12) | copy-start | bytes 12582916
  114.4 4.5 %copy-start.3 = (bf16[8,128,2048]{2,1,0:T(8,128)(2,1)S(1)}, bf16[8,128,2048]{2,1,0:T(8,128)(2,1)}, u32[]{:S(2)}) copy-start(bf16[8,128,2048]{2,1,0:T(8,128)(2,1)} %param.13) | copy-start | bytes 12582916
  123.8 0.9 copy-start.21
  124.7 21.3 %all-to-all-start.13 = ((bf16[4,2,20,2048]{3,1,2,0:T(2,128)(2,1)}), bf16[4,2,20,2048]{3,1,2,0:T(2,128)(2,1)}, u32[]{:S(2)}, u32[]{:S(2)}) async-start(bf16[4,2,20,2048]{3,1,2,0:T(2,128)(2,1)} %copy.117), calls=%async_computation.13 | async-start | bytes 1310720 | tf_op jit(solution)/shard_map/all_to_all | solution.py:131
  130.4 8.4 %copy-start.18 = (bf16[4,2,20,2048]{3,1,2,0:T(2,128)(2,1)S(1)}, bf16[4,2,20,2048]{3,1,2,0:T(2,128)(2,1)}, u32[]{:S(2)}) copy-start(bf16[4,2,20,2048]{3,1,2,0:T(2,128)(2,1)} %copy-done.17) | copy-start | bytes 1966084
  130.4 8.7 %copy-start.20 = (bf16[4,2,20,2048]{3,1,2,0:T(2,128)(2,1)S(1)}, bf16[4,2,20,2048]{3,1,2,0:T(2,128)(2,1)}, u32[]{:S(2)}) copy-start(bf16[4,2,20,2048]{3,1,2,0:T(2,128)(2,1)} %copy-done.19) | copy-start | bytes 1966084
  130.4 8.9 %copy-start.22 = (bf16[4,2,20,2048]{3,1,2,0:T(2,128)(2,1)S(1)}, bf16[4,2,20,2048]{3,1,2,0:T(2,128)(2,1)}, u32[]{:S(2)}) copy-start(bf16[4,2,20,2048]{3,1,2,0:T(2,128)(2,1)} %copy-done.21) | copy-start | bytes 1966084
  137.4 2.4 copy-start.9
  139.1 3.8 %copy-start.8 = (bf16[8,128,2048]{2,0,1:T(8,128)(2,1)S(1)}, bf16[8,128,2048]{2,0,1:T(8,128)(2,1)}, u32[]{:S(2)}) copy-start(bf16[8,128,2048]{2,0,1:T(8,128)(2,1)} %convolution_convert_fusion.3) | copy-start | bytes 12582916
  139.3 13.5 %copy-start.10 = (bf16[4,2,20,2048]{3,2,1,0:T(8,128)(2,1)}, bf16[4,2,20,2048]{3,2,1,0:T(8,128)(2,1)S(1)}, u32[]{:S(2)}) copy-start(bf16[4,2,20,2048]{3,2,1,0:T(8,128)(2,1)S(1)} %copy.89) | copy-start | bytes 1966084
  139.6 18.9 %copy-start.11 = (bf16[4,2,20,2048]{3,2,1,0:T(8,128)(2,1)}, bf16[4,2,20,2048]{3,2,1,0:T(8,128)(2,1)S(1)}, u32[]{:S(2)}) copy-start(bf16[4,2,20,2048]{3,2,1,0:T(8,128)(2,1)S(1)} %copy.116) | copy-start | bytes 1966084
  146.1 20.4 %all-to-all-start.14 = ((bf16[4,2,20,2048]{3,1,2,0:T(2,128)(2,1)}), bf16[4,2,20,2048]{3,1,2,0:T(2,128)(2,1)}, u32[]{:S(2)}, u32[]{:S(2)}) async-start(bf16[4,2,20,2048]{3,1,2,0:T(2,128)(2,1)} %copy.119), calls=%async_computation.14 | async-start | bytes 1310720 | tf_op jit(solution)/shard_map/all_to_all | solution.py:131
  151.2 60.2 %all-reduce.3.cloned.1.call-start = ((), (), s32[]{:S(2)}) async-start(), calls=%async_computation.16 | async-start | bytes 1179648 | tf_op jit(solution)/shard_map/psum | solution.py:29
  151.3 7.1 %copy-start.6 = (bf16[8,2048,128]{2,0,1:T(8,128)(2,1)S(1)}, bf16[8,2048,128]{2,0,1:T(8,128)(2,1)}, u32[]{:S(2)}) copy-start(bf16[8,2048,128]{2,0,1:T(8,128)(2,1)} %fusion.30) | copy-start | bytes 12582916
  152.8 7.6 %copy-start.12 = (bf16[4,2,20,2048]{3,2,1,0:T(8,128)(2,1)}, bf16[4,2,20,2048]{3,2,1,0:T(8,128)(2,1)S(1)}, u32[]{:S(2)}) copy-start(bf16[4,2,20,2048]{3,2,1,0:T(8,128)(2,1)S(1)} %copy.118) | copy-start | bytes 1966084
  158.4 2.2 copy-start.7
  167.7 0.9 copy-start.13
  168.6 4.3 %copy-start.5 = (bf16[3,8,20,2048]{3,1,2,0:T(8,128)(2,1)S(1)}, bf16[3,8,20,2048]{3,1,2,0:T(8,128)(2,1)}, u32[]{:S(2)}) copy-start(bf16[3,8,20,2048]{3,1,2,0:T(8,128)(2,1)} %broadcast_multiply_fusion) | copy-start | bytes 5898244
  172.9 156.9 %all-gather.2.cloned.1.call-start = ((), (), s32[]{:S(2)}) async-start(), calls=%async_computation.15 | async-start | bytes 9830400 | tf_op jit(solution)/shard_map/all_gather | solution.py:82
  175.5 4.0 %copy-start.32 = (s32[3,8]{1,0:T(4,128)S(1)}, s32[3,8]{1,0:T(4,128)}, u32[]{:S(2)}) copy-start(s32[3,8]{1,0:T(4,128)} %get-tuple-element.12) | copy-start | bytes 292
  175.5 30.1 %copy-start.14 = (bf16[4,2,20,2048]{3,2,1,0:T(8,128)(2,1)S(1)}, bf16[4,2,20,2048]{3,2,1,0:T(8,128)(2,1)}, u32[]{:S(2)}) copy-start(bf16[4,2,20,2048]{3,2,1,0:T(8,128)(2,1)} %copy-done.13) | copy-start | bytes 1966084
  196.3 8.7 %all-to-all-start.2 = ((bf16[4,2,128]{2,1,0:T(2,128)(2,1)}), bf16[4,2,128]{2,1,0:T(2,128)(2,1)S(1)}, u32[]{:S(2)}, u32[]{:S(2)}) async-start(bf16[4,2,128]{2,1,0:T(2,128)(2,1)} %get-tuple-element.26), calls=%async_computation.2 | async-start | bytes 4096 | tf_op jit(solution)/shard_map/all_to_all | solution.py:140
  211.4 11.1 %copy-start.31 = (f32[8,128]{1,0:T(8,128)S(1)}, f32[8,128]{1,0:T(8,128)}, u32[]{:S(2)}) copy-start(f32[8,128]{1,0:T(8,128)} %convert.3) | copy-start | bytes 12292
  212.5 10.9 %copy-start.30 = (bf16[4,2,8]{2,1,0:T(2,128)(2,1)S(1)}, bf16[4,2,8]{2,1,0:T(2,128)(2,1)}, u32[]{:S(2)}) copy-start(bf16[4,2,8]{2,1,0:T(2,128)(2,1)} %copy-done.29) | copy-start | bytes 388
  212.5 11.1 %copy-start.28 = (bf16[4,2,8]{2,1,0:T(2,128)(2,1)S(1)}, bf16[4,2,8]{2,1,0:T(2,128)(2,1)}, u32[]{:S(2)}) copy-start(bf16[4,2,8]{2,1,0:T(2,128)(2,1)} %copy-done.27) | copy-start | bytes 388
  218.8 28.8 %all-to-all-start.11 = ((bf16[4,2,20,2048]{3,1,2,0:T(2,128)(2,1)}), bf16[4,2,20,2048]{3,1,2,0:T(2,128)(2,1)S(1)}, u32[]{:S(2)}, u32[]{:S(2)}) async-start(bf16[4,2,20,2048]{3,1,2,0:T(2,128)(2,1)} %copy.111), calls=%async_computation.11 | async-start | bytes 1310720 | tf_op jit(solution)/shard_map/all_to_all | solution.py:155
  229.5 1.4 copy-start.16
  235.5 4.7 %copy-start.26 = (bf16[4,2,8]{2,1,0:T(2,128)(2,1)S(1)}, bf16[4,2,8]{2,1,0:T(2,128)(2,1)}, u32[]{:S(2)}) copy-start(bf16[4,2,8]{2,1,0:T(2,128)(2,1)} %copy-done.25) | copy-start | bytes 388
  235.5 6.3 %copy-start.15 = (bf16[160,2048]{1,0:T(8,128)(2,1)S(1)}, bf16[160,2048]{1,0:T(8,128)(2,1)}, u32[]{:S(2)}) copy-start(bf16[160,2048]{1,0:T(8,128)(2,1)} %reshape_reshape.20) | copy-start | bytes 1966084
  247.5 54.5 %all-to-all-start.7 = ((bf16[4,2,20,2048]{3,1,2,0:T(2,128)(2,1)}), bf16[4,2,20,2048]{3,1,2,0:T(2,128)(2,1)S(1)}, u32[]{:S(2)}, u32[]{:S(2)}) async-start(bf16[4,2,20,2048]{3,1,2,0:T(2,128)(2,1)} %copy.103), calls=%async_computation.7 | async-start | bytes 1310720 | tf_op jit(solution)/shard_map/all_to_all | solution.py:155
  302.0 24.4 %all-to-all-start.3 = ((bf16[4,2,20,2048]{3,1,2,0:T(2,128)(2,1)}), bf16[4,2,20,2048]{3,1,2,0:T(2,128)(2,1)S(1)}, u32[]{:S(2)}, u32[]{:S(2)}) async-start(bf16[4,2,20,2048]{3,1,2,0:T(2,128)(2,1)} %copy.95), calls=%async_computation.3 | async-start | bytes 1310720 | tf_op jit(solution)/shard_map/all_to_all | solution.py:155
  325.1 2.1 copy-start.24
  358.5 8.4 %copy-start.1 = (bf16[3,8,20,2048]{3,1,2,0:T(8,128)(2,1)S(1)}, bf16[3,8,20,2048]{3,1,2,0:T(8,128)(2,1)}, u32[]{:S(2)}) copy-start(bf16[3,8,20,2048]{3,1,2,0:T(8,128)(2,1)} %param.9) | copy-start | bytes 5898244
Sparse Core Ops, SparseCore 0:
  173.0 33.1 all-reduce.2
  208.4 55.3 all-gather.1
where the time goes:
time: 380 us; the launch traced here: 374 us
  matrix products  128 us (34%)
  local copies, waits for them, and re-layouts  62.6 us (16%)
  starting transfers between devices  57.8 us (15%)
  blocking collectives  46.3 us (12%)
  waiting for transfers between devices  33.9 us (9%)
  other arithmetic  28.9 us (8%)
  between operations  16.7 us (4%)
    pmax x1, blocking collectives, local(): highest = lax.pmax(largest, ('grp', 'tp'))  30.4 us
    dot_general x1, matrix products, fold_columns(): lax.dot_general(gathered, frozen_weight_matrix, (((1,), (1,)), ((), ())),...  23.6 us
    all_to_all x3, waiting for transfers between devices, local(): lax.all_to_all(send_masked[:, :, micro_step], 'grp', split_axis=0, concat...  21.8 us
    dot_general x3, matrix products, lowrank_product(): lax.dot_general(spread_lift, masked_items.reshape(item_count * token_row_...  20.4 us
    dot_general x3, matrix products, lowrank_product(): jnp.einsum('ne,ewr->nwr', slot_picks, down_adapter_matrix, preferred_elem...  18.3 us
    all_to_all x3, starting transfers between devices, local(): lax.all_to_all(send_acts[:, :, micro_step], 'grp', split_axis=0, concat_a...  16 us
    all_to_all x2, blocking collectives, local(): lax.all_to_all(send_lanes[:, :, micro_step], 'grp', split_axis=0, concat_...  15.9 us
    dot_general x3, matrix products, lowrank_product(): jnp.einsum('ne,erw->nrw', slot_picks, up_adapter_matrix, preferred_elemen...  14.8 us
  transfers between devices with their start and end apart: 15, of which 7 were waited for; matrix products, arithmetic and copies ran while one was open for 46% of the time, Pallas kernels for 0%

commit v1 on v0

v1 whole, which is shorter than its diff:
```python
import functools

import jax
import jax.numpy as jnp
from jax import lax
from jax.experimental import pallas as pl
from jax.experimental.pallas import tpu as pltpu
from jax.sharding import PartitionSpec as P

WINDOWS_PER_OWNER = 2

grad_limit = 4.0

BF16 = jnp.bfloat16
F32 = jnp.float32
VMEM_LIMIT = 48 * 1024 * 1024
SMEM_SPEC = pl.BlockSpec(memory_space=pltpu.SMEM)


def params(grid_rank=1):
    return pltpu.CompilerParams(
        dimension_semantics=("arbitrary",) * grid_rank, vmem_limit_bytes=VMEM_LIMIT
    )


def cost(flops, moved):
    return pl.CostEstimate(flops=int(flops), bytes_accessed=int(moved), transcendentals=0)


def feature_block(features, wanted=512):
    return wanted if features % wanted == 0 else features


def window_order(adapter_ref, slot_ref, order_ref, count_ref, groups, slots):
    micro, windows = adapter_ref.shape
    for m in range(micro):
        for o in range(groups):
            count_ref[o] = 0
            for k in range(WINDOWS_PER_OWNER):
                order_ref[(m * groups + o) * WINDOWS_PER_OWNER + k] = -1
        for j in range(windows):
            owner = lax.div(slot_ref[adapter_ref[m, j]], slots)
            k = jnp.minimum(count_ref[owner], WINDOWS_PER_OWNER - 1)
            order_ref[(m * groups + owner) * WINDOWS_PER_OWNER + k] = j
            count_ref[owner] = k + 1


def pack_body(groups, slots, masking, me_ref, adapter_ref, slot_ref, live_ref, x_ref, *rest):
    out_refs = rest[:groups]
    order_ref, count_ref, rows_ref = rest[-3:]
    micro, windows, piece, width = x_ref.shape

    @pl.when(pl.program_id(0) == 0)
    def _():
        window_order(adapter_ref, slot_ref, order_ref, count_ref, groups, slots)

    row = lax.broadcasted_iota(jnp.int32, (piece, width), 0)
    for s in range(groups):
        owner = lax.rem(me_ref[0] + s, groups)
        for m in range(micro):
            for k in range(WINDOWS_PER_OWNER):
                j = order_ref[(m * groups + owner) * WINDOWS_PER_OWNER + k]
                at = jnp.maximum(j, 0)
                values = x_ref[m, at].astype(F32)
                if masking:
                    live = jnp.where(j >= 0, live_ref[m, at], 0)
                    values = jnp.where(row < live, values, 0.0)
                first = (m * WINDOWS_PER_OWNER + k) * piece
                rows_ref[first : first + piece, :] = values
        out_refs[s][...] = rows_ref[...].astype(BF16)


def pack(x, me, adapter, slot_per_adapter, live, groups, slots, masking):
    micro, windows, piece, features = x.shape
    rows = micro * WINDOWS_PER_OWNER * piece
    fb = feature_block(features)
    return pl.pallas_call(
        functools.partial(pack_body, groups, slots, masking),
        grid=(features // fb,),
        out_shape=[jax.ShapeDtypeStruct((rows, features), BF16)] * groups,
        in_specs=[SMEM_SPEC] * 4
        + [pl.BlockSpec((micro, windows, piece, fb), lambda f: (0, 0, 0, f))],
        out_specs=[pl.BlockSpec((rows, fb), lambda f: (0, f))] * groups,
        scratch_shapes=[
            pltpu.SMEM((micro * groups * WINDOWS_PER_OWNER,), jnp.int32),
            pltpu.SMEM((groups,), jnp.int32),
            pltpu.VMEM((rows, fb), F32),
        ],
        compiler_params=params(),
        cost_estimate=cost(0, 2 * x.size * 2),
    )(me, adapter, slot_per_adapter, live, x)


def flat_body(live_ref, x_ref, out_ref, rows_ref):
    micro, windows, piece, width = x_ref.shape
    row = lax.broadcasted_iota(jnp.int32, (piece, width), 0)
    for m in range(micro):
        for j in range(windows):
            first = (m * windows + j) * piece
            rows_ref[first : first + piece, :] = jnp.where(
                row < live_ref[m, j], x_ref[m, j].astype(F32), 0.0
            )
    out_ref[...] = rows_ref[...].astype(BF16)


def flat(x, live):
    micro, windows, piece, features = x.shape
    rows = micro * windows * piece
    fb = feature_block(features)
    return pl.pallas_call(
        flat_body,
        grid=(features // fb,),
        out_shape=jax.ShapeDtypeStruct((rows, features), BF16),
        in_specs=[
            SMEM_SPEC,
            pl.BlockSpec((micro, windows, piece, fb), lambda f: (0, 0, 0, f)),
        ],
        out_specs=pl.BlockSpec((rows, fb), lambda f: (0, f)),
        scratch_shapes=[pltpu.VMEM((rows, fb), F32)],
        compiler_params=params(),
        cost_estimate=cost(0, 2 * x.size * 2),
    )(live, x)


def meta_body(groups, slots, piece, me_ref, slot_ref, rank_ref, *rest):
    adapter_refs = rest[:groups]
    pick_ref, lane_ref, order_ref, count_ref = rest[groups:]
    micro, windows = adapter_refs[0].shape
    top = lane_ref.shape[1]
    column = lax.broadcasted_iota(jnp.int32, (piece, top), 1)
    me = me_ref[0]
    for s in range(groups):
        window_order(adapter_refs[s], slot_ref, order_ref, count_ref, groups, slots)
        for m in range(micro):
            for k in range(WINDOWS_PER_OWNER):
                j = order_ref[(m * groups + me) * WINDOWS_PER_OWNER + k]
                adapter = adapter_refs[s][m, jnp.maximum(j, 0)]
                local = lax.rem(slot_ref[adapter], slots)
                rank = rank_ref[adapter]
                limit = jnp.where(j >= 0, rank, 0)
                wide_rank = jnp.full((piece, top), rank, jnp.int32).astype(F32)
                first = ((s * micro + m) * WINDOWS_PER_OWNER + k) * piece
                lane_ref[first : first + piece, :] = jnp.where(
                    column < limit, (top // 8) / wide_rank, 0.0
                )
                pick_ref[first : first + piece, :] = jnp.full((piece, top), local, jnp.int32)


def meta(me, slot_per_adapter, rank_per_adapter, adapters, slots, piece, top):
    groups = len(adapters)
    micro, windows = adapters[0].shape
    rows = groups * micro * WINDOWS_PER_OWNER * piece
    whole = pl.BlockSpec(memory_space=pltpu.VMEM)
    return pl.pallas_call(
        functools.partial(meta_body, groups, slots, piece),
        out_shape=[
            jax.ShapeDtypeStruct((rows, top), jnp.int32),
            jax.ShapeDtypeStruct((rows, top), F32),
        ],
        in_specs=[SMEM_SPEC] * (3 + groups),
        out_specs=[whole, whole],
        scratch_shapes=[
            pltpu.SMEM((micro * groups * WINDOWS_PER_OWNER,), jnp.int32),
            pltpu.SMEM((groups,), jnp.int32),
        ],
        compiler_params=pltpu.CompilerParams(vmem_limit_bytes=VMEM_LIMIT),
    )(me, slot_per_adapter, rank_per_adapter, *adapters)


def joined(refs):
    return jnp.concatenate([ref[...].astype(F32) for ref in refs], axis=0).astype(BF16)


def project_body(groups, down, pick_ref, *rest):
    row_refs = rest[:groups]
    table_ref, out_ref, rows_ref = rest[groups:]
    step = pl.program_id(0)

    @pl.when(step == 0)
    def _():
        rows_ref[...] = joined(row_refs)
        out_ref[...] = jnp.zeros_like(out_ref)

    together = table_ref.shape[0]
    top = out_ref.shape[1]
    rows = rows_ref[...]
    if down:
        table = jnp.concatenate([table_ref[i] for i in range(together)], axis=1)
        product = jnp.dot(rows, table, preferred_element_type=F32)
    else:
        table = table_ref[...].reshape(together * top, table_ref.shape[2])
        product = lax.dot_general(
            rows, table, (((1,), (1,)), ((), ())), preferred_element_type=F32
        )
    chosen = out_ref[...]
    for i in range(together):
        chosen = jnp.where(
            pick_ref[...] == step * together + i, product[:, i * top : (i + 1) * top], chosen
        )
    out_ref[...] = chosen


def project(row_blocks, pick, table, down):
    groups = len(row_blocks)
    rows, top = pick.shape
    slots = table.shape[0]
    features = row_blocks[0].shape[1]
    together = 2 if slots % 2 == 0 else 1
    whole = pl.BlockSpec(memory_space=pltpu.VMEM)
    return pl.pallas_call(
        functools.partial(project_body, groups, down),
        grid=(slots // together,),
        out_shape=jax.ShapeDtypeStruct((rows, top), F32),
        in_specs=[whole] * (1 + groups)
        + [pl.BlockSpec((together,) + table.shape[1:], lambda e: (e, 0, 0))],
        out_specs=pl.BlockSpec((rows, top), lambda e: (0, 0)),
        scratch_shapes=[pltpu.VMEM((rows, features), BF16)],
        compiler_params=params(),
        cost_estimate=cost(2 * rows * table.size, table.size * 2 + rows * features * 2),
    )(pick, *row_blocks, table)


def spread(values, pick, slots):
    return jnp.concatenate(
        [jnp.where(pick == e, values, 0.0) for e in range(slots)], axis=1
    ).astype(BF16)


def back_body(groups, mine_ref, other_ref, lane_ref, pick_ref, down_ref, *rest):
    out_refs = rest[:groups]
    spread_ref = rest[groups]
    slots, width, top = down_ref.shape

    @pl.when(pl.program_id(0) == 0)
    def _():
        lowered = ((mine_ref[...] + other_ref[...]) * lane_ref[...]).astype(BF16).astype(F32)
        spread_ref[...] = spread(lowered, pick_ref[...], slots)

    table = jnp.concatenate([down_ref[e] for e in range(slots)], axis=1)
    product = lax.dot_general(
        spread_ref[...], table, (((1,), (1,)), ((), ())), preferred_element_type=F32
    )
    rows = out_refs[0].shape[0]
    for s in range(groups):
        out_refs[s][...] = product[s * rows : (s + 1) * rows].astype(BF16)


def back(mine, other, lane, pick, down, groups):
    rows, top = pick.shape
    slots, features, _ = down.shape
    fb = feature_block(features)
    whole = pl.BlockSpec(memory_space=pltpu.VMEM)
    each = rows // groups
    return pl.pallas_call(
        functools.partial(back_body, groups),
        grid=(features // fb,),
        out_shape=[jax.ShapeDtypeStruct((each, features), BF16)] * groups
        + [jax.ShapeDtypeStruct((rows, slots * top), BF16)],
        in_specs=[whole] * 4 + [pl.BlockSpec((slots, fb, top), lambda f: (0, f, 0))],
        out_specs=[pl.BlockSpec((each, fb), lambda f: (0, f))] * groups
        + [pl.BlockSpec((rows, slots * top), lambda f: (0, 0))],
        compiler_params=params(),
        cost_estimate=cost(2 * rows * down.size, down.size * 2 + rows * features * 2),
    )(mine, other, lane, pick, down)


def grads_body(groups, mine_ref, other_ref, lane_ref, pick_ref, low_ref, *rest):
    act_refs = rest[:groups]
    masked_refs = rest[groups : 2 * groups]
    down_ref, up_ref, largest_ref, lift_ref = rest[2 * groups :]
    slots, width, top = down_ref.shape

    @pl.when(pl.program_id(0) == 0)
    def _():
        lifted = ((mine_ref[...] + other_ref[...]) * lane_ref[...]).astype(BF16).astype(F32)
        for e in range(slots):
            part = jnp.where(pick_ref[...] == e, lifted, 0.0)
            lift_ref[e * top : (e + 1) * top, :] = part.T.astype(BF16)
        largest_ref[...] = jnp.zeros_like(largest_ref)

    acts = joined(act_refs)
    masked = joined(masked_refs)
    up = jnp.dot(lift_ref[...], masked, preferred_element_type=F32)
    down = lax.dot_general(
        acts, low_ref[...], (((0,), (0,)), ((), ())), preferred_element_type=F32
    )
    top_up = jnp.zeros((8, width), F32)
    for e in range(slots):
        part = up[e * top : (e + 1) * top]
        up_ref[e] = part
        top_up = jnp.maximum(top_up, jnp.max(jnp.abs(part).reshape(top // 8, 8, width), axis=0))
    top_down = jnp.zeros((8, top), F32)
    for e in range(slots):
        part = down[:, e * top : (e + 1) * top]
        down_ref[e] = part
        top_down = jnp.maximum(
            top_down, jnp.max(jnp.abs(part).reshape(width // 8, 8, top), axis=0)
        )
    for c in range(width // top):
        top_down = jnp.maximum(top_down, top_up[:, c * top : (c + 1) * top])
    largest_ref[...] = jnp.maximum(largest_ref[...], top_down)


def grads(mine, other, lane, pick, low, acts, masked, slots):
    groups = len(acts)
    rows, top = pick.shape
    each, features = acts[0].shape
    fb = feature_block(features)
    whole = pl.BlockSpec(memory_space=pltpu.VMEM)
    return pl.pallas_call(
        functools.partial(grads_body, groups),
        grid=(features // fb,),
        out_shape=[
            jax.ShapeDtypeStruct((slots, features, top), F32),
            jax.ShapeDtypeStruct((slots, top, features), F32),
            jax.ShapeDtypeStruct((8, top), F32),
        ],
        in_specs=[whole] * 5 + [pl.BlockSpec((each, fb), lambda f: (0, f))] * (2 * groups),
        out_specs=[
            pl.BlockSpec((slots, fb, top), lambda f: (0, f, 0)),
            pl.BlockSpec((slots, top, fb), lambda f: (0, 0, f)),
            pl.BlockSpec((8, top), lambda f: (0, 0)),
        ],
        scratch_shapes=[pltpu.VMEM((slots * top, rows), BF16)],
        compiler_params=params(),
        cost_estimate=cost(4 * rows * slots * top * features, 8 * slots * top * features),
    )(mine, other, lane, pick, low, *acts, *masked)


def finish_body(groups, slots, me_ref, adapter_ref, slot_ref, frozen_ref, *rest):
    back_refs = rest[:groups]
    out_ref, count_ref, rows_ref = rest[groups:]
    micro, windows, piece, width = out_ref.shape
    pair = WINDOWS_PER_OWNER * piece
    for s in range(groups):
        for m in range(micro):
            rows_ref[s * micro + m] = back_refs[s][...].astype(F32)[m * pair : (m + 1) * pair]
    for m in range(micro):
        for o in range(groups):
            count_ref[o] = 0
        for j in range(windows):
            owner = lax.div(slot_ref[adapter_ref[m, j]], slots)
            k = count_ref[owner]
            count_ref[owner] = k + 1
            s = lax.rem(owner + groups - me_ref[0], groups)
            both = rows_ref[s * micro + m]
            part = both[:piece]
            for other in range(1, WINDOWS_PER_OWNER):
                part = jnp.where(k == other, both[other * piece : (other + 1) * piece], part)
            first = (m * windows + j) * piece
            out_ref[m, j] = (frozen_ref[first : first + piece, :] + part).astype(BF16)


def finish(me, adapter, slot_per_adapter, frozen, backs, slots, shape):
    groups = len(backs)
    micro, windows, piece, features = shape
    rows, each = frozen.shape[0], backs[0].shape[0]
    fb = feature_block(features)
    return pl.pallas_call(
        functools.partial(finish_body, groups, slots),
        grid=(features // fb,),
        out_shape=jax.ShapeDtypeStruct(shape, BF16),
        in_specs=[SMEM_SPEC] * 3
        + [pl.BlockSpec((rows, fb), lambda f: (0, f))]
        + [pl.BlockSpec((each, fb), lambda f: (0, f))] * groups,
        out_specs=pl.BlockSpec((micro, windows, piece, fb), lambda f: (0, 0, 0, f)),
        scratch_shapes=[
            pltpu.SMEM((groups,), jnp.int32),
            pltpu.VMEM((groups * micro, WINDOWS_PER_OWNER * piece, fb), F32),
        ],
        compiler_params=params(),
        cost_estimate=cost(0, rows * features * 8),
    )(me, adapter, slot_per_adapter, frozen, *backs)


def partner(x, axis, bit):
    count = lax.axis_size(axis)
    return lax.ppermute(x, axis, [(i, i ^ bit) for i in range(count)])


def all_but_last_sum(x, axis):
    count = lax.axis_size(axis)
    bit = 1
    while bit < count:
        other = partner(x, axis, bit)
        if 2 * bit == count:
            return x, other
        x = x + other
        bit *= 2
    return x, jnp.zeros_like(x)


def all_max(x, axis):
    count = lax.axis_size(axis)
    bit = 1
    while bit < count:
        x = jnp.maximum(x, partner(x, axis, bit))
        bit *= 2
    return x


def local(
    activations,
    cotangent,
    frozen_weight_matrix,
    adapter_down_weights,
    adapter_up_weights,
    window_adapter,
    window_live_rows,
    rank_per_adapter,
    slot_per_adapter,
):
    groups = lax.axis_size("grp")
    slots, features, top = adapter_down_weights.shape
    piece = activations.shape[2]
    me = lax.axis_index("grp").astype(jnp.int32).reshape(1)

    def shifted(x, s):
        return lax.ppermute(x, "grp", [(i, (i + s) % groups) for i in range(groups)])

    def to_owners(blocks):
        return [blocks[0]] + [shifted(blocks[s], s) for s in range(1, groups)]

    masked_out = pack(
        cotangent, me, window_adapter, slot_per_adapter, window_live_rows, groups, slots, True
    )
    masked = to_owners(masked_out)
    masked_flat = flat(cotangent, window_live_rows)
    gathered = lax.all_gather(masked_flat, "tp", axis=1, tiled=True)
    adapters = [window_adapter] + [shifted(window_adapter, s) for s in range(1, groups)]
    acts_out = pack(
        activations, me, window_adapter, slot_per_adapter, window_live_rows, groups, slots, False
    )
    acts = to_owners(acts_out)
    pick, lane = meta(
        me, slot_per_adapter, rank_per_adapter, adapters, slots, piece, top
    )
    frozen = lax.dot_general(
        gathered,
        frozen_weight_matrix,
        (((1,), (1,)), ((), ())),
        preferred_element_type=F32,
    )
    low_mine, low_other = all_but_last_sum(
        project(masked, pick, adapter_up_weights, False), "tp"
    )
    *backs, low = back(low_mine, low_other, lane, pick, adapter_down_weights, groups)
    returned = [backs[0]] + [shifted(backs[s], groups - s) for s in range(1, groups)]
    lift_mine, lift_other = all_but_last_sum(
        project(acts, pick, adapter_down_weights, True), "tp"
    )
    down_sum, up_sum, largest = grads(
        lift_mine, lift_other, lane, pick, low, acts, masked, slots
    )
    highest = jnp.max(all_max(all_max(largest, "tp"), "grp"))
    factor = grad_limit / jnp.maximum(highest, grad_limit)
    input_grad = finish(
        me, window_adapter, slot_per_adapter, frozen, returned, slots, activations.shape
    )
    return (
        input_grad,
        (down_sum * factor).astype(BF16),
        (up_sum * factor).astype(BF16),
    )


def solution(mesh):
    return jax.shard_map(
        local,
        mesh=mesh,
        in_specs=(
            P("rep", "grp", None, "tp"),
            P("rep", "grp", None, "tp"),
            P("tp", None),
            P(("rep", "grp"), "tp", None),
            P(("rep", "grp"), None, "tp"),
            P("rep", "grp"),
            P("rep", "grp"),
            P("rep"),
            P("rep"),
        ),
        out_specs=(
            P("rep", "grp", None, "tp"),
            P(("rep", "grp"), "tp", None),
            P(("rep", "grp"), None, "tp"),
        ),
        check_vma=False,
    )
```

time: 380 us -> 203 us (0.53); the launches traced: 374 us -> 202 us
  matrix products: 128 us -> 23.7 us
  local copies, waits for them, and re-layouts: 62.6 us -> 9.9 us
  blocking collectives: 46.3 us -> 0 us
  Pallas kernels: 0 us -> 34.1 us
  waiting for transfers between devices: 33.9 us -> 61.5 us
  other arithmetic: 28.9 us -> 10.1 us
  starting transfers between devices: 57.8 us -> 48.3 us
    dot_general x27 -> x1, matrix products: 128 us -> 23.7 us  [local(): lax.dot_general(gathered, frozen_weight_matrix, (((1,), (1,)), ((), ())),...]
    ppermute x0 -> x20, waiting for transfers between devices: none -> 61.5 us  [the longest x12 50.9 us: shifted(): lax.ppermute(x, 'grp', [(i, (i + s) % groups) for i in range(groups)])]
    all_to_all x13 -> x0, starting transfers between devices: 57.6 us -> none  [the longest x3 16 us: local(): lax.all_to_all(send_acts[:, :, micro_step], 'grp', split_axis=0, concat_a...]
    ppermute x0 -> x20, starting transfers between devices: none -> 48.2 us  [the longest x12 31.7 us: shifted(): lax.ppermute(x, 'grp', [(i, (i + s) % groups) for i in range(groups)])]
    pallas_call x0 -> x9, Pallas kernels: none -> 34.1 us  [the longest x2 9.61 us: project(): pl.pallas_call(functools.partial(project_body, groups, down), grid=(slots...]
    all_to_all x13 -> x0, waiting for transfers between devices: 33.9 us -> none  [the longest x3 21.8 us: local(): lax.all_to_all(send_masked[:, :, micro_step], 'grp', split_axis=0, concat...]
    pmax x1 -> x0, blocking collectives: 30.4 us -> none  [local(): highest = lax.pmax(largest, ('grp', 'tp'))]
    reshape x7 -> x0, local copies, waits for them, and re-layouts: 22.2 us -> none  [the longest x1 5.08 us: local(): frozen_weight_gradient.reshape(micro_iterations, window_count, token_row_...]
  transfers between devices with their start and end apart: 15 -> 21, of which waited for: 7 -> 9; matrix products, arithmetic and copies ran while one was open for 46% -> 18% of each run, Pallas kernels for 0% -> 14%
where the time goes in v1:
time: 203 us; the launch traced here: 202 us
  waiting for transfers between devices  61.5 us (30%)
  starting transfers between devices  48.3 us (24%)
  Pallas kernels  34.1 us (17%)
  matrix products  23.7 us (12%)
  between operations  14.9 us (7%)
  other arithmetic  10.1 us (5%)
  local copies, waits for them, and re-layouts  9.9 us (5%)
    ppermute x12, waiting for transfers between devices, shifted(): lax.ppermute(x, 'grp', [(i, (i + s) % groups) for i in range(groups)])  50.9 us
    ppermute x12, starting transfers between devices, shifted(): lax.ppermute(x, 'grp', [(i, (i + s) % groups) for i in range(groups)])  31.7 us
    dot_general x1, matrix products, local(): lax.dot_general(gathered, frozen_weight_matrix, (((1,), (1,)), ((), ())),...  23.7 us
    ppermute x8, starting transfers between devices, partner(): return lax.ppermute(x, axis, [(i, i ^ bit) for i in range(count)])  16.5 us
    ppermute x8, waiting for transfers between devices, partner(): return lax.ppermute(x, axis, [(i, i ^ bit) for i in range(count)])  10.6 us
    unnamed x17, local copies, waits for them, and re-layouts  9.9 us
    pallas_call x2, Pallas kernels, project(): pl.pallas_call(functools.partial(project_body, groups, down), grid=(slots...  9.61 us
    pallas_call x1, Pallas kernels, grads(): pl.pallas_call(functools.partial(grads_body, groups), grid=(features // f...  8.62 us
  transfers between devices with their start and end apart: 21, of which 9 were waited for; matrix products, arithmetic and copies ran while one was open for 18% of the time, Pallas kernels for 14%

profile of v1, /device:TPU:0, one launch (start us, length us, event | category | flops | bytes accessed | tf_op | source)
XLA Modules:
  0.0 202.5 jit_solution(5815494131312978137)
XLA Ops:
  7.2 0.0 all-gather.2.cloned.1.call-start
  7.2 2.6 %copy.12.x_ref = bf16[3,8,20,2048]{3,2,1,0:T(8,128)(2,1)S(1)} copy(bf16[3,8,20,2048]{3,1,2,0:T(8,128)(2,1)} %param.10) | data formatting | bytes 3932160 | tf_op args[1]
  9.9 0.7 copy-done.2
  10.6 1.6 shard_map.112
  12.2 0.0 copy-start
  12.2 1.3 copy-done
  13.5 0.0 all-gather.2.cloned.1.call-update
  13.5 1.9 shard_map.114
  15.4 3.1 %collective-permute-start.3 = (bf16[120,2048]{1,0:T(8,128)(2,1)S(1)}, bf16[120,2048]{1,0:T(8,128)(2,1)S(1)}, u32[]{:S(2)}, u32[]{:S(2)}) collective-permute-start(bf16[120,2048]{1,0:T(8,128)(2,1)S(1)} %get-tuple-element.23), channel_id=1, source_target_pairs={{0,4},{4,8},{8,12},{12,0},{1,5},{5,9},{9,13},{13,1},{2,6},{6,10},{... | collective-permute-start | bytes 1474568 | tf_op jit(solution)/shard_map/ppermute | solution.py:419
  18.5 2.6 %collective-permute-start.4 = (bf16[120,2048]{1,0:T(8,128)(2,1)S(1)}, bf16[120,2048]{1,0:T(8,128)(2,1)S(1)}, u32[]{:S(2)}, u32[]{:S(2)}) collective-permute-start(bf16[120,2048]{1,0:T(8,128)(2,1)S(1)} %get-tuple-element.24), channel_id=1, source_target_pairs={{0,8},{4,12},{8,0},{12,4},{1,9},{5,13},{9,1},{13,5},{2,10},{6,14},... | collective-permute-start | bytes 1474568 | tf_op jit(solution)/shard_map/ppermute | solution.py:419
  21.1 1.3 collective-permute-start.5
  22.4 0.4 collective-permute-start.2
  22.9 1.7 collective-permute-start.1
  24.6 2.9 %copy.14.x_ref = bf16[3,8,20,2048]{3,2,1,0:T(8,128)(2,1)S(1)} copy(bf16[3,8,20,2048]{3,1,2,0:T(8,128)(2,1)} %param.9) | data formatting | bytes 3932160 | tf_op args[0]
  27.5 1.6 shard_map.118
  29.2 21.0 %collective-permute-done.2.rest_3_ = s32[3,8]{1,0:T(4,128)S(1)} collective-permute-done((s32[3,8]{1,0:T(4,128)S(1)}, s32[3,8]{1,0:T(4,128)S(1)}, u32[]{:S(2)}, u32[]{:S(2)}) %collective-permute-start.2) | collective-permute-done | bytes 128 | tf_op jit(solution)/shard_map/ppermute | solution.py:419
  50.2 13.9 %collective-permute-start = (s32[3,8]{1,0:T(4,128)S(1)}, s32[3,8]{1,0:T(4,128)S(1)}, u32[]{:S(2)}, u32[]{:S(2)}) collective-permute-start(s32[3,8]{1,0:T(4,128)S(1)} %copy-done.1), channel_id=1, source_target_pairs={{0,4},{4,8},{8,12},{12,0},{1,5},{5,9},{9,13},{13,1},{2,6},{6,10},{... | collective-permute-start | bytes 296 | tf_op jit(solution)/shard_map/ppermute | solution.py:419
  64.1 0.0 collective-permute-start.11
  64.1 1.3 collective-permute-done.rest_1_
  65.4 1.7 collective-permute-start.12
  67.1 2.9 %collective-permute-start.13 = (bf16[120,2048]{1,0:T(8,128)(2,1)S(1)}, bf16[120,2048]{1,0:T(8,128)(2,1)S(1)}, u32[]{:S(2)}, u32[]{:S(2)}) collective-permute-start(bf16[120,2048]{1,0:T(8,128)(2,1)S(1)} %get-tuple-element.34), channel_id=1, source_target_pairs={{0,12},{4,0},{8,4},{12,8},{1,13},{5,1},{9,5},{13,9},{2,14},{6,2},{... | collective-permute-start | bytes 1474568 | tf_op jit(solution)/shard_map/ppermute | solution.py:419
  70.1 1.5 shard_map.113
  71.6 4.9 %shard_map.115 = f32[480,128]{1,0:T(8,128)S(1)} custom-call(s32[480,128]{1,0:T(8,128)S(1)} %get-tuple-element.21.pick_ref, bf16[120,2048]{1,0:T(8,128)(2,1)S(1)} %get-tuple-element.22.rest_0_.rest_4_, bf16[120,2048]{1,0:T(8,128)(2,1)S(1)} %collective-permute-done.3.rest_1_.rest_5_, bf16[120,2048]{1,0:T(8,128)(2,1)S(1)} %collective-permute-done.4.rest_2_.rest_6_, ...), custom_call_target="tpu_custom_call" | custom-call | flops 2013265920 | bytes 6160384 | tf_op jit(solution)/shard_map/pallas_call | solution.py:210
  76.4 0.1 collective-permute-start.6
  76.5 3.6 %collective-permute-done.11.rest_1_ = bf16[120,2048]{1,0:T(8,128)(2,1)S(1)} collective-permute-done((bf16[120,2048]{1,0:T(8,128)(2,1)S(1)}, bf16[120,2048]{1,0:T(8,128)(2,1)S(1)}, u32[]{:S(2)}, u32[]{:S(2)}) %collective-permute-start.11) | collective-permute-done | bytes 491552 | tf_op jit(solution)/shard_map/ppermute | solution.py:419
  80.1 19.9 %collective-permute-done.12.rest_2_ = bf16[120,2048]{1,0:T(8,128)(2,1)S(1)} collective-permute-done((bf16[120,2048]{1,0:T(8,128)(2,1)S(1)}, bf16[120,2048]{1,0:T(8,128)(2,1)S(1)}, u32[]{:S(2)}, u32[]{:S(2)}) %collective-permute-start.12) | collective-permute-done | bytes 491552 | tf_op jit(solution)/shard_map/ppermute | solution.py:419
  100.1 4.8 %shard_map.119 = f32[480,128]{1,0:T(8,128)S(1)} custom-call(s32[480,128]{1,0:T(8,128)S(1)} %get-tuple-element.21.pick_ref, bf16[120,2048]{1,0:T(8,128)(2,1)S(1)} %get-tuple-element.31.rest_0_, bf16[120,2048]{1,0:T(8,128)(2,1)S(1)} %collective-permute-done.11.rest_1_, bf16[120,2048]{1,0:T(8,128)(2,1)S(1)} %collective-permute-done.12.rest_2_, ...), custom_call_target="tpu_custom_call" | custom-call | flops 2013265920 | bytes 6160384 | tf_op jit(solution)/shard_map/pallas_call | solution.py:210
  104.8 0.1 collective-permute-start.14
  105.0 1.6 collective-permute-start.7
  106.6 1.4 collective-permute-start.15
  108.0 5.8 %collective-permute-done.7.other_ref = f32[480,128]{1,0:T(8,128)S(1)} collective-permute-done((f32[480,128]{1,0:T(8,128)S(1)}, f32[480,128]{1,0:T(8,128)S(1)}, u32[]{:S(2)}, u32[]{:S(2)}) %collective-permute-start.7) | collective-permute-done | bytes 245792 | tf_op jit(solution)/shard_map/ppermute | solution.py:378
  113.8 5.6 %shard_map.116 = (bf16[120,2048]{1,0:T(8,128)(2,1)S(1)}, bf16[120,2048]{1,0:T(8,128)(2,1)}, bf16[120,2048]{1,0:T(8,128)(2,1)S(1)}, bf16[120,2048]{1,0:T(8,128)(2,1)S(1)}, bf16[480,1024]{1,0:T(8,128)(2,1)S(1)}) custom-call(f32[480,128]{1,0:T(8,128)S(1)} %add.6.mine_ref, f32[480,128]{1,0:T(8,128)S(1)} %collective-permute-done.7.other_ref, ...), custom_call_target="tpu_custom_call" | custom-call | flops 2013265920 | bytes 6160384 | tf_op jit(solution)/shard_map/pallas_call | solution.py:254
  119.4 8.6 %shard_map.120 = (f32[8,2048,128]{2,1,0:T(8,128)}, f32[8,128,2048]{2,1,0:T(8,128)}, f32[8,128]{1,0:T(8,128)S(1)}) custom-call(f32[480,128]{1,0:T(8,128)S(1)} %add.7.mine_ref, f32[480,128]{1,0:T(8,128)S(1)} %collective-permute-done.15.other_ref, f32[480,128]{1,0:T(8,128)S(1)} %get-tuple-element.26.lane_ref, s32[480,128]{1,0:T(8,128)S(1)} %get-tuple-element.21.pick_ref, ...), custom_call_target="tpu_custom_call" | custom-call | flops 4026531840 | bytes 16777216 | tf_op jit(solution)/shard_map/pallas_call | solution.py:310
  128.0 1.2 collective-permute-done.16
  129.2 1.5 collective-permute-start.17
  130.7 2.1 %collective-permute-done.17 = f32[8,128]{1,0:T(8,128)S(1)} collective-permute-done((f32[8,128]{1,0:T(8,128)S(1)}, f32[8,128]{1,0:T(8,128)S(1)}, u32[]{:S(2)}, u32[]{:S(2)}) %collective-permute-start.17) | collective-permute-done | bytes 4128 | tf_op jit(solution)/shard_map/ppermute | solution.py:378
  132.8 10.8 %collective-permute-start.18 = (f32[8,128]{1,0:T(8,128)S(1)}, f32[8,128]{1,0:T(8,128)S(1)}, u32[]{:S(2)}, u32[]{:S(2)}) collective-permute-start(f32[8,128]{1,0:T(8,128)S(1)} %max.16), channel_id=1, source_target_pairs={{0,4},{4,0},{8,12},{12,8},{1,5},{5,1},{9,13},{13,9},{2,6},{6,2},{1... | collective-permute-start | bytes 12296 | tf_op jit(solution)/shard_map/ppermute | solution.py:378
  143.6 1.6 collective-permute-done.18
  145.2 1.0 collective-permute-start.19
  146.2 3.4 %collective-permute-start.8 = (bf16[120,2048]{1,0:T(8,128)(2,1)}, bf16[120,2048]{1,0:T(8,128)(2,1)S(1)}, u32[]{:S(2)}, u32[]{:S(2)}) collective-permute-start(bf16[120,2048]{1,0:T(8,128)(2,1)} %get-tuple-element.28), channel_id=1, source_target_pairs={{0,12},{4,0},{8,4},{12,8},{1,13},{5,1},{9,5},{13,9},{2,14},{6,2},{... | collective-permute-start | bytes 1474568 | tf_op jit(solution)/shard_map/ppermute | solution.py:419
  149.6 0.6 collective-permute-start.10
  150.2 0.6 maximum_reduce_fusion
  151.5 6.7 %multiply_convert_fusion = bf16[8,128,2048]{2,1,0:T(8,128)(2,1)} fusion(f32[8,128,2048]{2,1,0:T(8,128)} %get-tuple-element.38, f32[]{:T(128)S(6)} %div.3), kind=kLoop, calls=%fused_computation | loop fusion | flops 4194304 | bytes 12582916 | tf_op jit(solution)/shard_map/convert_element_type | solution.py:463
  158.2 2.7 %multiply_convert_fusion.1 = bf16[8,2048,128]{2,1,0:T(8,128)(2,1)} fusion(f32[8,2048,128]{2,1,0:T(8,128)S(1)} %copy-done.6, f32[]{:T(128)S(6)} %div.3), kind=kLoop, calls=%fused_computation.1 | loop fusion | flops 4194304 | bytes 12582916 | tf_op jit(solution)/shard_map/convert_element_type | solution.py:462
  160.9 23.7 %fusion.frozen_ref = f32[480,2048]{1,0:T(8,128)} fusion(bf16[480,8192]{1,0:T(8,128)(2,1)} %all-gather.2.cloned.1.call-done, bf16[2048,8192]{1,0:T(8,128)(2,1)} %param.11), kind=kOutput, calls=%fused_computation.3 | convolution fusion | flops 16106127360 | bytes 45350912 | tf_op jit(solution)/shard_map/dot_general | solution.py:438
  184.6 5.0 %collective-permute-done.9.rest_2_ = bf16[120,2048]{1,0:T(8,128)(2,1)S(1)} collective-permute-done((bf16[120,2048]{1,0:T(8,128)(2,1)S(1)}, bf16[120,2048]{1,0:T(8,128)(2,1)S(1)}, u32[]{:S(2)}, u32[]{:S(2)}) %collective-permute-start.9) | collective-permute-done | bytes 491552 | tf_op jit(solution)/shard_map/ppermute | solution.py:419
  189.6 3.6 %shard_map.117 = bf16[3,8,20,2048]{3,2,1,0:T(8,128)(2,1)S(1)} custom-call(s32[1]{0:T(128)} %bitcast.me_ref, s32[3,8]{1,0:T(4,128)S(1)} %copy-done.1, s32[32]{0:T(128)S(1)} %copy-done.4, f32[480,2048]{1,0:T(8,128)} %fusion.frozen_ref, bf16[120,2048]{1,0:T(8,128)(2,1)S(1)} %get-tuple-element.27.rest_0_, bf16[120,2048]{1,0:T(8,128)(2,1)S(1)} %collective-permute-done.8.rest_1_, ...), custom_call_target="tpu_custom_call" | custom-call | bytes 7864320 | tf_op jit(solution)/shard_map/pallas_call | solution.py:359
  193.3 2.4 %copy.15 = bf16[3,8,20,2048]{3,1,2,0:T(8,128)(2,1)} copy(bf16[3,8,20,2048]{3,2,1,0:T(8,128)(2,1)S(1)} %shard_map.117) | data formatting | bytes 3932160
  (30 shorter events, 0.1 us)
Async XLA Ops:
  7.2 6.3 %copy-start.3 = (s32[3,8]{1,0:T(4,128)S(1)}, s32[3,8]{1,0:T(4,128)}, u32[]{:S(2)}) copy-start(s32[3,8]{1,0:T(4,128)} %live_ref.5) | copy-start | bytes 292
  7.2 6.3 %copy-start.1 = (s32[3,8]{1,0:T(4,128)S(1)}, s32[3,8]{1,0:T(4,128)}, u32[]{:S(2)}) copy-start(s32[3,8]{1,0:T(4,128)} %adapter_ref.5) | copy-start | bytes 292
  7.2 6.3 %copy-start.4 = (s32[32]{0:T(128)S(1)}, s32[32]{0:T(128)}, u32[]{:S(2)}) copy-start(s32[32]{0:T(128)} %slot_ref.7) | copy-start | bytes 388
  7.2 153.7 %all-gather.2.cloned.1.call-start = ((), (), s32[]{:S(2)}) async-start(), calls=%async_computation | async-start | bytes 9830400 | tf_op jit(solution)/shard_map/all_gather | solution.py:429
  9.9 0.7 copy-start.2
  10.6 59.5 %copy-start.5 = (s32[32]{0:T(128)S(1)}, s32[32]{0:T(128)}, u32[]{:S(2)}) copy-start(s32[32]{0:T(128)} %rank_ref.1) | copy-start | bytes 388
  12.2 1.3 copy-start
  15.4 51.7 %collective-permute-start.3 = (bf16[120,2048]{1,0:T(8,128)(2,1)S(1)}, bf16[120,2048]{1,0:T(8,128)(2,1)S(1)}, u32[]{:S(2)}, u32[]{:S(2)}) collective-permute-start(bf16[120,2048]{1,0:T(8,128)(2,1)S(1)} %get-tuple-element.23), channel_id=1, source_target_pairs={{0,4},{4,8},{8,12},{12,0},{1,5},{5,9},{9,13},{13,1},{2,6},{6,10},{... | collective-permute-start | bytes 1474568 | tf_op jit(solution)/shard_map/ppermute | solution.py:419
  18.5 53.0 %collective-permute-start.4 = (bf16[120,2048]{1,0:T(8,128)(2,1)S(1)}, bf16[120,2048]{1,0:T(8,128)(2,1)S(1)}, u32[]{:S(2)}, u32[]{:S(2)}) collective-permute-start(bf16[120,2048]{1,0:T(8,128)(2,1)S(1)} %get-tuple-element.24), channel_id=1, source_target_pairs={{0,8},{4,12},{8,0},{12,4},{1,9},{5,13},{9,1},{13,5},{2,10},{6,14},... | collective-permute-start | bytes 1474568 | tf_op jit(solution)/shard_map/ppermute | solution.py:419
  21.1 50.5 %collective-permute-start.5 = (bf16[120,2048]{1,0:T(8,128)(2,1)S(1)}, bf16[120,2048]{1,0:T(8,128)(2,1)S(1)}, u32[]{:S(2)}, u32[]{:S(2)}) collective-permute-start(bf16[120,2048]{1,0:T(8,128)(2,1)S(1)} %get-tuple-element.25), channel_id=1, source_target_pairs={{0,12},{4,0},{8,4},{12,8},{1,13},{5,1},{9,5},{13,9},{2,14},{6,2},{... | collective-permute-start | bytes 1474568 | tf_op jit(solution)/shard_map/ppermute | solution.py:419
  22.4 27.7 %collective-permute-start.2 = (s32[3,8]{1,0:T(4,128)S(1)}, s32[3,8]{1,0:T(4,128)S(1)}, u32[]{:S(2)}, u32[]{:S(2)}) collective-permute-start(s32[3,8]{1,0:T(4,128)S(1)} %copy-done.1), channel_id=1, source_target_pairs={{0,12},{4,0},{8,4},{12,8},{1,13},{5,1},{9,5},{13,9},{2,14},{6,2},{... | collective-permute-start | bytes 296 | tf_op jit(solution)/shard_map/ppermute | solution.py:419
  22.9 41.2 %collective-permute-start.1 = (s32[3,8]{1,0:T(4,128)S(1)}, s32[3,8]{1,0:T(4,128)S(1)}, u32[]{:S(2)}, u32[]{:S(2)}) collective-permute-start(s32[3,8]{1,0:T(4,128)S(1)} %copy-done.1), channel_id=1, source_target_pairs={{0,8},{4,12},{8,0},{12,4},{1,9},{5,13},{9,1},{13,5},{2,10},{6,14},... | collective-permute-start | bytes 296 | tf_op jit(solution)/shard_map/ppermute | solution.py:419
  50.2 15.3 %collective-permute-start = (s32[3,8]{1,0:T(4,128)S(1)}, s32[3,8]{1,0:T(4,128)S(1)}, u32[]{:S(2)}, u32[]{:S(2)}) collective-permute-start(s32[3,8]{1,0:T(4,128)S(1)} %copy-done.1), channel_id=1, source_target_pairs={{0,4},{4,8},{8,12},{12,0},{1,5},{5,9},{9,13},{13,1},{2,6},{6,10},{... | collective-permute-start | bytes 296 | tf_op jit(solution)/shard_map/ppermute | solution.py:419
  64.1 16.0 %collective-permute-start.11 = (bf16[120,2048]{1,0:T(8,128)(2,1)S(1)}, bf16[120,2048]{1,0:T(8,128)(2,1)S(1)}, u32[]{:S(2)}, u32[]{:S(2)}) collective-permute-start(bf16[120,2048]{1,0:T(8,128)(2,1)S(1)} %get-tuple-element.32), channel_id=1, source_target_pairs={{0,4},{4,8},{8,12},{12,0},{1,5},{5,9},{9,13},{13,1},{2,6},{6,10},{... | collective-permute-start | bytes 1474568 | tf_op jit(solution)/shard_map/ppermute | solution.py:419
  65.4 34.6 %collective-permute-start.12 = (bf16[120,2048]{1,0:T(8,128)(2,1)S(1)}, bf16[120,2048]{1,0:T(8,128)(2,1)S(1)}, u32[]{:S(2)}, u32[]{:S(2)}) collective-permute-start(bf16[120,2048]{1,0:T(8,128)(2,1)S(1)} %get-tuple-element.33), channel_id=1, source_target_pairs={{0,8},{4,12},{8,0},{12,4},{1,9},{5,13},{9,1},{13,5},{2,10},{6,14},... | collective-permute-start | bytes 1474568 | tf_op jit(solution)/shard_map/ppermute | solution.py:419
  67.1 32.9 %collective-permute-start.13 = (bf16[120,2048]{1,0:T(8,128)(2,1)S(1)}, bf16[120,2048]{1,0:T(8,128)(2,1)S(1)}, u32[]{:S(2)}, u32[]{:S(2)}) collective-permute-start(bf16[120,2048]{1,0:T(8,128)(2,1)S(1)} %get-tuple-element.34), channel_id=1, source_target_pairs={{0,12},{4,0},{8,4},{12,8},{1,13},{5,1},{9,5},{13,9},{2,14},{6,2},{... | collective-permute-start | bytes 1474568 | tf_op jit(solution)/shard_map/ppermute | solution.py:419
  76.4 28.5 %collective-permute-start.6 = (f32[480,128]{1,0:T(8,128)S(1)}, f32[480,128]{1,0:T(8,128)S(1)}, u32[]{:S(2)}, u32[]{:S(2)}) collective-permute-start(f32[480,128]{1,0:T(8,128)S(1)} %shard_map.115), channel_id=1, source_target_pairs={{0,1},{1,0},{2,3},{3,2},{4,5},{5,4},{6,7},{7,6},{8,9},{9,8},{10,11... | collective-permute-start | bytes 737288 | tf_op jit(solution)/shard_map/ppermute | solution.py:378
  104.8 1.7 collective-permute-start.14
  105.0 8.8 %collective-permute-start.7 = (f32[480,128]{1,0:T(8,128)S(1)}, f32[480,128]{1,0:T(8,128)S(1)}, u32[]{:S(2)}, u32[]{:S(2)}) collective-permute-start(f32[480,128]{1,0:T(8,128)S(1)} %add.6.mine_ref), channel_id=1, source_target_pairs={{0,2},{1,3},{2,0},{3,1},{4,6},{5,7},{6,4},{7,5},{8,10},{9,11},{10,... | collective-permute-start | bytes 737288 | tf_op jit(solution)/shard_map/ppermute | solution.py:378
  106.6 12.8 %collective-permute-start.15 = (f32[480,128]{1,0:T(8,128)S(1)}, f32[480,128]{1,0:T(8,128)S(1)}, u32[]{:S(2)}, u32[]{:S(2)}) collective-permute-start(f32[480,128]{1,0:T(8,128)S(1)} %add.7.mine_ref), channel_id=1, source_target_pairs={{0,2},{1,3},{2,0},{3,1},{4,6},{5,7},{6,4},{7,5},{8,10},{9,11},{10,... | collective-permute-start | bytes 737288 | tf_op jit(solution)/shard_map/ppermute | solution.py:378
  128.0 1.2 collective-permute-start.16
  129.2 3.6 %collective-permute-start.17 = (f32[8,128]{1,0:T(8,128)S(1)}, f32[8,128]{1,0:T(8,128)S(1)}, u32[]{:S(2)}, u32[]{:S(2)}) collective-permute-start(f32[8,128]{1,0:T(8,128)S(1)} %max.15), channel_id=1, source_target_pairs={{0,2},{1,3},{2,0},{3,1},{4,6},{5,7},{6,4},{7,5},{8,10},{9,11},{10,... | collective-permute-start | bytes 12296 | tf_op jit(solution)/shard_map/ppermute | solution.py:378
  132.8 12.4 %collective-permute-start.18 = (f32[8,128]{1,0:T(8,128)S(1)}, f32[8,128]{1,0:T(8,128)S(1)}, u32[]{:S(2)}, u32[]{:S(2)}) collective-permute-start(f32[8,128]{1,0:T(8,128)S(1)} %max.16), channel_id=1, source_target_pairs={{0,4},{4,0},{8,12},{12,8},{1,5},{5,1},{9,13},{13,9},{2,6},{6,2},{1... | collective-permute-start | bytes 12296 | tf_op jit(solution)/shard_map/ppermute | solution.py:378
  145.2 5.0 %collective-permute-start.19 = (f32[8,128]{1,0:T(8,128)S(1)}, f32[8,128]{1,0:T(8,128)S(1)}, u32[]{:S(2)}, u32[]{:S(2)}) collective-permute-start(f32[8,128]{1,0:T(8,128)S(1)} %max.17), channel_id=1, source_target_pairs={{0,8},{4,12},{8,0},{12,4},{1,9},{5,13},{9,1},{13,5},{2,10},{6,14},... | collective-permute-start | bytes 12296 | tf_op jit(solution)/shard_map/ppermute | solution.py:378
  146.2 38.4 %collective-permute-start.8 = (bf16[120,2048]{1,0:T(8,128)(2,1)}, bf16[120,2048]{1,0:T(8,128)(2,1)S(1)}, u32[]{:S(2)}, u32[]{:S(2)}) collective-permute-start(bf16[120,2048]{1,0:T(8,128)(2,1)} %get-tuple-element.28), channel_id=1, source_target_pairs={{0,12},{4,0},{8,4},{12,8},{1,13},{5,1},{9,5},{13,9},{2,14},{6,2},{... | collective-permute-start | bytes 1474568 | tf_op jit(solution)/shard_map/ppermute | solution.py:419
  149.6 40.0 %collective-permute-start.9 = (bf16[120,2048]{1,0:T(8,128)(2,1)S(1)}, bf16[120,2048]{1,0:T(8,128)(2,1)S(1)}, u32[]{:S(2)}, u32[]{:S(2)}) collective-permute-start(bf16[120,2048]{1,0:T(8,128)(2,1)S(1)} %get-tuple-element.29), channel_id=1, source_target_pairs={{0,8},{4,12},{8,0},{12,4},{1,9},{5,13},{9,1},{13,5},{2,10},{6,14},... | collective-permute-start | bytes 1474568 | tf_op jit(solution)/shard_map/ppermute | solution.py:419
  149.6 40.0 %collective-permute-start.10 = (bf16[120,2048]{1,0:T(8,128)(2,1)S(1)}, bf16[120,2048]{1,0:T(8,128)(2,1)S(1)}, u32[]{:S(2)}, u32[]{:S(2)}) collective-permute-start(bf16[120,2048]{1,0:T(8,128)(2,1)S(1)} %get-tuple-element.30), channel_id=1, source_target_pairs={{0,4},{4,8},{8,12},{12,0},{1,5},{5,9},{9,13},{13,1},{2,6},{6,10},{... | collective-permute-start | bytes 1474568 | tf_op jit(solution)/shard_map/ppermute | solution.py:419
  151.5 6.7 %copy-start.6 = (f32[8,2048,128]{2,1,0:T(8,128)S(1)}, f32[8,2048,128]{2,1,0:T(8,128)}, u32[]{:S(2)}) copy-start(f32[8,2048,128]{2,1,0:T(8,128)} %get-tuple-element.36) | copy-start | bytes 25165828
Sparse Core Ops, SparseCore 0:
  13.6 57.9 all-gather.1

commit v2 on v0

v2 whole, which is shorter than its diff:
```python
import functools

import jax
import jax.numpy as jnp
from jax import lax
from jax.experimental import pallas as pl
from jax.experimental.pallas import tpu as pltpu
from jax.sharding import PartitionSpec as P

WINDOWS_PER_OWNER = 2
NOTES = 8

grad_limit = 4.0

BF16 = jnp.bfloat16
F32 = jnp.float32
VMEM_LIMIT = 60
WHOLE = pl.BlockSpec(memory_space=pltpu.VMEM)
ANY = pl.BlockSpec(memory_space=pl.ANY)


def params(limit=VMEM_LIMIT):
    return pltpu.CompilerParams(
        dimension_semantics=("arbitrary",), vmem_limit_bytes=limit * 1024 * 1024
    )


SMALL = pl.CostEstimate(flops=1000000, bytes_accessed=100000, transcendentals=0)


def feature_block(features, wanted=512):
    return wanted if features % wanted == 0 else features


def window_order(adapter_ref, slot_ref, order_ref, count_ref, groups, slots):
    micro, windows = adapter_ref.shape
    for m in range(micro):
        for o in range(groups):
            count_ref[o] = 0
            for k in range(WINDOWS_PER_OWNER):
                order_ref[(m * groups + o) * WINDOWS_PER_OWNER + k] = -1
        for j in range(windows):
            owner = lax.div(slot_ref[adapter_ref[m, j]], slots)
            k = jnp.minimum(count_ref[owner], WINDOWS_PER_OWNER - 1)
            order_ref[(m * groups + owner) * WINDOWS_PER_OWNER + k] = j
            count_ref[owner] = k + 1


def live_rows_native(live_ref, m, windows):
    sublane = lax.broadcasted_iota(jnp.int32, (windows, 128), 0)
    live = jnp.zeros((windows, 128), jnp.int32)
    for j in range(windows):
        live = jnp.where(sublane == j, live_ref[m, j], live)
    return live


def route_body(
    groups,
    slots,
    piece,
    adapter_in,
    slot_in,
    rank_in,
    live_in,
    x_ref,
    packed_ref,
    flat_ref,
    hot_ref,
    adapter_ref,
    slot_ref,
    rank_ref,
    live_ref,
    arrived,
    order_ref,
    count_ref,
    target_ref,
    alive_ref,
    note_ref,
):
    micro, windows = adapter_ref.shape

    @pl.when(pl.program_id(0) == 0)
    def _():
        copies = [
            pltpu.make_async_copy(there, here, arrived.at[i])
            for i, (there, here) in enumerate(
                (
                    (adapter_in, adapter_ref),
                    (slot_in, slot_ref),
                    (rank_in, rank_ref),
                    (live_in, live_ref),
                )
            )
        ]
        for copy in copies:
            copy.start()
        for copy in copies:
            copy.wait()
        window_order(adapter_ref, slot_ref, order_ref, count_ref, groups, slots)
        row = lax.broadcasted_iota(jnp.int32, (piece, 128), 0)
        note_row = lax.broadcasted_iota(jnp.int32, (NOTES, 128), 0)
        note_column = lax.broadcasted_iota(jnp.int32, (NOTES, 128), 1)
        note_ref[...] = jnp.zeros_like(note_ref)
        for o in range(groups):
            note = jnp.zeros((NOTES, 128), jnp.int32)
            for m in range(micro):
                for k in range(WINDOWS_PER_OWNER):
                    j = order_ref[(m * groups + o) * WINDOWS_PER_OWNER + k]
                    at = jnp.maximum(j, 0)
                    adapter = adapter_ref[m, at]
                    live = jnp.where(j >= 0, live_ref[m, at], 0)
                    limit = jnp.where(j >= 0, rank_ref[adapter], 0)
                    first = ((o * micro + m) * WINDOWS_PER_OWNER + k) * piece
                    target_ref[first : first + piece, :] = jnp.where(
                        row < live, (m * piece + row) * windows + j, -1
                    )
                    value = jnp.where(note_row == 0, lax.rem(slot_ref[adapter], slots), limit)
                    note = jnp.where(note_column == m * WINDOWS_PER_OWNER + k, value, note)
            note_ref[o, :, :128] = note.astype(F32)
        column = lax.broadcasted_iota(jnp.int32, hot_ref.shape, 1)
        hot_ref[...] = jnp.where(column == target_ref[:, :1], 1.0, 0.0).astype(BF16)
        for m in range(micro):
            live = live_rows_native(live_ref, m, windows)
            for p in range(piece):
                first = (m * piece + p) * windows
                alive_ref[first : first + windows, :] = jnp.where(live > p, 1.0, 0.0)

    x = x_ref[...]
    packed = jnp.dot(hot_ref[...], x, preferred_element_type=F32)
    rows = packed.shape[0] // groups
    parts = []
    for o in range(groups):
        parts += [packed[o * rows : (o + 1) * rows], note_ref[o]]
    packed_ref[...] = jnp.concatenate(parts, axis=0).astype(BF16)
    flat_ref[...] = jnp.where(alive_ref[:, :1] > 0.0, x.astype(F32), 0.0).astype(BF16)


def route(x, adapter, slot_per_adapter, rank_per_adapter, live, groups, slots):
    micro, windows = adapter.shape
    native, features = x.shape
    piece = native // (micro * windows)
    rows = groups * micro * WINDOWS_PER_OWNER * piece
    sent = rows + groups * NOTES
    fb = feature_block(features)
    far = pl.BlockSpec(memory_space=pltpu.MemorySpace.HBM)
    return pl.pallas_call(
        functools.partial(route_body, groups, slots, piece),
        grid=(features // fb,),
        out_shape=[
            jax.ShapeDtypeStruct((sent, features), BF16),
            jax.ShapeDtypeStruct((native, features), BF16),
            jax.ShapeDtypeStruct((rows, native), BF16),
        ],
        in_specs=[far] * 4 + [pl.BlockSpec((native, fb), lambda f: (0, f))],
        out_specs=[
            pl.BlockSpec((sent, fb), lambda f: (0, f)),
            pl.BlockSpec((native, fb), lambda f: (0, f)),
            pl.BlockSpec((rows, native), lambda f: (0, 0)),
        ],
        scratch_shapes=[
            pltpu.SMEM(adapter.shape, jnp.int32),
            pltpu.SMEM(slot_per_adapter.shape, jnp.int32),
            pltpu.SMEM(rank_per_adapter.shape, jnp.int32),
            pltpu.SMEM(live.shape, jnp.int32),
            pltpu.SemaphoreType.DMA((4,)),
            pltpu.SMEM((micro * groups * WINDOWS_PER_OWNER,), jnp.int32),
            pltpu.SMEM((groups,), jnp.int32),
            pltpu.VMEM((rows, 128), jnp.int32),
            pltpu.VMEM((native, 128), F32),
            pltpu.VMEM((groups, NOTES, fb), F32),
        ],
        compiler_params=params(),
        cost_estimate=SMALL,
    )(adapter, slot_per_adapter, rank_per_adapter, live, x)


def pack_body(hot_ref, x_ref, out_ref, hot_back_ref):
    @pl.when(pl.program_id(0) == 0)
    def _():
        hot_back_ref[...] = hot_ref[...].astype(F32).T.astype(BF16)

    out_ref[...] = jnp.dot(hot_ref[...], x_ref[...], preferred_element_type=F32).astype(BF16)


def pack(x, hot):
    native, features = x.shape
    rows = hot.shape[0]
    fb = feature_block(features)
    return pl.pallas_call(
        pack_body,
        grid=(features // fb,),
        out_shape=[
            jax.ShapeDtypeStruct((rows, features), BF16),
            jax.ShapeDtypeStruct((native, rows), BF16),
        ],
        in_specs=[WHOLE, pl.BlockSpec((native, fb), lambda f: (0, f))],
        out_specs=[
            pl.BlockSpec((rows, fb), lambda f: (0, f)),
            pl.BlockSpec((native, rows), lambda f: (0, 0)),
        ],
        compiler_params=params(),
        cost_estimate=SMALL,
    )(hot, x)


def frozen_body(parts, more, source_ref, *rest):
    row_refs, weight_refs, out_ref = rest[:parts], rest[parts : 2 * parts], rest[-1]
    total = rest[2 * parts][...] if more else jnp.zeros(out_ref.shape, F32)
    for q in range(parts):
        total += lax.dot_general(
            row_refs[q][...],
            weight_refs[q][...],
            (((1,), (1,)), ((), ())),
            preferred_element_type=F32,
        )
    out_ref[...] = total


def frozen_product(sources, row_blocks, weights, so_far, *after):
    parts = len(row_blocks)
    rows, features = row_blocks[0].shape
    inputs = weights.shape[0]
    nb = 256 if inputs % 256 == 0 else inputs

    def columns(q):
        return pl.BlockSpec((nb, features), lambda n, source: (n, source[q]))

    more = () if so_far is None else (so_far,)
    out_spec = pl.BlockSpec((rows, nb), lambda n, source: (0, n))
    return pl.pallas_call(
        functools.partial(frozen_body, parts, so_far is not None),
        grid_spec=pltpu.PrefetchScalarGridSpec(
            num_scalar_prefetch=1,
            grid=(inputs // nb,),
            in_specs=[WHOLE] * parts
            + [columns(q) for q in range(parts)]
            + [out_spec] * len(more)
            + [ANY] * len(after),
            out_specs=out_spec,
        ),
        out_shape=jax.ShapeDtypeStruct((rows, inputs), F32),
        compiler_params=params(),
        cost_estimate=SMALL,
    )(sources, *row_blocks, *([weights] * parts), *more, *after)


def receive_body(
    groups, windows, piece, sent_ref, table_ref, *rest
):
    out_ref, pick_ref, lane_ref, rows_ref, note_ref = rest[-5:]
    top = out_ref.shape[1]
    count = windows * piece
    together = table_ref.shape[0]
    step = pl.program_id(0)

    @pl.when(step == 0)
    def _():
        sent = sent_ref[...].astype(F32)
        rows_ref[...] = jnp.concatenate(
            [sent[g * (count + NOTES) : g * (count + NOTES) + count] for g in range(groups)], axis=0
        ).astype(BF16)
        column = lax.broadcasted_iota(jnp.int32, (piece, top), 1).astype(F32)
        for g in range(groups):
            first = g * (count + NOTES) + count
            note_ref[...] = sent[first : first + NOTES, :128]
            for at in range(windows):
                limit = note_ref[1:2, at : at + 1]
                first = (g * windows + at) * piece
                lane_ref[first : first + piece, :] = jnp.where(
                    column < limit, (top // 8) / jnp.maximum(limit, 1.0), 0.0
                )
                pick_ref[first : first + piece, :] = jnp.broadcast_to(
                    note_ref[0:1, at : at + 1], (piece, top)
                )
        out_ref[...] = jnp.zeros_like(out_ref)

    table = table_ref[...].reshape(together * top, table_ref.shape[2])
    product = lax.dot_general(
        rows_ref[...], table, (((1,), (1,)), ((), ())), preferred_element_type=F32
    )
    out_ref[...] = choose(pick_ref, product, out_ref[...], step * together, together)


def choose(pick_ref, product, chosen, first, together):
    top = chosen.shape[1]
    for i in range(together):
        here = pick_ref[...] == (first + i).astype(F32)
        chosen = jnp.where(here, product[:, i * top : (i + 1) * top], chosen)
    return chosen


def receive(sent, table, groups, windows, piece, *after):
    slots, top, features = table.shape
    rows = groups * windows * piece
    together = 2 if slots % 2 == 0 else 1
    fixed = pl.BlockSpec((rows, top), lambda e: (0, 0))
    return pl.pallas_call(
        functools.partial(receive_body, groups, windows, piece),
        grid=(slots // together,),
        out_shape=[jax.ShapeDtypeStruct((rows, top), F32)] * 3
        + [jax.ShapeDtypeStruct((rows, features), BF16)],
        in_specs=[WHOLE, pl.BlockSpec((together, top, features), lambda e: (e, 0, 0))]
        + [ANY] * len(after),
        out_specs=[fixed] * 3 + [pl.BlockSpec((rows, features), lambda e: (0, 0))],
        scratch_shapes=[pltpu.VMEM((NOTES, 128), F32)],
        compiler_params=params(),
        cost_estimate=SMALL,
    )(sent, table, *after)


def gate_body(*refs):
    pass


def gate(x, *after):
    return pl.pallas_call(
        gate_body,
        out_shape=jax.ShapeDtypeStruct(x.shape, x.dtype),
        in_specs=[ANY] * (1 + len(after)),
        out_specs=ANY,
        input_output_aliases={0: 0},
        cost_estimate=SMALL,
    )(x, *after)


def project_body(pick_ref, rows_ref, table_ref, *rest):
    out_ref = rest[-1]
    step = pl.program_id(0)
    together = table_ref.shape[0]
    table = jnp.concatenate([table_ref[i] for i in range(together)], axis=1)
    product = jnp.dot(rows_ref[...], table, preferred_element_type=F32)
    chosen = jnp.where(step == 0, jnp.zeros(out_ref.shape, F32), out_ref[...])
    out_ref[...] = choose(pick_ref, product, chosen, step * together, together)


def project(rows, pick, table, *after):
    count, top = pick.shape
    slots = table.shape[0]
    together = 2 if slots % 2 == 0 else 1
    return pl.pallas_call(
        project_body,
        grid=(slots // together,),
        out_shape=jax.ShapeDtypeStruct((count, top), F32),
        in_specs=[
            WHOLE,
            WHOLE,
            pl.BlockSpec((together,) + table.shape[1:], lambda e: (e, 0, 0)),
        ]
        + [ANY] * len(after),
        out_specs=pl.BlockSpec((count, top), lambda e: (0, 0)),
        compiler_params=params(),
        cost_estimate=SMALL,
    )(pick, rows, table, *after)


def spread(values, pick, slots):
    return jnp.concatenate(
        [jnp.where(pick == float(e), values, 0.0) for e in range(slots)], axis=1
    ).astype(BF16)


def back_body(mine_ref, other_ref, lane_ref, pick_ref, down_ref, *rest):
    out_ref, spread_ref = rest[-2:]
    slots, width, top = down_ref.shape

    @pl.when(pl.program_id(0) == 0)
    def _():
        lowered = ((mine_ref[...] + other_ref[...]) * lane_ref[...]).astype(BF16).astype(F32)
        spread_ref[...] = spread(lowered, pick_ref[...], slots)

    table = jnp.concatenate([down_ref[e] for e in range(slots)], axis=1)
    out_ref[...] = lax.dot_general(
        spread_ref[...], table, (((1,), (1,)), ((), ())), preferred_element_type=F32
    ).astype(BF16)


def back(mine, other, lane, pick, down, *after):
    rows, top = pick.shape
    slots, features, _ = down.shape
    fb = feature_block(features)
    return pl.pallas_call(
        back_body,
        grid=(features // fb,),
        out_shape=[
            jax.ShapeDtypeStruct((rows, features), BF16),
            jax.ShapeDtypeStruct((rows, slots * top), BF16),
        ],
        in_specs=[WHOLE] * 4
        + [pl.BlockSpec((slots, fb, top), lambda f: (0, f, 0))]
        + [ANY] * len(after),
        out_specs=[
            pl.BlockSpec((rows, fb), lambda f: (0, f)),
            pl.BlockSpec((rows, slots * top), lambda f: (0, 0)),
        ],
        compiler_params=params(),
        cost_estimate=SMALL,
    )(mine, other, lane, pick, down, *after)


def grads_body(
    slots,
    mine_ref,
    other_ref,
    lane_ref,
    pick_ref,
    low_ref,
    acts_ref,
    masked_ref,
    down_ref,
    up_ref,
    largest_ref,
    lift_ref,
):
    top = lane_ref.shape[1]

    @pl.when(pl.program_id(0) == 0)
    def _():
        lifted = ((mine_ref[...] + other_ref[...]) * lane_ref[...]).astype(BF16).astype(F32)
        for e in range(slots):
            part = jnp.where(pick_ref[...] == float(e), lifted, 0.0)
            lift_ref[e * top : (e + 1) * top, :] = part.T.astype(BF16)
        largest_ref[...] = jnp.zeros_like(largest_ref)

    up = jnp.dot(lift_ref[...], masked_ref[...], preferred_element_type=F32)
    down = lax.dot_general(
        acts_ref[...], low_ref[...], (((0,), (0,)), ((), ())), preferred_element_type=F32
    )
    for e in range(slots):
        up_ref[e] = up[e * top : (e + 1) * top]
        down_ref[e] = down[:, e * top : (e + 1) * top]
    top_up = jnp.max(jnp.abs(up).reshape(slots * top // 8, 8, up.shape[1]), axis=0)
    top_down = jnp.max(jnp.abs(down).reshape(down.shape[0] // 8, 8, slots * top), axis=0)
    largest = largest_ref[...]
    for c in range(up.shape[1] // top):
        largest = jnp.maximum(largest, top_up[:, c * top : (c + 1) * top])
    for e in range(slots):
        largest = jnp.maximum(largest, top_down[:, e * top : (e + 1) * top])
    largest_ref[...] = largest


def grads(mine, other, lane, pick, low, acts, masked, slots):
    rows, top = pick.shape
    features = acts.shape[1]
    fb = feature_block(features)
    return pl.pallas_call(
        functools.partial(grads_body, slots),
        grid=(features // fb,),
        out_shape=[
            jax.ShapeDtypeStruct((slots, features, top), F32),
            jax.ShapeDtypeStruct((slots, top, features), F32),
            jax.ShapeDtypeStruct((8, top), F32),
        ],
        in_specs=[WHOLE] * 5 + [pl.BlockSpec((rows, fb), lambda f: (0, f))] * 2,
        out_specs=[
            pl.BlockSpec((slots, fb, top), lambda f: (0, f, 0)),
            pl.BlockSpec((slots, top, fb), lambda f: (0, 0, f)),
            pl.BlockSpec((8, top), lambda f: (0, 0)),
        ],
        scratch_shapes=[pltpu.VMEM((slots * top, rows), BF16)],
        compiler_params=params(28),
        cost_estimate=SMALL,
    )(mine, other, lane, pick, low, acts, masked)


def scaled_body(largest_ref, down_ref, up_ref, down_out, up_out):
    highest = jnp.max(largest_ref[...], keepdims=True)
    factor = grad_limit / jnp.maximum(highest, grad_limit)
    for e in range(down_ref.shape[0]):
        down_out[e] = (down_ref[e] * factor).astype(BF16)
        up_out[e] = (up_ref[e] * factor).astype(BF16)


def scaled(largest, down, up):
    slots, features, top = down.shape
    down_spec = pl.BlockSpec((1, features, top), lambda e: (e, 0, 0))
    up_spec = pl.BlockSpec((1, top, features), lambda e: (e, 0, 0))
    return pl.pallas_call(
        scaled_body,
        grid=(slots,),
        out_shape=[
            jax.ShapeDtypeStruct(down.shape, BF16),
            jax.ShapeDtypeStruct(up.shape, BF16),
        ],
        in_specs=[WHOLE, down_spec, up_spec],
        out_specs=[down_spec, up_spec],
        compiler_params=params(16),
        cost_estimate=SMALL,
    )(largest, down, up)


def finish_body(hot_ref, frozen_ref, back_ref, out_ref):
    own = jnp.dot(hot_ref[...], back_ref[...], preferred_element_type=F32)
    out_ref[...] = (frozen_ref[...] + own).astype(BF16)


def finish(hot, frozen, returned):
    native, features = frozen.shape
    rows = returned.shape[0]
    fb = feature_block(features)
    return pl.pallas_call(
        finish_body,
        grid=(features // fb,),
        out_shape=jax.ShapeDtypeStruct((native, features), BF16),
        in_specs=[
            WHOLE,
            pl.BlockSpec((native, fb), lambda f: (0, f)),
            pl.BlockSpec((rows, fb), lambda f: (0, f)),
        ],
        out_specs=pl.BlockSpec((native, fb), lambda f: (0, f)),
        compiler_params=params(),
        cost_estimate=SMALL,
    )(hot, frozen, returned)


def partner(x, axis, bit):
    count = lax.axis_size(axis)
    return lax.ppermute(x, axis, [(i, i ^ bit) for i in range(count)])


def all_but_last_sum(x, axis):
    count = lax.axis_size(axis)
    bit = 1
    while bit < count:
        other = partner(x, axis, bit)
        if 2 * bit == count:
            return x, other
        x = x + other
        bit *= 2
    return x, jnp.zeros_like(x)


def gather_rows(x):
    count = lax.axis_size("tp")
    me = lax.axis_index("tp").astype(jnp.int32)
    near = jnp.stack([me, me ^ 1]), [x, partner(x, "tp", 1)]
    sources, blocks = [], []
    for step in range(2, count, 2):
        far = lax.ppermute(x, "tp", [(i, (i + step) % count) for i in range(count)])
        blocks += [far, partner(far, "tp", 1)]
        sources += [(me - step) % count, ((me ^ 1) - step) % count]
    return near, ((jnp.stack(sources), blocks) if blocks else None), blocks[::2]


def all_max(x, axis):
    count = lax.axis_size(axis)
    bit = 1
    while bit < count:
        x = jnp.maximum(x, partner(x, axis, bit))
        bit *= 2
    return x


def local(
    activations,
    cotangent,
    frozen_weight_matrix,
    adapter_down_weights,
    adapter_up_weights,
    window_adapter,
    window_live_rows,
    rank_per_adapter,
    slot_per_adapter,
):
    groups = lax.axis_size("grp")
    slots, features, top = adapter_down_weights.shape
    micro, windows, piece, _ = activations.shape

    def native(x):
        return x.transpose(0, 2, 1, 3).reshape(micro * piece * windows, features)

    def across(x):
        return lax.all_to_all(x, "grp", split_axis=0, concat_axis=0, tiled=True)

    masked_out, masked_flat, hot = route(
        native(cotangent),
        window_adapter,
        slot_per_adapter,
        rank_per_adapter,
        window_live_rows,
        groups,
        slots,
    )
    masked_sent = across(masked_out)
    acts_out, hot_back = pack(native(activations), hot)
    near, far, first_far = gather_rows(masked_flat)
    frozen = frozen_product(*near, frozen_weight_matrix, None)
    acts = across(gate(acts_out, frozen, *first_far))
    low_part, pick, lane, masked = receive(
        masked_sent, adapter_up_weights, groups, micro * WINDOWS_PER_OWNER, piece
    )
    low_mine, low_other = all_but_last_sum(low_part, "tp")
    if far:
        frozen = frozen_product(*far, frozen_weight_matrix, frozen, low_part)
    backs, low = back(low_mine, low_other, lane, pick, adapter_down_weights, frozen)
    returned = across(backs)
    lift_mine, lift_other = all_but_last_sum(
        project(acts, pick, adapter_down_weights, low), "tp"
    )
    down_sum, up_sum, largest = grads(
        lift_mine, lift_other, lane, pick, low, acts, masked, slots
    )
    largest = all_max(all_max(largest, "tp"), "grp")
    grad_down, grad_up = scaled(largest, down_sum, up_sum)
    input_grad = finish(hot_back, frozen, returned)
    return (
        input_grad.reshape(micro, piece, windows, features).transpose(0, 2, 1, 3),
        grad_down,
        grad_up,
    )


def solution(mesh):
    return jax.shard_map(
        local,
        mesh=mesh,
        in_specs=(
            P("rep", "grp", None, "tp"),
            P("rep", "grp", None, "tp"),
            P("tp", None),
            P(("rep", "grp"), "tp", None),
            P(("rep", "grp"), None, "tp"),
            P("rep", "grp"),
            P("rep", "grp"),
            P("rep"),
            P("rep"),
        ),
        out_specs=(
            P("rep", "grp", None, "tp"),
            P(("rep", "grp"), "tp", None),
            P(("rep", "grp"), None, "tp"),
        ),
        check_vma=False,
    )
```

time: 380 us -> 173 us (0.46); the launches traced: 374 us -> 172 us
  matrix products: 128 us -> 0 us
  Pallas kernels: 0 us -> 79.7 us
  local copies, waits for them, and re-layouts: 62.6 us -> 4.84 us
  blocking collectives: 46.3 us -> 0 us
  starting transfers between devices: 57.8 us -> 25.9 us
  other arithmetic: 28.9 us -> 3.19 us
  waiting for transfers between devices: 33.9 us -> 57.8 us
  between operations: 16.7 us -> 0.78 us
    dot_general x27 -> x0, matrix products: 128 us -> none  [the longest x1 23.6 us: fold_columns(): lax.dot_general(gathered, frozen_weight_matrix, (((1,), (1,)), ((), ())),...]
    pallas_call x0 -> x11, Pallas kernels: none -> 79.7 us  [the longest x2 32.7 us: frozen_product(): pl.pallas_call(functools.partial(frozen_body, parts, so_far is not None),...]
    ppermute x0 -> x11, waiting for transfers between devices: none -> 45.5 us  [the longest x10 23 us: partner(): return lax.ppermute(x, axis, [(i, i ^ bit) for i in range(count)])]
    all_to_all x13 -> x3, starting transfers between devices: 57.6 us -> 14.3 us  [across(): return lax.all_to_all(x, 'grp', split_axis=0, concat_axis=0, tiled=True)]
    pmax x1 -> x0, blocking collectives: 30.4 us -> none  [local(): highest = lax.pmax(largest, ('grp', 'tp'))]
    convert_element_type x9 -> x0, other arithmetic: 23.6 us -> none  [the longest x1 6.56 us: local(): (grad_down * factor).astype(jnp.bfloat16)]
    reshape x7 -> x0, local copies, waits for them, and re-layouts: 22.2 us -> none  [the longest x1 5.08 us: local(): frozen_weight_gradient.reshape(micro_iterations, window_count, token_row_...]
    all_to_all x13 -> x3, waiting for transfers between devices: 33.9 us -> 12.3 us  [across(): return lax.all_to_all(x, 'grp', split_axis=0, concat_axis=0, tiled=True)]
  transfers between devices with their start and end apart: 15 -> 14, of which waited for: 7 -> 10; matrix products, arithmetic and copies ran while one was open for 46% -> 2% of each run, Pallas kernels for 0% -> 40%
where the time goes in v2:
time: 173 us; the launch traced here: 172 us
  Pallas kernels  79.7 us (46%)
  waiting for transfers between devices  57.8 us (33%)
  starting transfers between devices  25.9 us (15%)
  local copies, waits for them, and re-layouts  4.84 us (3%)
  other arithmetic  3.19 us (2%)
    pallas_call x2, Pallas kernels, frozen_product(): pl.pallas_call(functools.partial(frozen_body, parts, so_far is not None),...  32.7 us
    ppermute x10, waiting for transfers between devices, partner(): return lax.ppermute(x, axis, [(i, i ^ bit) for i in range(count)])  23 us
    ppermute x1, waiting for transfers between devices, gather_rows(): far = lax.ppermute(x, 'tp', [(i, (i + step) % count) for i in range(count)])  22.6 us
    all_to_all x3, starting transfers between devices, across(): return lax.all_to_all(x, 'grp', split_axis=0, concat_axis=0, tiled=True)  14.3 us
    all_to_all x3, waiting for transfers between devices, across(): return lax.all_to_all(x, 'grp', split_axis=0, concat_axis=0, tiled=True)  12.3 us
    ppermute x10, starting transfers between devices, partner(): return lax.ppermute(x, axis, [(i, i ^ bit) for i in range(count)])  10.1 us
    pallas_call x1, Pallas kernels, grads(): pl.pallas_call(functools.partial(grads_body, slots), grid=(features // fb...  6.75 us
    pallas_call x1, Pallas kernels, receive(): pl.pallas_call(functools.partial(receive_body, groups, windows, piece), g...  6.45 us
  transfers between devices with their start and end apart: 14, of which 10 were waited for; matrix products, arithmetic and copies ran while one was open for 2% of the time, Pallas kernels for 40%

profile of v2, /device:TPU:0, one launch (start us, length us, event | category | flops | bytes accessed | tf_op | source)
XLA Modules:
  0.0 172.2 jit_solution(1040348971844422960)
XLA Ops:
  0.6 6.0 %shard_map.112 = (bf16[512,2048]{1,0:T(8,128)(2,1)}, bf16[480,2048]{1,0:T(8,128)(2,1)}, bf16[480,480]{1,0:T(8,128)(2,1)}) custom-call(s32[3,8]{1,0:T(4,128)} %adapter_in.1, s32[32]{0:T(128)} %slot_in.1, s32[32]{0:T(128)} %rank_in.1, s32[3,8]{1,0:T(4,128)} %live_in.1, bf16[480,2048]{1,0:T(8,128)(2,1)} %bitcast.24), custom_call_target="tpu_custom_call" | custom-call | flops 1000000 | bytes 100000 | tf_op jit(solution)/shard_map/pallas_call | solution.py:146
  6.6 6.3 %all-to-all-start = ((bf16[4,128,2048]{2,1,0:T(8,128)(2,1)}), bf16[4,128,2048]{2,1,0:T(8,128)(2,1)S(1)}, u32[]{:S(2)}, u32[]{:S(2)}) async-start(bf16[4,128,2048]{2,1,0:T(8,128)(2,1)} %bitcast.23), calls=%async_computation | async-start | bytes 4194304 | tf_op jit(solution)/shard_map/all_to_all | solution.py:572
  13.0 0.0 collective-permute-start.2
  13.0 1.5 collective-permute-start
  14.5 5.0 %shard_map.113 = (bf16[480,2048]{1,0:T(8,128)(2,1)}, bf16[480,480]{1,0:T(8,128)(2,1)}) custom-call(bf16[480,480]{1,0:T(8,128)(2,1)} %get-tuple-element.19.hot_ref, bf16[480,2048]{1,0:T(8,128)(2,1)} %bitcast.25), custom_call_target="tpu_custom_call" | custom-call | flops 1000000 | bytes 100000 | tf_op jit(solution)/shard_map/pallas_call | solution.py:189
  19.5 0.6 pad_add_fusion.1.source_ref
  20.1 0.0 collective-permute-done.2.rest_1_
  20.1 15.9 %shard_map.114.rest_4_.refs_1_ = f32[480,2048]{1,0:T(8,128)} custom-call(s32[2]{0:T(128)} %pad_add_fusion.1.source_ref, bf16[480,2048]{1,0:T(8,128)(2,1)} %get-tuple-element.21.rest_0_, bf16[480,2048]{1,0:T(8,128)(2,1)} %collective-permute-done.2.rest_1_, bf16[2048,8192]{1,0:T(8,128)(2,1)} %rest_3_.3, bf16[2048,8192]{1,0:T(8,128)(2,1)} %rest_3_.3), custom_call_target="tpu_custom_call" | custom-call | flops 1000000 | bytes 100000 | tf_op jit(solution)/shard_map/pallas_call | solution.py:230
  35.9 22.6 %collective-permute-done.rest_0_.refs_2_ = bf16[480,2048]{1,0:T(8,128)(2,1)} collective-permute-done((bf16[480,2048]{1,0:T(8,128)(2,1)}, bf16[480,2048]{1,0:T(8,128)(2,1)}, u32[]{:S(2)}, u32[]{:S(2)}) %collective-permute-start) | collective-permute-done | bytes 1966112 | tf_op jit(solution)/shard_map/ppermute | solution.py:538
  58.5 2.6 %all-to-all-done = bf16[4,128,2048]{2,1,0:T(8,128)(2,1)S(1)} async-done(((bf16[4,128,2048]{2,1,0:T(8,128)(2,1)}), bf16[4,128,2048]{2,1,0:T(8,128)(2,1)S(1)}, u32[]{:S(2)}, u32[]{:S(2)}) %all-to-all-start) | async-done | bytes 2097184 | tf_op jit(solution)/shard_map/all_to_all | solution.py:572
  61.2 1.3 copy-done.6
  62.5 3.6 %all-to-all-start.2 = ((bf16[4,120,2048]{2,1,0:T(8,128)(2,1)}), bf16[4,120,2048]{2,1,0:T(8,128)(2,1)S(1)}, u32[]{:S(2)}, u32[]{:S(2)}) async-start(bf16[4,120,2048]{2,1,0:T(8,128)(2,1)} %bitcast.22), calls=%async_computation.2 | async-start | bytes 3932160 | tf_op jit(solution)/shard_map/all_to_all | solution.py:572
  66.1 0.1 collective-permute-start.1
  66.2 6.5 %shard_map.115 = (f32[480,128]{1,0:T(8,128)}, f32[480,128]{1,0:T(8,128)}, f32[480,128]{1,0:T(8,128)}, bf16[480,2048]{1,0:T(8,128)(2,1)}) custom-call(bf16[512,2048]{1,0:T(8,128)(2,1)} %bitcast.21, bf16[8,128,2048]{2,1,0:T(8,128)(2,1)} %table_ref.2), custom_call_target="tpu_custom_call" | custom-call | flops 1000000 | bytes 100000 | tf_op jit(solution)/shard_map/pallas_call | solution.py:297
  72.6 0.5 collective-permute-start.3
  73.1 1.3 collective-permute-done.3
  74.4 1.0 add.17.mine_ref
  75.4 1.6 collective-permute-start.4
  77.0 0.6 pad_add_fusion.source_ref
  77.6 0.0 collective-permute-done.1.rest_1_
  77.6 16.8 %shard_map.116.rest_0_.frozen_ref = f32[480,2048]{1,0:T(8,128)} custom-call(s32[2]{0:T(128)} %pad_add_fusion.source_ref, bf16[480,2048]{1,0:T(8,128)(2,1)} %collective-permute-done.rest_0_.refs_2_, bf16[480,2048]{1,0:T(8,128)(2,1)} %collective-permute-done.1.rest_1_, bf16[2048,8192]{1,0:T(8,128)(2,1)} %rest_3_.3, bf16[2048,8192]{1,0:T(8,128)(2,1)} %rest_3_.3, ...), custom_call_target="tpu_custom_call" | custom-call | flops 1000000 | bytes 100000 | tf_op jit(solution)/shard_map/pallas_call | solution.py:230
  94.5 0.0 collective-permute-done.4.other_ref
  94.5 0.0 copy-start.8
  94.5 0.7 copy-done.8
  95.2 6.2 %shard_map.117 = (bf16[480,2048]{1,0:T(8,128)(2,1)}, bf16[480,1024]{1,0:T(8,128)(2,1)}) custom-call(f32[480,128]{1,0:T(8,128)} %copy-done.7, f32[480,128]{1,0:T(8,128)} %copy-done.8, f32[480,128]{1,0:T(8,128)} %get-tuple-element.24.lane_ref, f32[480,128]{1,0:T(8,128)} %get-tuple-element.25.pick_ref, bf16[8,2048,128]{2,1,0:T(8,128)(2,1)} %table_ref.3, ...), custom_call_target="tpu_custom_call" | custom-call | flops 1000000 | bytes 100000 | tf_op jit(solution)/shard_map/pallas_call | solution.py:381
  101.3 9.6 %all-to-all-done.2 = bf16[4,120,2048]{2,1,0:T(8,128)(2,1)S(1)} async-done(((bf16[4,120,2048]{2,1,0:T(8,128)(2,1)}), bf16[4,120,2048]{2,1,0:T(8,128)(2,1)S(1)}, u32[]{:S(2)}, u32[]{:S(2)}) %all-to-all-start.2) | async-done | bytes 1966112 | tf_op jit(solution)/shard_map/all_to_all | solution.py:572
  111.0 1.3 copy-done
  112.2 4.4 %all-to-all-start.1 = ((bf16[4,120,2048]{2,1,0:T(8,128)(2,1)}), bf16[4,120,2048]{2,1,0:T(8,128)(2,1)}, u32[]{:S(2)}, u32[]{:S(2)}) async-start(bf16[4,120,2048]{2,1,0:T(8,128)(2,1)} %bitcast.26), calls=%async_computation.1 | async-start | bytes 3932160 | tf_op jit(solution)/shard_map/all_to_all | solution.py:572
  116.6 0.0 copy-start.1
  116.7 0.0 copy-start.2
  116.7 6.2 %shard_map.120 = f32[480,128]{1,0:T(8,128)} custom-call(f32[480,128]{1,0:T(8,128)} %get-tuple-element.25.pick_ref, bf16[480,2048]{1,0:T(8,128)(2,1)} %bitcast.19, bf16[8,2048,128]{2,1,0:T(8,128)(2,1)} %table_ref.3, bf16[480,1024]{1,0:T(8,128)(2,1)} %get-tuple-element.28.rest_0_.low_ref), custom_call_target="tpu_custom_call" | custom-call | flops 1000000 | bytes 100000 | tf_op jit(solution)/shard_map/pallas_call | solution.py:340
  122.9 1.7 collective-permute-done.5
  124.6 1.0 add.18.mine_ref
  125.6 1.6 collective-permute-start.6
  127.1 6.5 %collective-permute-done.6.other_ref = f32[480,128]{1,0:T(8,128)S(1)} collective-permute-done((f32[480,128]{1,0:T(8,128)S(1)}, f32[480,128]{1,0:T(8,128)S(1)}, u32[]{:S(2)}, u32[]{:S(2)}) %collective-permute-start.6) | collective-permute-done | bytes 245792 | tf_op jit(solution)/shard_map/ppermute | solution.py:517
  133.6 0.0 copy-start.4
  133.6 1.5 copy-done.4
  135.2 6.7 %shard_map.121 = (f32[8,2048,128]{2,1,0:T(8,128)S(1)}, f32[8,128,2048]{2,1,0:T(8,128)S(1)}, f32[8,128]{1,0:T(8,128)S(1)}) custom-call(f32[480,128]{1,0:T(8,128)S(1)} %add.18.mine_ref, f32[480,128]{1,0:T(8,128)S(1)} %collective-permute-done.6.other_ref, f32[480,128]{1,0:T(8,128)S(1)} %copy-done.5, f32[480,128]{1,0:T(8,128)S(1)} %copy-done.3, ...), custom_call_target="tpu_custom_call" | custom-call | flops 1000000 | bytes 100000 | tf_op jit(solution)/shard_map/pallas_call | solution.py:445
  141.9 0.1 collective-permute-start.7
  142.0 1.2 collective-permute-done.7
  143.2 1.5 collective-permute-start.8
  144.7 2.1 %collective-permute-done.8 = f32[8,128]{1,0:T(8,128)S(1)} collective-permute-done((f32[8,128]{1,0:T(8,128)S(1)}, f32[8,128]{1,0:T(8,128)S(1)}, u32[]{:S(2)}, u32[]{:S(2)}) %collective-permute-start.8) | collective-permute-done | bytes 4128 | tf_op jit(solution)/shard_map/ppermute | solution.py:517
  146.8 1.9 %collective-permute-start.9 = (f32[8,128]{1,0:T(8,128)S(1)}, f32[8,128]{1,0:T(8,128)S(1)}, u32[]{:S(2)}, u32[]{:S(2)}) collective-permute-start(f32[8,128]{1,0:T(8,128)S(1)} %max.13), channel_id=1, source_target_pairs={{0,4},{4,0},{8,12},{12,8},{1,5},{5,1},{9,13},{13,9},{2,6},{6,2},{1... | collective-permute-start | bytes 12296 | tf_op jit(solution)/shard_map/ppermute | solution.py:517
  148.7 1.7 collective-permute-done.9
  150.4 2.8 %collective-permute-start.10 = (f32[8,128]{1,0:T(8,128)S(1)}, f32[8,128]{1,0:T(8,128)S(1)}, u32[]{:S(2)}, u32[]{:S(2)}) collective-permute-start(f32[8,128]{1,0:T(8,128)S(1)} %max.14), channel_id=1, source_target_pairs={{0,8},{4,12},{8,0},{12,4},{1,9},{5,13},{9,1},{13,5},{2,10},{6,14},... | collective-permute-start | bytes 12296 | tf_op jit(solution)/shard_map/ppermute | solution.py:517
  153.2 8.5 %collective-permute-done.10 = f32[8,128]{1,0:T(8,128)S(1)} collective-permute-done((f32[8,128]{1,0:T(8,128)S(1)}, f32[8,128]{1,0:T(8,128)S(1)}, u32[]{:S(2)}, u32[]{:S(2)}) %collective-permute-start.10) | collective-permute-done | bytes 4128 | tf_op jit(solution)/shard_map/ppermute | solution.py:517
  161.7 5.1 %shard_map.122 = (bf16[8,2048,128]{2,1,0:T(8,128)(2,1)}, bf16[8,128,2048]{2,1,0:T(8,128)(2,1)}) custom-call(f32[8,128]{1,0:T(8,128)S(1)} %max.15.largest_ref, f32[8,2048,128]{2,1,0:T(8,128)S(1)} %get-tuple-element.31.down_ref, f32[8,128,2048]{2,1,0:T(8,128)S(1)} %get-tuple-element.32.up_ref), custom_call_target="tpu_custom_call" | custom-call | flops 1000000 | bytes 100000 | tf_op jit(solution)/shard_map/pallas_call | solution.py:477
  166.8 5.4 %shard_map.118 = bf16[480,2048]{1,0:T(8,128)(2,1)} custom-call(bf16[480,480]{1,0:T(8,128)(2,1)} %get-tuple-element.20.hot_ref, f32[480,2048]{1,0:T(8,128)} %shard_map.116.rest_0_.frozen_ref, bf16[480,2048]{1,0:T(8,128)(2,1)} %bitcast.11.back_ref), custom_call_target="tpu_custom_call" | custom-call | flops 1000000 | bytes 100000 | tf_op jit(solution)/shard_map/pallas_call | solution.py:500
  (17 shorter events, 0.0 us)
Async XLA Ops:
  6.6 54.5 %all-to-all-start = ((bf16[4,128,2048]{2,1,0:T(8,128)(2,1)}), bf16[4,128,2048]{2,1,0:T(8,128)(2,1)S(1)}, u32[]{:S(2)}, u32[]{:S(2)}) async-start(bf16[4,128,2048]{2,1,0:T(8,128)(2,1)} %bitcast.23), calls=%async_computation | async-start | bytes 4194304 | tf_op jit(solution)/shard_map/all_to_all | solution.py:572
  13.0 7.1 %collective-permute-start.2 = (bf16[480,2048]{1,0:T(8,128)(2,1)}, bf16[480,2048]{1,0:T(8,128)(2,1)}, u32[]{:S(2)}, u32[]{:S(2)}) collective-permute-start(bf16[480,2048]{1,0:T(8,128)(2,1)} %get-tuple-element.21.rest_0_), channel_id=1, source_target_pairs={{0,1},{1,0},{2,3},{3,2},{4,5},{5,4},{6,7},{7,6},{8,9},{9,8},{10,11... | collective-permute-start | bytes 5898248 | tf_op jit(solution)/shard_map/ppermute | solution.py:517
  13.0 45.5 %collective-permute-start = (bf16[480,2048]{1,0:T(8,128)(2,1)}, bf16[480,2048]{1,0:T(8,128)(2,1)}, u32[]{:S(2)}, u32[]{:S(2)}) collective-permute-start(bf16[480,2048]{1,0:T(8,128)(2,1)} %get-tuple-element.21.rest_0_), channel_id=1, source_target_pairs={{0,2},{1,3},{2,0},{3,1},{4,6},{5,7},{6,4},{7,5},{8,10},{9,11},{10,... | collective-permute-start | bytes 5898248 | tf_op jit(solution)/shard_map/ppermute | solution.py:538
  61.2 1.3 copy-start.6
  62.5 48.5 %all-to-all-start.2 = ((bf16[4,120,2048]{2,1,0:T(8,128)(2,1)}), bf16[4,120,2048]{2,1,0:T(8,128)(2,1)S(1)}, u32[]{:S(2)}, u32[]{:S(2)}) async-start(bf16[4,120,2048]{2,1,0:T(8,128)(2,1)} %bitcast.22), calls=%async_computation.2 | async-start | bytes 3932160 | tf_op jit(solution)/shard_map/all_to_all | solution.py:572
  66.1 11.5 %collective-permute-start.1 = (bf16[480,2048]{1,0:T(8,128)(2,1)}, bf16[480,2048]{1,0:T(8,128)(2,1)}, u32[]{:S(2)}, u32[]{:S(2)}) collective-permute-start(bf16[480,2048]{1,0:T(8,128)(2,1)} %collective-permute-done.rest_0_.refs_2_), channel_id=1, source_target_pairs={{0,1},{1,0},{2,3},{3,2},{4,5},{5,4},{6,7},{7,6},{8,9},{9,8},{10,11... | collective-permute-start | bytes 5898248 | tf_op jit(solution)/shard_map/ppermute | solution.py:517
  72.6 1.8 %collective-permute-start.3 = (f32[480,128]{1,0:T(8,128)}, f32[480,128]{1,0:T(8,128)S(1)}, u32[]{:S(2)}, u32[]{:S(2)}) collective-permute-start(f32[480,128]{1,0:T(8,128)} %get-tuple-element.23.rest_5_), channel_id=1, source_target_pairs={{0,1},{1,0},{2,3},{3,2},{4,5},{5,4},{6,7},{7,6},{8,9},{9,8},{10,11... | collective-permute-start | bytes 737288 | tf_op jit(solution)/shard_map/ppermute | solution.py:517
  75.4 19.0 %copy-start.7 = (f32[480,128]{1,0:T(8,128)}, f32[480,128]{1,0:T(8,128)S(1)}, u32[]{:S(2)}) copy-start(f32[480,128]{1,0:T(8,128)S(1)} %add.17.mine_ref) | copy-start | bytes 737284
  75.4 19.0 %collective-permute-start.4 = (f32[480,128]{1,0:T(8,128)S(1)}, f32[480,128]{1,0:T(8,128)S(1)}, u32[]{:S(2)}, u32[]{:S(2)}) collective-permute-start(f32[480,128]{1,0:T(8,128)S(1)} %add.17.mine_ref), channel_id=1, source_target_pairs={{0,2},{1,3},{2,0},{3,1},{4,6},{5,7},{6,4},{7,5},{8,10},{9,11},{10,... | collective-permute-start | bytes 737288 | tf_op jit(solution)/shard_map/ppermute | solution.py:517
  94.5 0.7 copy-start.8
  110.9 1.3 copy-start
  112.2 54.6 %all-to-all-start.1 = ((bf16[4,120,2048]{2,1,0:T(8,128)(2,1)}), bf16[4,120,2048]{2,1,0:T(8,128)(2,1)}, u32[]{:S(2)}, u32[]{:S(2)}) async-start(bf16[4,120,2048]{2,1,0:T(8,128)(2,1)} %bitcast.26), calls=%async_computation.1 | async-start | bytes 3932160 | tf_op jit(solution)/shard_map/all_to_all | solution.py:572
  116.6 17.0 %copy-start.1 = (bf16[4,120,2048]{2,1,0:T(8,128)(2,1)S(1)}, bf16[4,120,2048]{2,1,0:T(8,128)(2,1)}, u32[]{:S(2)}) copy-start(bf16[4,120,2048]{2,1,0:T(8,128)(2,1)} %copy-done) | copy-start | bytes 5898244
  116.7 17.0 %copy-start.2 = (bf16[480,1024]{1,0:T(8,128)(2,1)S(1)}, bf16[480,1024]{1,0:T(8,128)(2,1)}, u32[]{:S(2)}) copy-start(bf16[480,1024]{1,0:T(8,128)(2,1)} %get-tuple-element.28.rest_0_.low_ref) | copy-start | bytes 2949124
  116.7 17.0 %copy-start.3 = (f32[480,128]{1,0:T(8,128)S(1)}, f32[480,128]{1,0:T(8,128)}, u32[]{:S(2)}) copy-start(f32[480,128]{1,0:T(8,128)} %get-tuple-element.25.pick_ref) | copy-start | bytes 737284
  116.7 17.0 %copy-start.5 = (f32[480,128]{1,0:T(8,128)S(1)}, f32[480,128]{1,0:T(8,128)}, u32[]{:S(2)}) copy-start(f32[480,128]{1,0:T(8,128)} %get-tuple-element.24.lane_ref) | copy-start | bytes 737284
  122.9 1.7 %collective-permute-start.5 = (f32[480,128]{1,0:T(8,128)}, f32[480,128]{1,0:T(8,128)S(1)}, u32[]{:S(2)}, u32[]{:S(2)}) collective-permute-start(f32[480,128]{1,0:T(8,128)} %shard_map.120), channel_id=1, source_target_pairs={{0,1},{1,0},{2,3},{3,2},{4,5},{5,4},{6,7},{7,6},{8,9},{9,8},{10,11... | collective-permute-start | bytes 737288 | tf_op jit(solution)/shard_map/ppermute | solution.py:517
  125.6 8.1 %collective-permute-start.6 = (f32[480,128]{1,0:T(8,128)S(1)}, f32[480,128]{1,0:T(8,128)S(1)}, u32[]{:S(2)}, u32[]{:S(2)}) collective-permute-start(f32[480,128]{1,0:T(8,128)S(1)} %add.18.mine_ref), channel_id=1, source_target_pairs={{0,2},{1,3},{2,0},{3,1},{4,6},{5,7},{6,4},{7,5},{8,10},{9,11},{10,... | collective-permute-start | bytes 737288 | tf_op jit(solution)/shard_map/ppermute | solution.py:517
  133.6 1.5 copy-start.4
  141.9 1.2 collective-permute-start.7
  143.2 3.6 %collective-permute-start.8 = (f32[8,128]{1,0:T(8,128)S(1)}, f32[8,128]{1,0:T(8,128)S(1)}, u32[]{:S(2)}, u32[]{:S(2)}) collective-permute-start(f32[8,128]{1,0:T(8,128)S(1)} %max.12), channel_id=1, source_target_pairs={{0,2},{1,3},{2,0},{3,1},{4,6},{5,7},{6,4},{7,5},{8,10},{9,11},{10,... | collective-permute-start | bytes 12296 | tf_op jit(solution)/shard_map/ppermute | solution.py:517
  146.8 3.6 %collective-permute-start.9 = (f32[8,128]{1,0:T(8,128)S(1)}, f32[8,128]{1,0:T(8,128)S(1)}, u32[]{:S(2)}, u32[]{:S(2)}) collective-permute-start(f32[8,128]{1,0:T(8,128)S(1)} %max.13), channel_id=1, source_target_pairs={{0,4},{4,0},{8,12},{12,8},{1,5},{5,1},{9,13},{13,9},{2,6},{6,2},{1... | collective-permute-start | bytes 12296 | tf_op jit(solution)/shard_map/ppermute | solution.py:517
  150.4 11.3 %collective-permute-start.10 = (f32[8,128]{1,0:T(8,128)S(1)}, f32[8,128]{1,0:T(8,128)S(1)}, u32[]{:S(2)}, u32[]{:S(2)}) collective-permute-start(f32[8,128]{1,0:T(8,128)S(1)} %max.14), channel_id=1, source_target_pairs={{0,8},{4,12},{8,0},{12,4},{1,9},{5,13},{9,1},{13,5},{2,10},{6,14},... | collective-permute-start | bytes 12296 | tf_op jit(solution)/shard_map/ppermute | solution.py:517

commit v3 on v2

--- a/solution.py
+++ b/solution.py
@@ -63,7 +63,10 @@
     rank_in,
     live_in,
     x_ref,
-    packed_ref,
+    *rest,
+):
+    out_refs = rest[:groups]
+    (
     flat_ref,
     hot_ref,
     adapter_ref,
@@ -76,7 +79,8 @@
     target_ref,
     alive_ref,
     note_ref,
-):
+    packed_ref,
+    ) = rest[groups:]
     micro, windows = adapter_ref.shape
 
     @pl.when(pl.program_id(0) == 0)
@@ -131,7 +135,11 @@
     parts = []
     for o in range(groups):
         parts += [packed[o * rows : (o + 1) * rows], note_ref[o]]
-    packed_ref[...] = jnp.concatenate(parts, axis=0).astype(BF16)
+    packed_ref[...] = jnp.concatenate(parts, axis=0)
+    for s in range(groups):
+        owner = lax.rem(lax.axis_index("grp") + s, groups)
+        first = pl.multiple_of(owner * (rows + NOTES), 8)
+        out_refs[s][...] = packed_ref[pl.ds(first, rows + NOTES), :].astype(BF16)
     flat_ref[...] = jnp.where(alive_ref[:, :1] > 0.0, x.astype(F32), 0.0).astype(BF16)
 
 
@@ -140,20 +148,20 @@
     native, features = x.shape
     piece = native // (micro * windows)
     rows = groups * micro * WINDOWS_PER_OWNER * piece
-    sent = rows + groups * NOTES
+    sent = rows // groups + NOTES
     fb = feature_block(features)
     far = pl.BlockSpec(memory_space=pltpu.MemorySpace.HBM)
     return pl.pallas_call(
         functools.partial(route_body, groups, slots, piece),
         grid=(features // fb,),
-        out_shape=[
-            jax.ShapeDtypeStruct((sent, features), BF16),
+        out_shape=[jax.ShapeDtypeStruct((sent, features), BF16)] * groups
+        + [
             jax.ShapeDtypeStruct((native, features), BF16),
             jax.ShapeDtypeStruct((rows, native), BF16),
         ],
         in_specs=[far] * 4 + [pl.BlockSpec((native, fb), lambda f: (0, f))],
-        out_specs=[
-            pl.BlockSpec((sent, fb), lambda f: (0, f)),
+        out_specs=[pl.BlockSpec((sent, fb), lambda f: (0, f))] * groups
+        + [
             pl.BlockSpec((native, fb), lambda f: (0, f)),
             pl.BlockSpec((rows, native), lambda f: (0, 0)),
         ],
@@ -168,39 +176,59 @@
             pltpu.VMEM((rows, 128), jnp.int32),
             pltpu.VMEM((native, 128), F32),
             pltpu.VMEM((groups, NOTES, fb), F32),
+            pltpu.VMEM((groups * sent, fb), F32),
         ],
         compiler_params=params(),
         cost_estimate=SMALL,
     )(adapter, slot_per_adapter, rank_per_adapter, live, x)
 
 
-def pack_body(hot_ref, x_ref, out_ref, hot_back_ref):
+def by_shift(out_refs, wide_ref, sign):
+    groups = len(out_refs)
+    rows = out_refs[0].shape[0]
+    for s in range(groups):
+        group = lax.rem(lax.axis_index("grp") + groups + sign * s, groups)
+        here = pl.ds(pl.multiple_of(group * rows, 8), rows)
+        out_refs[s][...] = wide_ref[here, :].astype(BF16)
+
+
+def by_group(wide_ref, in_refs, sign):
+    groups = len(in_refs)
+    rows = in_refs[0].shape[0]
+    for s in range(groups):
+        group = lax.rem(lax.axis_index("grp") + groups + sign * s, groups)
+        here = pl.ds(pl.multiple_of(group * rows, 8), rows)
+        wide_ref[here, :] = in_refs[s][...].astype(F32)
+    return wide_ref[...].astype(BF16)
+
+
+def pack_body(groups, hot_ref, x_ref, *rest):
+    out_refs, hot_back_ref, wide_ref = rest[-2 - groups : -2], rest[-2], rest[-1]
+
     @pl.when(pl.program_id(0) == 0)
     def _():
         hot_back_ref[...] = hot_ref[...].astype(F32).T.astype(BF16)
 
-    out_ref[...] = jnp.dot(hot_ref[...], x_ref[...], preferred_element_type=F32).astype(BF16)
-
-
-def pack(x, hot):
+    wide_ref[...] = jnp.dot(hot_ref[...], x_ref[...], preferred_element_type=F32)
+    by_shift(out_refs, wide_ref, 1)
+
+
+def pack(x, hot, groups, *after):
     native, features = x.shape
     rows = hot.shape[0]
     fb = feature_block(features)
     return pl.pallas_call(
-        pack_body,
+        functools.partial(pack_body, groups),
         grid=(features // fb,),
-        out_shape=[
-            jax.ShapeDtypeStruct((rows, features), BF16),
-            jax.ShapeDtypeStruct((native, rows), BF16),
-        ],
-        in_specs=[WHOLE, pl.BlockSpec((native, fb), lambda f: (0, f))],
-        out_specs=[
-            pl.BlockSpec((rows, fb), lambda f: (0, f)),
-            pl.BlockSpec((native, rows), lambda f: (0, 0)),
-        ],
+        out_shape=[jax.ShapeDtypeStruct((rows // groups, features), BF16)] * groups
+        + [jax.ShapeDtypeStruct((native, rows), BF16)],
+        in_specs=[WHOLE, pl.BlockSpec((native, fb), lambda f: (0, f))] + [ANY] * len(after),
+        out_specs=[pl.BlockSpec((rows // groups, fb), lambda f: (0, f))] * groups
+        + [pl.BlockSpec((native, rows), lambda f: (0, 0))],
+        scratch_shapes=[pltpu.VMEM((rows, fb), F32)],
         compiler_params=params(),
         cost_estimate=SMALL,
-    )(hot, x)
+    )(hot, x, *after)
 
 
 def frozen_body(parts, more, source_ref, *rest):
@@ -220,7 +248,7 @@
     parts = len(row_blocks)
     rows, features = row_blocks[0].shape
     inputs = weights.shape[0]
-    nb = 256 if inputs % 256 == 0 else inputs
+    nb = 512 if inputs % 512 == 0 else inputs
 
     def columns(q):
         return pl.BlockSpec((nb, features), lambda n, source: (n, source[q]))
@@ -244,113 +272,131 @@
     )(sources, *row_blocks, *([weights] * parts), *more, *after)
 
 
-def receive_body(
-    groups, windows, piece, sent_ref, table_ref, *rest
-):
-    out_ref, pick_ref, lane_ref, rows_ref, note_ref = rest[-5:]
-    top = out_ref.shape[1]
+def receive_body(groups, windows, piece, table_ref, *rest):
+    sent_refs = rest[:groups]
+    out_ref, pick_ref, lane_ref, rows_ref, wide_ref, pick_one, lane_one, total_ref = rest[-8:]
+    slots, top, _ = table_ref.shape
     count = windows * piece
-    together = table_ref.shape[0]
     step = pl.program_id(0)
+
+    def place(s):
+        source = lax.rem(lax.axis_index("grp") + groups - s, groups)
+        return pl.ds(pl.multiple_of(source * count, 8), count)
 
     @pl.when(step == 0)
     def _():
-        sent = sent_ref[...].astype(F32)
-        rows_ref[...] = jnp.concatenate(
-            [sent[g * (count + NOTES) : g * (count + NOTES) + count] for g in range(groups)], axis=0
-        ).astype(BF16)
         column = lax.broadcasted_iota(jnp.int32, (piece, top), 1).astype(F32)
-        for g in range(groups):
-            first = g * (count + NOTES) + count
-            note_ref[...] = sent[first : first + NOTES, :128]
+        for s in range(groups):
+            notes = sent_refs[s][:, :128].astype(F32)[count:]
             for at in range(windows):
-                limit = note_ref[1:2, at : at + 1]
-                first = (g * windows + at) * piece
-                lane_ref[first : first + piece, :] = jnp.where(
+                limit = notes[1:2, at : at + 1]
+                rows = slice(at * piece, (at + 1) * piece)
+                lane_one[rows, :] = jnp.where(
                     column < limit, (top // 8) / jnp.maximum(limit, 1.0), 0.0
                 )
-                pick_ref[first : first + piece, :] = jnp.broadcast_to(
-                    note_ref[0:1, at : at + 1], (piece, top)
-                )
-        out_ref[...] = jnp.zeros_like(out_ref)
-
-    table = table_ref[...].reshape(together * top, table_ref.shape[2])
-    product = lax.dot_general(
-        rows_ref[...], table, (((1,), (1,)), ((), ())), preferred_element_type=F32
-    )
-    out_ref[...] = choose(pick_ref, product, out_ref[...], step * together, together)
-
-
-def choose(pick_ref, product, chosen, first, together):
-    top = chosen.shape[1]
-    for i in range(together):
-        here = pick_ref[...] == (first + i).astype(F32)
-        chosen = jnp.where(here, product[:, i * top : (i + 1) * top], chosen)
+                pick_one[rows, :] = jnp.broadcast_to(notes[0:1, at : at + 1], (piece, top))
+            lane_ref[place(s), :] = lane_one[...]
+            pick_ref[place(s), :] = pick_one[...]
+        total_ref[...] = jnp.zeros_like(total_ref)
+
+    for s in range(groups):
+        wide_ref[place(s), :] = sent_refs[s][...].astype(F32)[:count]
+    rows = wide_ref[...].astype(BF16)
+    rows_ref[...] = rows
+    total_ref[...] += lax.dot_general(
+        rows,
+        table_ref[...].reshape(slots * top, table_ref.shape[2]),
+        (((1,), (1,)), ((), ())),
+        preferred_element_type=F32,
+    )
+
+    @pl.when(step == pl.num_programs(0) - 1)
+    def _():
+        out_ref[...] = choose(pick_ref, total_ref, slots)
+
+
+def choose(pick_ref, total_ref, slots):
+    top = pick_ref.shape[1]
+    chosen = total_ref[:, :top]
+    for e in range(1, slots):
+        chosen = jnp.where(
+            pick_ref[...] == float(e), total_ref[:, e * top : (e + 1) * top], chosen
+        )
     return chosen
 
 
-def receive(sent, table, groups, windows, piece, *after):
+def receive(sent, table, windows, piece, *after):
+    groups = len(sent)
     slots, top, features = table.shape
-    rows = groups * windows * piece
-    together = 2 if slots % 2 == 0 else 1
-    fixed = pl.BlockSpec((rows, top), lambda e: (0, 0))
+    count = windows * piece
+    rows = groups * count
+    fb = feature_block(features)
+    fixed = pl.BlockSpec((rows, top), lambda f: (0, 0))
     return pl.pallas_call(
         functools.partial(receive_body, groups, windows, piece),
-        grid=(slots // together,),
+        grid=(features // fb,),
         out_shape=[jax.ShapeDtypeStruct((rows, top), F32)] * 3
         + [jax.ShapeDtypeStruct((rows, features), BF16)],
-        in_specs=[WHOLE, pl.BlockSpec((together, top, features), lambda e: (e, 0, 0))]
+        in_specs=[pl.BlockSpec((slots, top, fb), lambda f: (0, 0, f))]
+        + [pl.BlockSpec((count + NOTES, fb), lambda f: (0, f))] * groups
         + [ANY] * len(after),
-        out_specs=[fixed] * 3 + [pl.BlockSpec((rows, features), lambda e: (0, 0))],
-        scratch_shapes=[pltpu.VMEM((NOTES, 128), F32)],
+        out_specs=[fixed] * 3 + [pl.BlockSpec((rows, fb), lambda f: (0, f))],
+        scratch_shapes=[
+            pltpu.VMEM((rows, fb), F32),
+            pltpu.VMEM((count, top), F32),
+            pltpu.VMEM((count, top), F32),
+            pltpu.VMEM((rows, slots * top), F32),
+        ],
         compiler_params=params(),
         cost_estimate=SMALL,
-    )(sent, table, *after)
-
-
-def gate_body(*refs):
-    pass
-
-
-def gate(x, *after):
-    return pl.pallas_call(
-        gate_body,
-        out_shape=jax.ShapeDtypeStruct(x.shape, x.dtype),
-        in_specs=[ANY] * (1 + len(after)),
-        out_specs=ANY,
-        input_output_aliases={0: 0},
-        cost_estimate=SMALL,
-    )(x, *after)
-
-
-def project_body(pick_ref, rows_ref, table_ref, *rest):
-    out_ref = rest[-1]
+    )(table, *sent, *after)
+
+
+def project_body(groups, pick_ref, table_ref, *rest):
+    out_ref, rows_ref, wide_ref, total_ref = rest[-4:]
+    slots = table_ref.shape[0]
     step = pl.program_id(0)
-    together = table_ref.shape[0]
-    table = jnp.concatenate([table_ref[i] for i in range(together)], axis=1)
-    product = jnp.dot(rows_ref[...], table, preferred_element_type=F32)
-    chosen = jnp.where(step == 0, jnp.zeros(out_ref.shape, F32), out_ref[...])
-    out_ref[...] = choose(pick_ref, product, chosen, step * together, together)
-
-
-def project(rows, pick, table, *after):
+
+    @pl.when(step == 0)
+    def _():
+        total_ref[...] = jnp.zeros_like(total_ref)
+
+    rows = by_group(wide_ref, rest[:groups], -1)
+    rows_ref[...] = rows
+    table = jnp.concatenate([table_ref[e] for e in range(slots)], axis=1)
+    total_ref[...] += jnp.dot(rows, table, preferred_element_type=F32)
+
+    @pl.when(step == pl.num_programs(0) - 1)
+    def _():
+        out_ref[...] = choose(pick_ref, total_ref, slots)
+
+
+def project(blocks, pick, table, *after):
     count, top = pick.shape
-    slots = table.shape[0]
-    together = 2 if slots % 2 == 0 else 1
-    return pl.pallas_call(
-        project_body,
-        grid=(slots // together,),
-        out_shape=jax.ShapeDtypeStruct((count, top), F32),
-        in_specs=[
-            WHOLE,
-            WHOLE,
-            pl.BlockSpec((together,) + table.shape[1:], lambda e: (e, 0, 0)),
-        ]
+    groups = len(blocks)
+    slots, features = table.shape[:2]
+    fb = feature_block(features)
+    return pl.pallas_call(
+        functools.partial(project_body, groups),
+        grid=(features // fb,),
+        out_shape=[
+            jax.ShapeDtypeStruct((count, top), F32),
+            jax.ShapeDtypeStruct((count, features), BF16),
+        ],
+        in_specs=[WHOLE, pl.BlockSpec((slots, fb, top), lambda f: (0, f, 0))]
+        + [pl.BlockSpec((count // groups, fb), lambda f: (0, f))] * groups
         + [ANY] * len(after),
-        out_specs=pl.BlockSpec((count, top), lambda e: (0, 0)),
+        out_specs=[
+            pl.BlockSpec((count, top), lambda f: (0, 0)),
+            pl.BlockSpec((count, fb), lambda f: (0, f)),
+        ],
+        scratch_shapes=[
+            pltpu.VMEM((count, fb), F32),
+            pltpu.VMEM((count, slots * top), F32),
+        ],
         compiler_params=params(),
         cost_estimate=SMALL,
-    )(pick, rows, table, *after)
+    )(pick, table, *blocks, *after)
 
 
 def spread(values, pick, slots):
@@ -359,8 +405,8 @@
     ).astype(BF16)
 
 
-def back_body(mine_ref, other_ref, lane_ref, pick_ref, down_ref, *rest):
-    out_ref, spread_ref = rest[-2:]
+def back_body(groups, mine_ref, other_ref, lane_ref, pick_ref, down_ref, *rest):
+    out_refs, spread_ref, wide_ref = rest[-2 - groups : -2], rest[-2], rest[-1]
     slots, width, top = down_ref.shape
 
     @pl.when(pl.program_id(0) == 0)
@@ -369,29 +415,28 @@
         spread_ref[...] = spread(lowered, pick_ref[...], slots)
 
     table = jnp.concatenate([down_ref[e] for e in range(slots)], axis=1)
-    out_ref[...] = lax.dot_general(
+    wide_ref[...] = lax.dot_general(
         spread_ref[...], table, (((1,), (1,)), ((), ())), preferred_element_type=F32
-    ).astype(BF16)
-
-
-def back(mine, other, lane, pick, down, *after):
+    )
+    by_shift(out_refs, wide_ref, -1)
+
+
+def back(mine, other, lane, pick, down, groups, *after):
     rows, top = pick.shape
     slots, features, _ = down.shape
     fb = feature_block(features)
-    return pl.pallas_call(
-        back_body,
+    each = rows // groups
+    return pl.pallas_call(
+        functools.partial(back_body, groups),
         grid=(features // fb,),
-        out_shape=[
-            jax.ShapeDtypeStruct((rows, features), BF16),
-            jax.ShapeDtypeStruct((rows, slots * top), BF16),
-        ],
+        out_shape=[jax.ShapeDtypeStruct((each, features), BF16)] * groups
+        + [jax.ShapeDtypeStruct((rows, slots * top), BF16)],
         in_specs=[WHOLE] * 4
         + [pl.BlockSpec((slots, fb, top), lambda f: (0, f, 0))]
         + [ANY] * len(after),
-        out_specs=[
-            pl.BlockSpec((rows, fb), lambda f: (0, f)),
-            pl.BlockSpec((rows, slots * top), lambda f: (0, 0)),
-        ],
+        out_specs=[pl.BlockSpec((each, fb), lambda f: (0, f))] * groups
+        + [pl.BlockSpec((rows, slots * top), lambda f: (0, 0))],
+        scratch_shapes=[pltpu.VMEM((rows, fb), F32)],
         compiler_params=params(),
         cost_estimate=SMALL,
     )(mine, other, lane, pick, down, *after)
@@ -406,11 +451,9 @@
     low_ref,
     acts_ref,
     masked_ref,
-    down_ref,
-    up_ref,
-    largest_ref,
-    lift_ref,
+    *rest,
 ):
+    down_ref, up_ref, largest_ref, lift_ref = rest[-4:]
     top = lane_ref.shape[1]
 
     @pl.when(pl.program_id(0) == 0)
@@ -438,7 +481,7 @@
     largest_ref[...] = largest
 
 
-def grads(mine, other, lane, pick, low, acts, masked, slots):
+def grads(mine, other, lane, pick, low, acts, masked, slots, *after):
     rows, top = pick.shape
     features = acts.shape[1]
     fb = feature_block(features)
@@ -450,7 +493,9 @@
             jax.ShapeDtypeStruct((slots, top, features), F32),
             jax.ShapeDtypeStruct((8, top), F32),
         ],
-        in_specs=[WHOLE] * 5 + [pl.BlockSpec((rows, fb), lambda f: (0, f))] * 2,
+        in_specs=[WHOLE] * 5
+        + [pl.BlockSpec((rows, fb), lambda f: (0, f))] * 2
+        + [ANY] * len(after),
         out_specs=[
             pl.BlockSpec((slots, fb, top), lambda f: (0, f, 0)),
             pl.BlockSpec((slots, top, fb), lambda f: (0, 0, f)),
@@ -459,7 +504,7 @@
         scratch_shapes=[pltpu.VMEM((slots * top, rows), BF16)],
         compiler_params=params(28),
         cost_estimate=SMALL,
-    )(mine, other, lane, pick, low, acts, masked)
+    )(mine, other, lane, pick, low, acts, masked, *after)
 
 
 def scaled_body(largest_ref, down_ref, up_ref, down_out, up_out):
@@ -488,28 +533,30 @@
     )(largest, down, up)
 
 
-def finish_body(hot_ref, frozen_ref, back_ref, out_ref):
-    own = jnp.dot(hot_ref[...], back_ref[...], preferred_element_type=F32)
+def finish_body(groups, hot_ref, frozen_ref, *rest):
+    out_ref, wide_ref = rest[-2:]
+    own = jnp.dot(
+        hot_ref[...], by_group(wide_ref, rest[:groups], 1), preferred_element_type=F32
+    )
     out_ref[...] = (frozen_ref[...] + own).astype(BF16)
 
 
 def finish(hot, frozen, returned):
+    groups = len(returned)
     native, features = frozen.shape
-    rows = returned.shape[0]
+    each = returned[0].shape[0]
     fb = feature_block(features)
     return pl.pallas_call(
-        finish_body,
+        functools.partial(finish_body, groups),
         grid=(features // fb,),
         out_shape=jax.ShapeDtypeStruct((native, features), BF16),
-        in_specs=[
-            WHOLE,
-            pl.BlockSpec((native, fb), lambda f: (0, f)),
-            pl.BlockSpec((rows, fb), lambda f: (0, f)),
-        ],
+        in_specs=[WHOLE, pl.BlockSpec((native, fb), lambda f: (0, f))]
+        + [pl.BlockSpec((each, fb), lambda f: (0, f))] * groups,
         out_specs=pl.BlockSpec((native, fb), lambda f: (0, f)),
+        scratch_shapes=[pltpu.VMEM((groups * each, fb), F32)],
         compiler_params=params(),
         cost_estimate=SMALL,
-    )(hot, frozen, returned)
+    )(hot, frozen, *returned)
 
 
 def partner(x, axis, bit):
@@ -517,16 +564,12 @@
     return lax.ppermute(x, axis, [(i, i ^ bit) for i in range(count)])
 
 
-def all_but_last_sum(x, axis):
+def all_but_last_sum(near_first, x, axis):
     count = lax.axis_size(axis)
-    bit = 1
-    while bit < count:
-        other = partner(x, axis, bit)
-        if 2 * bit == count:
-            return x, other
-        x = x + other
-        bit *= 2
-    return x, jnp.zeros_like(x)
+    bits = [bit for bit in (1 << i for i in range(count.bit_length())) if bit < count]
+    for bit in bits[:-1] if near_first else bits[:0:-1]:
+        x = x + partner(x, axis, bit)
+    return x, partner(x, axis, bits[-1] if near_first else bits[0])
 
 
 def gather_rows(x):
@@ -536,9 +579,9 @@
     sources, blocks = [], []
     for step in range(2, count, 2):
         far = lax.ppermute(x, "tp", [(i, (i + step) % count) for i in range(count)])
-        blocks += [far, partner(far, "tp", 1)]
-        sources += [(me - step) % count, ((me ^ 1) - step) % count]
-    return near, ((jnp.stack(sources), blocks) if blocks else None), blocks[::2]
+        blocks.append(far)
+        sources.append((me - step) % count)
+    return near, ((jnp.stack(sources), blocks) if blocks else None)
 
 
 def all_max(x, axis):
@@ -568,10 +611,13 @@
     def native(x):
         return x.transpose(0, 2, 1, 3).reshape(micro * piece * windows, features)
 
-    def across(x):
-        return lax.all_to_all(x, "grp", split_axis=0, concat_axis=0, tiled=True)
-
-    masked_out, masked_flat, hot = route(
+    def across(blocks, sign):
+        return [blocks[0]] + [
+            lax.ppermute(blocks[s], "grp", [(i, (i + sign * s) % groups) for i in range(groups)])
+            for s in range(1, groups)
+        ]
+
+    *masked_out, masked_flat, hot = route(
         native(cotangent),
         window_adapter,
         slot_per_adapter,
@@ -580,27 +626,63 @@
         groups,
         slots,
     )
-    masked_sent = across(masked_out)
-    acts_out, hot_back = pack(native(activations), hot)
-    near, far, first_far = gather_rows(masked_flat)
-    frozen = frozen_product(*near, frozen_weight_matrix, None)
-    acts = across(gate(acts_out, frozen, *first_far))
+    masked_sent = across(masked_out, 1)
+    near, far = gather_rows(masked_flat)
+    frozen = frozen_product(*near, frozen_weight_matrix, None, masked_sent[1])
+    *acts_out, hot_back = pack(native(activations), hot, groups, masked_sent[3], frozen)
+    acts_sent = across(acts_out, 1)
     low_part, pick, lane, masked = receive(
-        masked_sent, adapter_up_weights, groups, micro * WINDOWS_PER_OWNER, piece
-    )
-    low_mine, low_other = all_but_last_sum(low_part, "tp")
-    if far:
-        frozen = frozen_product(*far, frozen_weight_matrix, frozen, low_part)
-    backs, low = back(low_mine, low_other, lane, pick, adapter_down_weights, frozen)
-    returned = across(backs)
-    lift_mine, lift_other = all_but_last_sum(
-        project(acts, pick, adapter_down_weights, low), "tp"
-    )
-    down_sum, up_sum, largest = grads(
-        lift_mine, lift_other, lane, pick, low, acts, masked, slots
-    )
-    largest = all_max(all_max(largest, "tp"), "grp")
-    grad_down, grad_up = scaled(largest, down_sum, up_sum)
+        masked_sent, adapter_up_weights, micro * WINDOWS_PER_OWNER, piece, frozen
+    )
+
+    def lower(near_first, low_part, pick, lane, table, far, weights, frozen):
+        low_mine, low_other = all_but_last_sum(near_first, low_part, "tp")
+        if far:
+            frozen = frozen_product(*far, weights, frozen, low_part)
+        *backs, low = back(low_mine, low_other, lane, pick, table, groups, frozen)
+        return backs, low, frozen
+
+    def lift(near_first, acts_sent, low, pick, lane, masked, table, far, weights, frozen):
+        lift_part, acts = project(acts_sent, pick, table, low)
+        lift_mine, lift_other = all_but_last_sum(near_first, lift_part, "tp")
+        if far:
+            sources, blocks = far
+            blocks = [partner(x, "tp", 1) for x in blocks]
+            frozen = frozen_product(sources ^ 1, blocks, weights, frozen, lift_part)
+        down_sum, up_sum, largest = grads(
+            lift_mine, lift_other, lane, pick, low, acts, masked, slots, frozen
+        )
+        largest = all_max(all_max(largest, "tp"), "grp")
+        return scaled(largest, down_sum, up_sum), frozen
+
+    early = window_live_rows[0, 0] <= piece
+    backs, low, frozen = lax.cond(
+        early,
+        functools.partial(lower, True),
+        functools.partial(lower, False),
+        low_part,
+        pick,
+        lane,
+        adapter_down_weights,
+        far,
+        frozen_weight_matrix,
+        frozen,
+    )
+    returned = across(backs, -1)
+    (grad_down, grad_up), frozen = lax.cond(
+        early,
+        functools.partial(lift, True),
+        functools.partial(lift, False),
+        acts_sent,
+        low,
+        pick,
+        lane,
+        masked,
+        adapter_down_weights,
+        far,
+        frozen_weight_matrix,
+        frozen,
+    )
     input_grad = finish(hot_back, frozen, returned)
     return (
         input_grad.reshape(micro, piece, windows, features).transpose(0, 2, 1, 3),

time: 173 us -> 160 us (0.925)
  waiting for transfers between devices: 57.8 us -> 23.3 us
  starting transfers between devices: 25.9 us -> 43.1 us
  Pallas kernels: 79.7 us -> 82.4 us
    ppermute x0 -> x9, starting transfers between devices: none -> 32.9 us  [across(): lax.ppermute(blocks[s], 'grp', [(i, (i + sign * s) % groups) for i in ran...]
    ppermute x1, waiting for transfers between devices: 22.6 us -> 0.01 us  [gather_rows(): far = lax.ppermute(x, 'tp', [(i, (i + step) % count) for i in range(count)])]
    all_to_all x3 -> x0, starting transfers between devices: 14.3 us -> none  [across(): return lax.all_to_all(x, 'grp', split_axis=0, concat_axis=0, tiled=True)]
    all_to_all x3 -> x0, waiting for transfers between devices: 12.3 us -> none  [across(): return lax.all_to_all(x, 'grp', split_axis=0, concat_axis=0, tiled=True)]
    ppermute x0 -> x9, waiting for transfers between devices: none -> 11.6 us  [across(): lax.ppermute(blocks[s], 'grp', [(i, (i + sign * s) % groups) for i in ran...]
    ppermute x10, waiting for transfers between devices: 23 us -> 11.8 us  [partner(): return lax.ppermute(x, axis, [(i, i ^ bit) for i in range(count)])]
    ppermute x10, starting transfers between devices: 10.1 us -> 7.69 us  [partner(): return lax.ppermute(x, axis, [(i, i ^ bit) for i in range(count)])]
    unnamed x18 -> x6, local copies, waits for them, and re-layouts: 4.84 us -> 2.7 us
  transfers between devices with their start and end apart: 14 -> 20, of which waited for: 10 -> 7; matrix products, arithmetic and copies ran while one was open for 2% -> 3% of each run, Pallas kernels for 40% -> 44%
where the time goes in v3:
time: 160 us; the launch traced here: 159 us
  Pallas kernels  82.4 us (52%)
  starting transfers between devices  43.1 us (27%)
  waiting for transfers between devices  23.3 us (15%)
  local copies, waits for them, and re-layouts  5.25 us (3%)
  other arithmetic  3.33 us (2%)
    ppermute x9, starting transfers between devices, across(): lax.ppermute(blocks[s], 'grp', [(i, (i + sign * s) % groups) for i in ran...  32.9 us
    pallas_call x3, Pallas kernels, frozen_product(): pl.pallas_call(functools.partial(frozen_body, parts, so_far is not None),...  32.2 us
    ppermute x10, waiting for transfers between devices, partner(): return lax.ppermute(x, axis, [(i, i ^ bit) for i in range(count)])  11.8 us
    ppermute x9, waiting for transfers between devices, across(): lax.ppermute(blocks[s], 'grp', [(i, (i + sign * s) % groups) for i in ran...  11.6 us
    ppermute x10, starting transfers between devices, partner(): return lax.ppermute(x, axis, [(i, i ^ bit) for i in range(count)])  7.69 us
    pallas_call x1, Pallas kernels, grads(): pl.pallas_call(functools.partial(grads_body, slots), grid=(features // fb...  7.61 us
    pallas_call x1, Pallas kernels, receive(): pl.pallas_call(functools.partial(receive_body, groups, windows, piece), g...  6.96 us
    pallas_call x1, Pallas kernels, project(): pl.pallas_call(functools.partial(project_body, groups), grid=(features //...  6.68 us
  transfers between devices with their start and end apart: 20, of which 7 were waited for; matrix products, arithmetic and copies ran while one was open for 3% of the time, Pallas kernels for 44%

profile of v3, /device:TPU:0, one launch (start us, length us, event | category | flops | bytes accessed | tf_op | source)
XLA Modules:
  0.0 159.0 jit_solution(9400074652568102636)
XLA Ops:
  0.6 6.2 %shard_map.112 = (bf16[128,2048]{1,0:T(8,128)(2,1)}, bf16[128,2048]{1,0:T(8,128)(2,1)}, bf16[128,2048]{1,0:T(8,128)(2,1)}, bf16[128,2048]{1,0:T(8,128)(2,1)}, bf...) custom-call(s32[3,8]{1,0:T(4,128)} %adapter_in.1, s32[32]{0:T(128)} %slot_in.1, s32[32]{0:T(128)} %rank_in.1, ...), custom_call_target="tpu_custom_call" | custom-call | flops 1000000 | bytes 100000 | tf_op jit(solution)/shard_map/pallas_call | solution.py:154
  6.9 0.5 collective-permute-start.19
  7.4 2.6 %collective-permute-start.25 = (bf16[480,2048]{1,0:T(8,128)(2,1)}, bf16[480,2048]{1,0:T(8,128)(2,1)}, u32[]{:S(2)}, u32[]{:S(2)}) collective-permute-start(bf16[480,2048]{1,0:T(8,128)(2,1)} %get-tuple-element.179.rest_0_), channel_id=1, source_target_pairs={{0,2},{1,3},{2,0},{3,1},{4,6},{5,7},{6,4},{7,5},{8,10},{9,11},{10,... | collective-permute-start | bytes 5898248 | tf_op jit(solution)/shard_map/ppermute | solution.py:581
  9.9 1.6 collective-permute-start.20
  11.5 2.2 %collective-permute-start.18 = (bf16[128,2048]{1,0:T(8,128)(2,1)}, bf16[128,2048]{1,0:T(8,128)(2,1)}, u32[]{:S(2)}, u32[]{:S(2)}) collective-permute-start(bf16[128,2048]{1,0:T(8,128)(2,1)} %get-tuple-element.178), channel_id=1, source_target_pairs={{0,12},{4,0},{8,4},{12,8},{1,13},{5,1},{9,5},{13,9},{2,14},{6,2},{... | collective-permute-start | bytes 1572872 | tf_op jit(solution)/shard_map/ppermute | solution.py:616
  13.8 0.8 collective-permute-start.21
  14.6 0.7 pad_add_fusion.source_ref
  15.2 11.5 %collective-permute-done.20.rest_4_.rest_1_ = bf16[128,2048]{1,0:T(8,128)(2,1)S(1)} collective-permute-done((bf16[128,2048]{1,0:T(8,128)(2,1)}, bf16[128,2048]{1,0:T(8,128)(2,1)S(1)}, u32[]{:S(2)}, u32[]{:S(2)}) %collective-permute-start.20) | collective-permute-done | bytes 524320 | tf_op jit(solution)/shard_map/ppermute | solution.py:616
  26.8 0.8 copy-done.12
  27.5 13.3 %shard_map.113.rest_1_.rest_4_ = f32[480,2048]{1,0:T(8,128)S(1)} custom-call(s32[2]{0:T(128)} %pad_add_fusion.source_ref, bf16[480,2048]{1,0:T(8,128)(2,1)} %get-tuple-element.179.rest_0_, bf16[480,2048]{1,0:T(8,128)(2,1)} %collective-permute-done.19.rest_1_, bf16[2048,8192]{1,0:T(8,128)(2,1)} %rest_3_.1, bf16[2048,8192]{1,0:T(8,128)(2,1)} %rest_3_.1, ...), custom_call_target="tpu_custom_call" | custom-call | flops 1000000 | bytes 100000 | tf_op jit(solution)/shard_map/pallas_call | solution.py:258
  40.9 0.0 copy-start.2
  40.9 1.9 %copy-done.2 = f32[480,2048]{1,0:T(8,128)} copy-done((f32[480,2048]{1,0:T(8,128)}, f32[480,2048]{1,0:T(8,128)S(1)}, u32[]{:S(2)}) %copy-start.2) | copy-done | bytes 3932184
  42.8 5.1 %shard_map.114 = (bf16[120,2048]{1,0:T(8,128)(2,1)}, bf16[120,2048]{1,0:T(8,128)(2,1)}, bf16[120,2048]{1,0:T(8,128)(2,1)}, bf16[120,2048]{1,0:T(8,128)(2,1)}, bf16[480,480]{1,0:T(8,128)(2,1)}) custom-call(bf16[480,480]{1,0:T(8,128)(2,1)} %get-tuple-element.177.hot_ref, bf16[480,2048]{1,0:T(8,128)(2,1)} %bitcast.14, ...), custom_call_target="tpu_custom_call" | custom-call | flops 1000000 | bytes 100000 | tf_op jit(solution)/shard_map/pallas_call | solution.py:220
  47.9 21.3 %collective-permute-start.22 = (bf16[120,2048]{1,0:T(8,128)(2,1)}, bf16[120,2048]{1,0:T(8,128)(2,1)}, u32[]{:S(2)}, u32[]{:S(2)}) collective-permute-start(bf16[120,2048]{1,0:T(8,128)(2,1)} %get-tuple-element.186), channel_id=1, source_target_pairs={{0,4},{4,8},{8,12},{12,0},{1,5},{5,9},{9,13},{13,1},{2,6},{6,10},{... | collective-permute-start | bytes 1474568 | tf_op jit(solution)/shard_map/ppermute | solution.py:616
  69.2 1.3 slice.3
  71.1 2.0 %collective-permute-start.23 = (bf16[120,2048]{1,0:T(8,128)(2,1)}, bf16[120,2048]{1,0:T(8,128)(2,1)}, u32[]{:S(2)}, u32[]{:S(2)}) collective-permute-start(bf16[120,2048]{1,0:T(8,128)(2,1)} %get-tuple-element.187), channel_id=1, source_target_pairs={{0,8},{4,12},{8,0},{12,4},{1,9},{5,13},{9,1},{13,5},{2,10},{6,14},... | collective-permute-start | bytes 1474568 | tf_op jit(solution)/shard_map/ppermute | solution.py:616
  73.2 2.9 %collective-permute-start.24 = (bf16[120,2048]{1,0:T(8,128)(2,1)}, bf16[120,2048]{1,0:T(8,128)(2,1)}, u32[]{:S(2)}, u32[]{:S(2)}) collective-permute-start(bf16[120,2048]{1,0:T(8,128)(2,1)} %get-tuple-element.188), channel_id=1, source_target_pairs={{0,12},{4,0},{8,4},{12,8},{1,13},{5,1},{9,5},{13,9},{2,14},{6,2},{... | collective-permute-start | bytes 1474568 | tf_op jit(solution)/shard_map/ppermute | solution.py:616
  76.1 7.0 %shard_map.115 = (f32[480,128]{1,0:T(8,128)}, f32[480,128]{1,0:T(8,128)}, f32[480,128]{1,0:T(8,128)}, bf16[480,2048]{1,0:T(8,128)(2,1)}) custom-call(bf16[8,128,2048]{2,1,0:T(8,128)(2,1)} %table_ref.1, bf16[128,2048]{1,0:T(8,128)(2,1)} %get-tuple-element.182.rest_0_, bf16[128,2048]{1,0:T(8,128)(2,1)} %copy-done.12, ...), custom_call_target="tpu_custom_call" | custom-call | flops 1000000 | bytes 100000 | tf_op jit(solution)/shard_map/pallas_call | solution.py:335
  83.1 19.5 %conditional.2 = (bf16[120,2048]{1,0:T(8,128)(2,1)}, bf16[120,2048]{1,0:T(8,128)(2,1)}, bf16[120,2048]{1,0:T(8,128)(2,1)}, bf16[120,2048]{1,0:T(8,128)(2,1)}, bf...) conditional(s32[]{:T(128)} %bitcast.6, (f32[480,128]{1,0:T(8,128)}, s32[1]{0:T(128)}, ...), branch_computations={%region_0.1_spmd, %region_1.2_spmd} | conditional | flops 2061440 | bytes 2903488 | solution.py:659
  83.1 0.1 collective-permute-start.2
  83.2 1.7 %collective-permute-done.2 = f32[480,128]{1,0:T(8,128)S(1)} collective-permute-done((f32[480,128]{1,0:T(8,128)}, f32[480,128]{1,0:T(8,128)S(1)}, u32[]{:S(2)}, u32[]{:S(2)}) %collective-permute-start.2) | collective-permute-done | bytes 245792 | tf_op jit(solution)/shard_map/cond/branch_1_fun/ppermute | solution.py:564
  84.9 1.7 %add.13.mine_ref = f32[480,128]{1,0:T(8,128)} add(f32[480,128]{1,0:T(8,128)} %get-tuple-element.97.rest_3_, f32[480,128]{1,0:T(8,128)S(1)} %collective-permute-done.2) | non-fusion elementwise | flops 61440 | bytes 737280 | tf_op jit(solution)/shard_map/cond/branch_1_fun/add | solution.py:571
  86.5 0.5 collective-permute-start.3
  87.1 9.0 %branch_1_fun.6.rest_0_ = f32[480,2048]{1,0:T(8,128)} custom-call(s32[1]{0:T(128)} %get-tuple-element.101.source_ref, bf16[480,2048]{1,0:T(8,128)(2,1)} %get-tuple-element.102.rest_0_, bf16[2048,8192]{1,0:T(8,128)(2,1)} %get-tuple-element.103.rest_1_, f32[480,2048]{1,0:T(8,128)S(1)} %get-tuple-element.104.rest_2_, f32[480,128]{1,0:T(8,128)} %get-tuple-element.97.rest_3_), custom_call_target="tpu_custom_call" | custom-call | flops 1000000 | bytes 100000 | tf_op jit(solution)/shard_map/cond/branch_1_fun/pallas_call | solution.py:258
  96.1 6.5 %branch_1_fun.7 = (bf16[120,2048]{1,0:T(8,128)(2,1)}, bf16[120,2048]{1,0:T(8,128)(2,1)}, bf16[120,2048]{1,0:T(8,128)(2,1)}, bf16[120,2048]{1,0:T(8,128)(2,1)}, bf16[480,1024]{1,0:T(8,128)(2,1)S(1)}) custom-call(f32[480,128]{1,0:T(8,128)} %add.13.mine_ref, f32[480,128]{1,0:T(8,128)} %collective-permute-done.3.other_ref, ...), custom_call_target="tpu_custom_call" | custom-call | flops 1000000 | bytes 100000 | tf_op jit(solution)/shard_map/cond/branch_1_fun/pallas_call | solution.py:429
  102.6 0.0 collective-permute-start.26
  102.6 0.5 collective-permute-start.27
  103.2 1.5 collective-permute-start.28
  104.6 48.2 %conditional.3 = (bf16[8,2048,128]{2,1,0:T(8,128)(2,1)}, bf16[8,128,2048]{2,1,0:T(8,128)(2,1)}, f32[480,2048]{1,0:T(8,128)}) conditional(s32[]{:T(128)} %bitcast.6, (f32[480,128]{1,0:T(8,128)}, bf16[8,2048,128]{2,1,0:T(8,128)(2,1)}, bf16[120,2048]{1,0:T(8,128)(2,1)}, bf16[120,2048]{1,0:T(8,128)(2,1)}, bf16[120,2048]{1,0:T(8,128)(2,1)}, ...), branch_computations={%region_2.3_spmd, %region_3.4_spmd} | conditional | flops 4065537 | bytes 36641892 | solution.py:672
  104.7 0.1 collective-permute-start.13
  104.7 6.7 %branch_1_fun.8 = (f32[480,128]{1,0:T(8,128)}, bf16[480,2048]{1,0:T(8,128)(2,1)}) custom-call(f32[480,128]{1,0:T(8,128)} %get-tuple-element.130.pick_ref, bf16[8,2048,128]{2,1,0:T(8,128)(2,1)} %get-tuple-element.131.table_ref, bf16[120,2048]{1,0:T(8,128)(2,1)} %get-tuple-element.132.rest_0_, bf16[120,2048]{1,0:T(8,128)(2,1)} %get-tuple-element.133.rest_1_, ...), custom_call_target="tpu_custom_call" | custom-call | flops 1000000 | bytes 100000 | tf_op jit(solution)/shard_map/cond/branch_1_fun/pallas_call | solution.py:379
  111.4 0.2 collective-permute-start.11
  111.6 1.5 collective-permute-done.11
  113.1 1.0 add.15.mine_ref
  114.1 1.5 collective-permute-start.12
  115.7 1.3 copy-done.14
  116.9 9.9 %branch_1_fun.9.rest_0_ = f32[480,2048]{1,0:T(8,128)} custom-call(s32[1]{0:T(128)S(6)} %xor.7.source_ref, bf16[480,2048]{1,0:T(8,128)(2,1)} %copy-done.14, bf16[2048,8192]{1,0:T(8,128)(2,1)} %get-tuple-element.143.rest_1_, f32[480,2048]{1,0:T(8,128)} %get-tuple-element.144.rest_2_, f32[480,128]{1,0:T(8,128)} %get-tuple-element.137.rest_3_), custom_call_target="tpu_custom_call" | custom-call | flops 1000000 | bytes 100000 | tf_op jit(solution)/shard_map/cond/branch_1_fun/pallas_call | solution.py:258
  126.9 7.6 %branch_1_fun.10 = (f32[8,2048,128]{2,1,0:T(8,128)S(1)}, f32[8,128,2048]{2,1,0:T(8,128)S(1)}, f32[8,128]{1,0:T(8,128)S(1)}) custom-call(f32[480,128]{1,0:T(8,128)S(1)} %add.15.mine_ref, f32[480,128]{1,0:T(8,128)S(1)} %collective-permute-done.12.other_ref, f32[480,128]{1,0:T(8,128)S(1)} %copy-done.11, f32[480,128]{1,0:T(8,128)S(1)} %copy-done.9, ...), custom_call_target="tpu_custom_call" | custom-call | flops 1000000 | bytes 100000 | tf_op jit(solution)/shard_map/cond/branch_1_fun/pallas_call | solution.py:488
  134.5 0.1 collective-permute-start.14
  134.6 1.2 collective-permute-done.14
  135.7 0.5 collective-permute-start.15
  136.3 3.1 %collective-permute-done.15 = f32[8,128]{1,0:T(8,128)S(1)} collective-permute-done((f32[8,128]{1,0:T(8,128)S(1)}, f32[8,128]{1,0:T(8,128)S(1)}, u32[]{:S(2)}, u32[]{:S(2)}) %collective-permute-start.15) | collective-permute-done | bytes 4128 | tf_op jit(solution)/shard_map/cond/branch_1_fun/ppermute | solution.py:564
  139.3 1.5 collective-permute-start.16
  140.8 2.4 %collective-permute-done.16 = f32[8,128]{1,0:T(8,128)S(1)} collective-permute-done((f32[8,128]{1,0:T(8,128)S(1)}, f32[8,128]{1,0:T(8,128)S(1)}, u32[]{:S(2)}, u32[]{:S(2)}) %collective-permute-start.16) | collective-permute-done | bytes 4128 | tf_op jit(solution)/shard_map/cond/branch_1_fun/ppermute | solution.py:564
  143.3 2.6 %collective-permute-start.17 = (f32[8,128]{1,0:T(8,128)S(1)}, f32[8,128]{1,0:T(8,128)S(1)}, u32[]{:S(2)}, u32[]{:S(2)}) collective-permute-start(f32[8,128]{1,0:T(8,128)S(1)} %max.22), channel_id=1, source_target_pairs={{0,8},{4,12},{8,0},{12,4},{1,9},{5,13},{9,1},{13,5},{2,10},{6,14},... | collective-permute-start | bytes 12296 | tf_op jit(solution)/shard_map/cond/branch_1_fun/ppermute | solution.py:564
  145.9 1.9 %collective-permute-done.17 = f32[8,128]{1,0:T(8,128)S(1)} collective-permute-done((f32[8,128]{1,0:T(8,128)S(1)}, f32[8,128]{1,0:T(8,128)S(1)}, u32[]{:S(2)}, u32[]{:S(2)}) %collective-permute-start.17) | collective-permute-done | bytes 4128 | tf_op jit(solution)/shard_map/cond/branch_1_fun/ppermute | solution.py:564
  147.8 5.1 %branch_1_fun.11 = (bf16[8,2048,128]{2,1,0:T(8,128)(2,1)}, bf16[8,128,2048]{2,1,0:T(8,128)(2,1)}) custom-call(f32[8,128]{1,0:T(8,128)S(1)} %max.23.largest_ref, f32[8,2048,128]{2,1,0:T(8,128)S(1)} %get-tuple-element.146.down_ref, f32[8,128,2048]{2,1,0:T(8,128)S(1)} %get-tuple-element.147.up_ref), custom_call_target="tpu_custom_call" | custom-call | flops 1000000 | bytes 100000 | tf_op jit(solution)/shard_map/cond/branch_1_fun/pallas_call | solution.py:522
  152.9 6.1 %shard_map.116 = bf16[480,2048]{1,0:T(8,128)(2,1)} custom-call(bf16[480,480]{1,0:T(8,128)(2,1)} %get-tuple-element.181.hot_ref, f32[480,2048]{1,0:T(8,128)} %get-tuple-element.194.frozen_ref, bf16[120,2048]{1,0:T(8,128)(2,1)} %get-tuple-element.195.rest_0_, bf16[120,2048]{1,0:T(8,128)(2,1)} %collective-permute-done.26.rest_1_, ...), custom_call_target="tpu_custom_call" | custom-call | flops 1000000 | bytes 100000 | tf_op jit(solution)/shard_map/pallas_call | solution.py:549
  (31 shorter events, 0.1 us)
Async XLA Ops:
  6.9 20.7 %collective-permute-start.19 = (bf16[480,2048]{1,0:T(8,128)(2,1)}, bf16[480,2048]{1,0:T(8,128)(2,1)}, u32[]{:S(2)}, u32[]{:S(2)}) collective-permute-start(bf16[480,2048]{1,0:T(8,128)(2,1)} %get-tuple-element.179.rest_0_), channel_id=1, source_target_pairs={{0,1},{1,0},{2,3},{3,2},{4,5},{5,4},{6,7},{7,6},{8,9},{9,8},{10,11... | collective-permute-start | bytes 5898248 | tf_op jit(solution)/shard_map/ppermute | solution.py:564
  7.4 75.7 %collective-permute-start.25 = (bf16[480,2048]{1,0:T(8,128)(2,1)}, bf16[480,2048]{1,0:T(8,128)(2,1)}, u32[]{:S(2)}, u32[]{:S(2)}) collective-permute-start(bf16[480,2048]{1,0:T(8,128)(2,1)} %get-tuple-element.179.rest_0_), channel_id=1, source_target_pairs={{0,2},{1,3},{2,0},{3,1},{4,6},{5,7},{6,4},{7,5},{8,10},{9,11},{10,... | collective-permute-start | bytes 5898248 | tf_op jit(solution)/shard_map/ppermute | solution.py:581
  9.9 16.8 %collective-permute-start.20 = (bf16[128,2048]{1,0:T(8,128)(2,1)}, bf16[128,2048]{1,0:T(8,128)(2,1)S(1)}, u32[]{:S(2)}, u32[]{:S(2)}) collective-permute-start(bf16[128,2048]{1,0:T(8,128)(2,1)} %get-tuple-element.180), channel_id=1, source_target_pairs={{0,4},{4,8},{8,12},{12,0},{1,5},{5,9},{9,13},{13,1},{2,6},{6,10},{... | collective-permute-start | bytes 1572872 | tf_op jit(solution)/shard_map/ppermute | solution.py:616
  11.5 29.4 %collective-permute-start.18 = (bf16[128,2048]{1,0:T(8,128)(2,1)}, bf16[128,2048]{1,0:T(8,128)(2,1)}, u32[]{:S(2)}, u32[]{:S(2)}) collective-permute-start(bf16[128,2048]{1,0:T(8,128)(2,1)} %get-tuple-element.178), channel_id=1, source_target_pairs={{0,12},{4,0},{8,4},{12,8},{1,13},{5,1},{9,5},{13,9},{2,14},{6,2},{... | collective-permute-start | bytes 1572872 | tf_op jit(solution)/shard_map/ppermute | solution.py:616
  13.8 62.3 %collective-permute-start.21 = (bf16[128,2048]{1,0:T(8,128)(2,1)}, bf16[128,2048]{1,0:T(8,128)(2,1)}, u32[]{:S(2)}, u32[]{:S(2)}) collective-permute-start(bf16[128,2048]{1,0:T(8,128)(2,1)} %get-tuple-element.183), channel_id=1, source_target_pairs={{0,8},{4,12},{8,0},{12,4},{1,9},{5,13},{9,1},{13,5},{2,10},{6,14},... | collective-permute-start | bytes 1572872 | tf_op jit(solution)/shard_map/ppermute | solution.py:616
  26.8 0.8 copy-start.12
  40.9 1.9 %copy-start.2 = (f32[480,2048]{1,0:T(8,128)}, f32[480,2048]{1,0:T(8,128)S(1)}, u32[]{:S(2)}) copy-start(f32[480,2048]{1,0:T(8,128)S(1)} %shard_map.113.rest_1_.rest_4_) | copy-start | bytes 11796484
  47.9 55.2 %collective-permute-start.22 = (bf16[120,2048]{1,0:T(8,128)(2,1)}, bf16[120,2048]{1,0:T(8,128)(2,1)}, u32[]{:S(2)}, u32[]{:S(2)}) collective-permute-start(bf16[120,2048]{1,0:T(8,128)(2,1)} %get-tuple-element.186), channel_id=1, source_target_pairs={{0,4},{4,8},{8,12},{12,0},{1,5},{5,9},{9,13},{13,1},{2,6},{6,10},{... | collective-permute-start | bytes 1474568 | tf_op jit(solution)/shard_map/ppermute | solution.py:616
  71.1 33.5 %collective-permute-start.23 = (bf16[120,2048]{1,0:T(8,128)(2,1)}, bf16[120,2048]{1,0:T(8,128)(2,1)}, u32[]{:S(2)}, u32[]{:S(2)}) collective-permute-start(bf16[120,2048]{1,0:T(8,128)(2,1)} %get-tuple-element.187), channel_id=1, source_target_pairs={{0,8},{4,12},{8,0},{12,4},{1,9},{5,13},{9,1},{13,5},{2,10},{6,14},... | collective-permute-start | bytes 1474568 | tf_op jit(solution)/shard_map/ppermute | solution.py:616
  73.2 31.5 %collective-permute-start.24 = (bf16[120,2048]{1,0:T(8,128)(2,1)}, bf16[120,2048]{1,0:T(8,128)(2,1)}, u32[]{:S(2)}, u32[]{:S(2)}) collective-permute-start(bf16[120,2048]{1,0:T(8,128)(2,1)} %get-tuple-element.188), channel_id=1, source_target_pairs={{0,12},{4,0},{8,4},{12,8},{1,13},{5,1},{9,5},{13,9},{2,14},{6,2},{... | collective-permute-start | bytes 1474568 | tf_op jit(solution)/shard_map/ppermute | solution.py:616
  76.1 7.0 %copy-start.3 = (f32[480,2048]{1,0:T(8,128)S(1)}, f32[480,2048]{1,0:T(8,128)}, u32[]{:S(2)}) copy-start(f32[480,2048]{1,0:T(8,128)} %copy-done.2) | copy-start | bytes 11796484
  83.1 1.8 %collective-permute-start.2 = (f32[480,128]{1,0:T(8,128)}, f32[480,128]{1,0:T(8,128)S(1)}, u32[]{:S(2)}, u32[]{:S(2)}) collective-permute-start(f32[480,128]{1,0:T(8,128)} %get-tuple-element.97.rest_3_), channel_id=1, source_target_pairs={{0,1},{1,0},{2,3},{3,2},{4,5},{5,4},{6,7},{7,6},{8,9},{9,8},{10,11... | collective-permute-start | bytes 737288 | tf_op jit(solution)/shard_map/cond/branch_1_fun/ppermute | solution.py:564
  86.5 9.6 %collective-permute-start.3 = (f32[480,128]{1,0:T(8,128)}, f32[480,128]{1,0:T(8,128)}, u32[]{:S(2)}, u32[]{:S(2)}) collective-permute-start(f32[480,128]{1,0:T(8,128)} %add.13.mine_ref), channel_id=1, source_target_pairs={{0,2},{1,3},{2,0},{3,1},{4,6},{5,7},{6,4},{7,5},{8,10},{9,11},{10,... | collective-permute-start | bytes 737288 | tf_op jit(solution)/shard_map/cond/branch_1_fun/ppermute | solution.py:564
  102.6 50.3 %collective-permute-start.26 = (bf16[120,2048]{1,0:T(8,128)(2,1)}, bf16[120,2048]{1,0:T(8,128)(2,1)}, u32[]{:S(2)}, u32[]{:S(2)}) collective-permute-start(bf16[120,2048]{1,0:T(8,128)(2,1)} %get-tuple-element.196), channel_id=1, source_target_pairs={{0,12},{4,0},{8,4},{12,8},{1,13},{5,1},{9,5},{13,9},{2,14},{6,2},{... | collective-permute-start | bytes 1474568 | tf_op jit(solution)/shard_map/ppermute | solution.py:616
  102.6 50.3 %collective-permute-start.27 = (bf16[120,2048]{1,0:T(8,128)(2,1)}, bf16[120,2048]{1,0:T(8,128)(2,1)}, u32[]{:S(2)}, u32[]{:S(2)}) collective-permute-start(bf16[120,2048]{1,0:T(8,128)(2,1)} %get-tuple-element.197), channel_id=1, source_target_pairs={{0,8},{4,12},{8,0},{12,4},{1,9},{5,13},{9,1},{13,5},{2,10},{6,14},... | collective-permute-start | bytes 1474568 | tf_op jit(solution)/shard_map/ppermute | solution.py:616
  103.2 49.7 %collective-permute-start.28 = (bf16[120,2048]{1,0:T(8,128)(2,1)}, bf16[120,2048]{1,0:T(8,128)(2,1)}, u32[]{:S(2)}, u32[]{:S(2)}) collective-permute-start(bf16[120,2048]{1,0:T(8,128)(2,1)} %get-tuple-element.198), channel_id=1, source_target_pairs={{0,4},{4,8},{8,12},{12,0},{1,5},{5,9},{9,13},{13,1},{2,6},{6,10},{... | collective-permute-start | bytes 1474568 | tf_op jit(solution)/shard_map/ppermute | solution.py:616
  104.6 7.0 %copy-start.6 = (bf16[480,1024]{1,0:T(8,128)(2,1)}, bf16[480,1024]{1,0:T(8,128)(2,1)S(1)}, u32[]{:S(2)}) copy-start(bf16[480,1024]{1,0:T(8,128)(2,1)S(1)} %get-tuple-element.136.rest_4_.low_ref) | copy-start | bytes 2949124 | tf_op jit(solution)/shard_map/cond
  104.7 11.0 %collective-permute-start.13 = (bf16[480,2048]{1,0:T(8,128)(2,1)}, bf16[480,2048]{1,0:T(8,128)(2,1)S(1)}, u32[]{:S(2)}, u32[]{:S(2)}) collective-permute-start(bf16[480,2048]{1,0:T(8,128)(2,1)} %get-tuple-element.142), channel_id=1, source_target_pairs={{0,1},{1,0},{2,3},{3,2},{4,5},{5,4},{6,7},{7,6},{8,9},{9,8},{10,11... | collective-permute-start | bytes 5898248 | tf_op jit(solution)/shard_map/cond/branch_1_fun/ppermute | solution.py:564
  111.4 1.7 %collective-permute-start.11 = (f32[480,128]{1,0:T(8,128)}, f32[480,128]{1,0:T(8,128)S(1)}, u32[]{:S(2)}, u32[]{:S(2)}) collective-permute-start(f32[480,128]{1,0:T(8,128)} %get-tuple-element.137.rest_3_), channel_id=1, source_target_pairs={{0,1},{1,0},{2,3},{3,2},{4,5},{5,4},{6,7},{7,6},{8,9},{9,8},{10,11... | collective-permute-start | bytes 737288 | tf_op jit(solution)/shard_map/cond/branch_1_fun/ppermute | solution.py:564
  114.1 12.7 %collective-permute-start.12 = (f32[480,128]{1,0:T(8,128)S(1)}, f32[480,128]{1,0:T(8,128)S(1)}, u32[]{:S(2)}, u32[]{:S(2)}) collective-permute-start(f32[480,128]{1,0:T(8,128)S(1)} %add.15.mine_ref), channel_id=1, source_target_pairs={{0,2},{1,3},{2,0},{3,1},{4,6},{5,7},{6,4},{7,5},{8,10},{9,11},{10,... | collective-permute-start | bytes 737288 | tf_op jit(solution)/shard_map/cond/branch_1_fun/ppermute | solution.py:564
  115.7 1.3 copy-start.14
  116.9 9.9 %copy-start.1 = (bf16[480,2048]{1,0:T(8,128)(2,1)S(1)}, bf16[480,2048]{1,0:T(8,128)(2,1)}, u32[]{:S(2)}) copy-start(bf16[480,2048]{1,0:T(8,128)(2,1)} %get-tuple-element.139.acts_ref) | copy-start | bytes 5898244 | tf_op jit(solution)/shard_map/cond
  116.9 9.9 %copy-start.7 = (bf16[480,1024]{1,0:T(8,128)(2,1)S(1)}, bf16[480,1024]{1,0:T(8,128)(2,1)}, u32[]{:S(2)}) copy-start(bf16[480,1024]{1,0:T(8,128)(2,1)} %copy-done.6) | copy-start | bytes 2949124 | tf_op jit(solution)/shard_map/cond
  116.9 9.9 %copy-start.9 = (f32[480,128]{1,0:T(8,128)S(1)}, f32[480,128]{1,0:T(8,128)}, u32[]{:S(2)}) copy-start(f32[480,128]{1,0:T(8,128)} %get-tuple-element.130.pick_ref) | copy-start | bytes 737284 | tf_op jit(solution)/shard_map/cond
  116.9 9.9 %copy-start.11 = (f32[480,128]{1,0:T(8,128)S(1)}, f32[480,128]{1,0:T(8,128)}, u32[]{:S(2)}) copy-start(f32[480,128]{1,0:T(8,128)} %get-tuple-element.138.lane_ref) | copy-start | bytes 737284 | tf_op jit(solution)/shard_map/cond
  134.5 1.2 collective-permute-start.14
  135.7 3.6 %collective-permute-start.15 = (f32[8,128]{1,0:T(8,128)S(1)}, f32[8,128]{1,0:T(8,128)S(1)}, u32[]{:S(2)}, u32[]{:S(2)}) collective-permute-start(f32[8,128]{1,0:T(8,128)S(1)} %max.20), channel_id=1, source_target_pairs={{0,2},{1,3},{2,0},{3,1},{4,6},{5,7},{6,4},{7,5},{8,10},{9,11},{10,... | collective-permute-start | bytes 12296 | tf_op jit(solution)/shard_map/cond/branch_1_fun/ppermute | solution.py:564
  139.3 3.9 %collective-permute-start.16 = (f32[8,128]{1,0:T(8,128)S(1)}, f32[8,128]{1,0:T(8,128)S(1)}, u32[]{:S(2)}, u32[]{:S(2)}) collective-permute-start(f32[8,128]{1,0:T(8,128)S(1)} %max.21), channel_id=1, source_target_pairs={{0,4},{4,0},{8,12},{12,8},{1,5},{5,1},{9,13},{13,9},{2,6},{6,2},{1... | collective-permute-start | bytes 12296 | tf_op jit(solution)/shard_map/cond/branch_1_fun/ppermute | solution.py:564
  143.3 4.5 %collective-permute-start.17 = (f32[8,128]{1,0:T(8,128)S(1)}, f32[8,128]{1,0:T(8,128)S(1)}, u32[]{:S(2)}, u32[]{:S(2)}) collective-permute-start(f32[8,128]{1,0:T(8,128)S(1)} %max.22), channel_id=1, source_target_pairs={{0,8},{4,12},{8,0},{12,4},{1,9},{5,13},{9,1},{13,5},{2,10},{6,14},... | collective-permute-start | bytes 12296 | tf_op jit(solution)/shard_map/cond/branch_1_fun/ppermute | solution.py:564

commit v4 on v3

--- a/solution.py
+++ b/solution.py
@@ -267,7 +267,7 @@
             out_specs=out_spec,
         ),
         out_shape=jax.ShapeDtypeStruct((rows, inputs), F32),
-        compiler_params=params(),
+        compiler_params=params(24 if more else VMEM_LIMIT),
         cost_estimate=SMALL,
     )(sources, *row_blocks, *([weights] * parts), *more, *after)
 
@@ -347,7 +347,7 @@
             pltpu.VMEM((count, top), F32),
             pltpu.VMEM((rows, slots * top), F32),
         ],
-        compiler_params=params(),
+        compiler_params=params(24),
         cost_estimate=SMALL,
     )(table, *sent, *after)
 
@@ -394,7 +394,7 @@
             pltpu.VMEM((count, fb), F32),
             pltpu.VMEM((count, slots * top), F32),
         ],
-        compiler_params=params(),
+        compiler_params=params(24),
         cost_estimate=SMALL,
     )(pick, table, *blocks, *after)
 
@@ -437,7 +437,7 @@
         out_specs=[pl.BlockSpec((each, fb), lambda f: (0, f))] * groups
         + [pl.BlockSpec((rows, slots * top), lambda f: (0, 0))],
         scratch_shapes=[pltpu.VMEM((rows, fb), F32)],
-        compiler_params=params(),
+        compiler_params=params(24),
         cost_estimate=SMALL,
     )(mine, other, lane, pick, down, *after)
 
@@ -554,7 +554,7 @@
         + [pl.BlockSpec((each, fb), lambda f: (0, f))] * groups,
         out_specs=pl.BlockSpec((native, fb), lambda f: (0, f)),
         scratch_shapes=[pltpu.VMEM((groups * each, fb), F32)],
-        compiler_params=params(),
+        compiler_params=params(24),
         cost_estimate=SMALL,
     )(hot, frozen, *returned)
 

time: 160 us -> 155 us (0.969)
  Pallas kernels: 82.4 us -> 73.9 us
  waiting for transfers between devices: 23.3 us -> 28 us
  other arithmetic: 3.33 us -> 0.67 us
    ppermute x10, waiting for transfers between devices: 11.8 us -> 16.4 us  [partner(): return lax.ppermute(x, axis, [(i, i ^ bit) for i in range(count)])]
    add x2, other arithmetic: 2.66 us -> 0.06 us  [all_but_last_sum(): x = x + partner(x, axis, bit)]
    pallas_call x1, Pallas kernels: 6.96 us -> 4.82 us  [receive(): pl.pallas_call(functools.partial(receive_body, groups, windows, piece), g...]
    unnamed x6 -> x18, local copies, waits for them, and re-layouts: 2.7 us -> 4.82 us
    pallas_call x1, Pallas kernels: 6.46 us -> 4.56 us  [back(): pl.pallas_call(functools.partial(back_body, groups), grid=(features // fb...]
  transfers between devices with their start and end apart: 20 -> 20, of which waited for: 7 -> 7; matrix products, arithmetic and copies ran while one was open for 3% -> 1% of each run, Pallas kernels for 44% -> 41%
where the time goes in v4:
time: 155 us; the launch traced here: 154 us
  Pallas kernels  73.9 us (48%)
  starting transfers between devices  43.6 us (28%)
  waiting for transfers between devices  28 us (18%)
  local copies, waits for them, and re-layouts  6.05 us (4%)
    ppermute x9, starting transfers between devices, across(): lax.ppermute(blocks[s], 'grp', [(i, (i + sign * s) % groups) for i in ran...  32.9 us
    pallas_call x3, Pallas kernels, frozen_product(): pl.pallas_call(functools.partial(frozen_body, parts, so_far is not None),...  31.4 us
    ppermute x10, waiting for transfers between devices, partner(): return lax.ppermute(x, axis, [(i, i ^ bit) for i in range(count)])  16.4 us
    ppermute x9, waiting for transfers between devices, across(): lax.ppermute(blocks[s], 'grp', [(i, (i + sign * s) % groups) for i in ran...  11.6 us
    ppermute x10, starting transfers between devices, partner(): return lax.ppermute(x, axis, [(i, i ^ bit) for i in range(count)])  8.12 us
    pallas_call x1, Pallas kernels, grads(): pl.pallas_call(functools.partial(grads_body, slots), grid=(features // fb...  6.75 us
    pallas_call x1, Pallas kernels, route(): pl.pallas_call(functools.partial(route_body, groups, slots, piece), grid=...  6.21 us
    pallas_call x1, Pallas kernels, project(): pl.pallas_call(functools.partial(project_body, groups), grid=(features //...  5.42 us
  transfers between devices with their start and end apart: 20, of which 7 were waited for; matrix products, arithmetic and copies ran while one was open for 1% of the time, Pallas kernels for 41%

profile of v4, /device:TPU:0, one launch (start us, length us, event | category | flops | bytes accessed | tf_op | source)
XLA Modules:
  0.0 153.9 jit_solution(6802224736580215440)
XLA Ops:
  0.6 6.2 %shard_map.112 = (bf16[128,2048]{1,0:T(8,128)(2,1)}, bf16[128,2048]{1,0:T(8,128)(2,1)}, bf16[128,2048]{1,0:T(8,128)(2,1)}, bf16[128,2048]{1,0:T(8,128)(2,1)}, bf...) custom-call(s32[3,8]{1,0:T(4,128)} %adapter_in.1, s32[32]{0:T(128)} %slot_in.1, s32[32]{0:T(128)} %rank_in.1, ...), custom_call_target="tpu_custom_call" | custom-call | flops 1000000 | bytes 100000 | tf_op jit(solution)/shard_map/pallas_call | solution.py:154
  6.9 0.5 collective-permute-start.19
  7.4 2.6 %collective-permute-start.25 = (bf16[480,2048]{1,0:T(8,128)(2,1)}, bf16[480,2048]{1,0:T(8,128)(2,1)}, u32[]{:S(2)}, u32[]{:S(2)}) collective-permute-start(bf16[480,2048]{1,0:T(8,128)(2,1)} %get-tuple-element.179.rest_0_), channel_id=1, source_target_pairs={{0,2},{1,3},{2,0},{3,1},{4,6},{5,7},{6,4},{7,5},{8,10},{9,11},{10,... | collective-permute-start | bytes 5898248 | tf_op jit(solution)/shard_map/ppermute | solution.py:581
  9.9 1.6 %collective-permute-start.20 = (bf16[128,2048]{1,0:T(8,128)(2,1)}, bf16[128,2048]{1,0:T(8,128)(2,1)S(1)}, u32[]{:S(2)}, u32[]{:S(2)}) collective-permute-start(bf16[128,2048]{1,0:T(8,128)(2,1)} %get-tuple-element.180), channel_id=1, source_target_pairs={{0,4},{4,8},{8,12},{12,0},{1,5},{5,9},{9,13},{13,1},{2,6},{6,10},{... | collective-permute-start | bytes 1572872 | tf_op jit(solution)/shard_map/ppermute | solution.py:616
  11.5 2.2 %collective-permute-start.18 = (bf16[128,2048]{1,0:T(8,128)(2,1)}, bf16[128,2048]{1,0:T(8,128)(2,1)S(1)}, u32[]{:S(2)}, u32[]{:S(2)}) collective-permute-start(bf16[128,2048]{1,0:T(8,128)(2,1)} %get-tuple-element.178), channel_id=1, source_target_pairs={{0,12},{4,0},{8,4},{12,8},{1,13},{5,1},{9,5},{13,9},{2,14},{6,2},{... | collective-permute-start | bytes 1572872 | tf_op jit(solution)/shard_map/ppermute | solution.py:616
  13.8 0.8 collective-permute-start.21
  14.6 0.6 pad_add_fusion.source_ref
  15.2 11.6 %collective-permute-done.20.rest_4_.rest_1_ = bf16[128,2048]{1,0:T(8,128)(2,1)S(1)} collective-permute-done((bf16[128,2048]{1,0:T(8,128)(2,1)}, bf16[128,2048]{1,0:T(8,128)(2,1)S(1)}, u32[]{:S(2)}, u32[]{:S(2)}) %collective-permute-start.20) | collective-permute-done | bytes 524320 | tf_op jit(solution)/shard_map/ppermute | solution.py:616
  26.8 0.0 collective-permute-done.19.rest_1_
  26.8 0.8 copy-done.1
  27.5 14.4 %shard_map.113.rest_1_.rest_4_ = f32[480,2048]{1,0:T(8,128)} custom-call(s32[2]{0:T(128)} %pad_add_fusion.source_ref, bf16[480,2048]{1,0:T(8,128)(2,1)} %get-tuple-element.179.rest_0_, bf16[480,2048]{1,0:T(8,128)(2,1)} %collective-permute-done.19.rest_1_, bf16[2048,8192]{1,0:T(8,128)(2,1)} %rest_3_.1, bf16[2048,8192]{1,0:T(8,128)(2,1)} %rest_3_.1, ...), custom_call_target="tpu_custom_call" | custom-call | flops 1000000 | bytes 100000 | tf_op jit(solution)/shard_map/pallas_call | solution.py:258
  42.0 0.8 copy-done.3
  42.8 5.1 %shard_map.114 = (bf16[120,2048]{1,0:T(8,128)(2,1)}, bf16[120,2048]{1,0:T(8,128)(2,1)}, bf16[120,2048]{1,0:T(8,128)(2,1)}, bf16[120,2048]{1,0:T(8,128)(2,1)}, bf16[480,480]{1,0:T(8,128)(2,1)}) custom-call(bf16[480,480]{1,0:T(8,128)(2,1)} %get-tuple-element.177.hot_ref, bf16[480,2048]{1,0:T(8,128)(2,1)} %bitcast.14, bf16[128,2048]{1,0:T(8,128)(2,1)} %copy-done.3, ...), custom_call_target="tpu_custom_call" | custom-call | flops 1000000 | bytes 100000 | tf_op jit(solution)/shard_map/pallas_call | solution.py:220
  47.9 21.3 %collective-permute-start.22 = (bf16[120,2048]{1,0:T(8,128)(2,1)}, bf16[120,2048]{1,0:T(8,128)(2,1)}, u32[]{:S(2)}, u32[]{:S(2)}) collective-permute-start(bf16[120,2048]{1,0:T(8,128)(2,1)} %get-tuple-element.186), channel_id=1, source_target_pairs={{0,4},{4,8},{8,12},{12,0},{1,5},{5,9},{9,13},{13,1},{2,6},{6,10},{... | collective-permute-start | bytes 1474568 | tf_op jit(solution)/shard_map/ppermute | solution.py:616
  69.2 1.2 slice.3
  71.0 2.0 %collective-permute-start.23 = (bf16[120,2048]{1,0:T(8,128)(2,1)}, bf16[120,2048]{1,0:T(8,128)(2,1)}, u32[]{:S(2)}, u32[]{:S(2)}) collective-permute-start(bf16[120,2048]{1,0:T(8,128)(2,1)} %get-tuple-element.187), channel_id=1, source_target_pairs={{0,8},{4,12},{8,0},{12,4},{1,9},{5,13},{9,1},{13,5},{2,10},{6,14},... | collective-permute-start | bytes 1474568 | tf_op jit(solution)/shard_map/ppermute | solution.py:616
  73.1 2.9 %collective-permute-start.24 = (bf16[120,2048]{1,0:T(8,128)(2,1)}, bf16[120,2048]{1,0:T(8,128)(2,1)}, u32[]{:S(2)}, u32[]{:S(2)}) collective-permute-start(bf16[120,2048]{1,0:T(8,128)(2,1)} %get-tuple-element.188), channel_id=1, source_target_pairs={{0,12},{4,0},{8,4},{12,8},{1,13},{5,1},{9,5},{13,9},{2,14},{6,2},{... | collective-permute-start | bytes 1474568 | tf_op jit(solution)/shard_map/ppermute | solution.py:616
  76.0 0.0 copy-start
  76.0 2.2 %copy-done = bf16[8,128,2048]{2,1,0:T(8,128)(2,1)S(1)} copy-done((bf16[8,128,2048]{2,1,0:T(8,128)(2,1)S(1)}, bf16[8,128,2048]{2,1,0:T(8,128)(2,1)}, u32[]{:S(2)}) %copy-start) | copy-done | bytes 4194328
  78.2 1.0 copy-done.4
  79.2 4.8 %shard_map.115 = (f32[480,128]{1,0:T(8,128)S(1)}, f32[480,128]{1,0:T(8,128)S(1)}, f32[480,128]{1,0:T(8,128)S(1)}, bf16[480,2048]{1,0:T(8,128)(2,1)}) custom-call(bf16[8,128,2048]{2,1,0:T(8,128)(2,1)S(1)} %copy-done, bf16[128,2048]{1,0:T(8,128)(2,1)S(1)} %copy-done.5, bf16[128,2048]{1,0:T(8,128)(2,1)S(1)} %copy-done.2, ...), custom_call_target="tpu_custom_call" | custom-call | flops 1000000 | bytes 100000 | tf_op jit(solution)/shard_map/pallas_call | solution.py:335
  84.1 15.9 %conditional.2 = (bf16[120,2048]{1,0:T(8,128)(2,1)}, bf16[120,2048]{1,0:T(8,128)(2,1)}, bf16[120,2048]{1,0:T(8,128)(2,1)}, bf16[120,2048]{1,0:T(8,128)(2,1)}, bf...) conditional(s32[]{:T(128)} %bitcast.6, (f32[480,128]{1,0:T(8,128)S(1)}, s32[1]{0:T(128)}, ...), branch_computations={%region_0.1_spmd, %region_1.2_spmd} | conditional | flops 2061440 | bytes 2903488 | solution.py:659
  84.1 0.1 collective-permute-start.2
  84.2 1.5 collective-permute-done.2
  85.7 0.6 collective-permute-start.3
  86.3 9.1 %branch_1_fun.6.rest_0_ = f32[480,2048]{1,0:T(8,128)} custom-call(s32[1]{0:T(128)} %get-tuple-element.101.source_ref, bf16[480,2048]{1,0:T(8,128)(2,1)} %get-tuple-element.102.rest_0_, bf16[2048,8192]{1,0:T(8,128)(2,1)} %get-tuple-element.103.rest_1_, f32[480,2048]{1,0:T(8,128)S(1)} %get-tuple-element.104.rest_2_, f32[480,128]{1,0:T(8,128)S(1)} %get-tuple-element.97.rest_3_), custom_call_target="tpu_custom_call" | custom-call | flops 1000000 | bytes 100000 | tf_op jit(solution)/shard_map/cond/branch_1_fun/pallas_call | solution.py:258
  95.4 4.6 %branch_1_fun.7 = (bf16[120,2048]{1,0:T(8,128)(2,1)}, bf16[120,2048]{1,0:T(8,128)(2,1)}, bf16[120,2048]{1,0:T(8,128)(2,1)}, bf16[120,2048]{1,0:T(8,128)(2,1)}, bf16[480,1024]{1,0:T(8,128)(2,1)S(1)}) custom-call(f32[480,128]{1,0:T(8,128)S(1)} %add.13.mine_ref, f32[480,128]{1,0:T(8,128)S(1)} %collective-permute-done.3.other_ref, ...), custom_call_target="tpu_custom_call" | custom-call | flops 1000000 | bytes 100000 | tf_op jit(solution)/shard_map/cond/branch_1_fun/pallas_call | solution.py:429
  100.0 0.0 collective-permute-start.26
  100.0 0.6 collective-permute-start.27
  100.6 1.4 collective-permute-start.28
  102.0 47.3 %conditional.3 = (bf16[8,2048,128]{2,1,0:T(8,128)(2,1)}, bf16[8,128,2048]{2,1,0:T(8,128)(2,1)}, f32[480,2048]{1,0:T(8,128)S(1)}) conditional(s32[]{:T(128)} %bitcast.6, (f32[480,128]{1,0:T(8,128)S(1)}, bf16[8,2048,128]{2,1,0:T(8,128)(2,1)}, bf16[120,2048]{1,0:T(8,128)(2,1)}, bf16[120,2048]{1,0:T(8,128)(2,1)}, bf16[120,2048]{1,0:T(8,128)(2,1)}, ...), branch_computations={%region_2.3_spmd, %region_3.4_spmd} | conditional | flops 4065537 | bytes 50404368 | solution.py:672
  102.2 0.1 collective-permute-start.13
  102.3 5.4 %branch_1_fun.8 = (f32[480,128]{1,0:T(8,128)S(1)}, bf16[480,2048]{1,0:T(8,128)(2,1)S(1)}) custom-call(f32[480,128]{1,0:T(8,128)S(1)} %get-tuple-element.130.pick_ref, bf16[8,2048,128]{2,1,0:T(8,128)(2,1)} %get-tuple-element.131.table_ref, bf16[120,2048]{1,0:T(8,128)(2,1)} %get-tuple-element.132.rest_0_, bf16[120,2048]{1,0:T(8,128)(2,1)} %get-tuple-element.133.rest_1_, ...), custom_call_target="tpu_custom_call" | custom-call | flops 1000000 | bytes 100000 | tf_op jit(solution)/shard_map/cond/branch_1_fun/pallas_call | solution.py:379
  107.7 0.5 collective-permute-start.11
  108.3 1.1 collective-permute-done.11
  109.5 1.6 %collective-permute-start.12 = (f32[480,128]{1,0:T(8,128)S(1)}, f32[480,128]{1,0:T(8,128)S(1)}, u32[]{:S(2)}, u32[]{:S(2)}) collective-permute-start(f32[480,128]{1,0:T(8,128)S(1)} %add.15.mine_ref), channel_id=1, source_target_pairs={{0,2},{1,3},{2,0},{3,1},{4,6},{5,7},{6,4},{7,5},{8,10},{9,11},{10,... | collective-permute-start | bytes 737288 | tf_op jit(solution)/shard_map/cond/branch_1_fun/ppermute | solution.py:564
  111.0 7.8 %branch_1_fun.9.rest_0_ = f32[480,2048]{1,0:T(8,128)S(1)} custom-call(s32[1]{0:T(128)S(6)} %xor.7.source_ref, bf16[480,2048]{1,0:T(8,128)(2,1)S(1)} %collective-permute-done.13.rest_0_, bf16[2048,8192]{1,0:T(8,128)(2,1)} %get-tuple-element.143.rest_1_, f32[480,2048]{1,0:T(8,128)} %get-tuple-element.144.rest_2_, f32[480,128]{1,0:T(8,128)S(1)} %get-tuple-element.137.rest_3_), custom_call_target="tpu_custom_call" | custom-call | flops 1000000 | bytes 100000 | tf_op jit(solution)/shard_map/cond/branch_1_fun/pallas_call | solution.py:258
  118.9 6.8 %branch_1_fun.10 = (f32[8,2048,128]{2,1,0:T(8,128)S(1)}, f32[8,128,2048]{2,1,0:T(8,128)S(1)}, f32[8,128]{1,0:T(8,128)S(1)}) custom-call(f32[480,128]{1,0:T(8,128)S(1)} %add.15.mine_ref, f32[480,128]{1,0:T(8,128)S(1)} %collective-permute-done.12.other_ref, f32[480,128]{1,0:T(8,128)S(1)} %get-tuple-element.138.lane_ref, ...), custom_call_target="tpu_custom_call" | custom-call | flops 1000000 | bytes 100000 | tf_op jit(solution)/shard_map/cond/branch_1_fun/pallas_call | solution.py:488
  125.7 0.1 collective-permute-start.14
  125.8 1.1 collective-permute-done.14
  126.9 0.5 collective-permute-start.15
  127.4 3.1 %collective-permute-done.15 = f32[8,128]{1,0:T(8,128)S(1)} collective-permute-done((f32[8,128]{1,0:T(8,128)S(1)}, f32[8,128]{1,0:T(8,128)S(1)}, u32[]{:S(2)}, u32[]{:S(2)}) %collective-permute-start.15) | collective-permute-done | bytes 4128 | tf_op jit(solution)/shard_map/cond/branch_1_fun/ppermute | solution.py:564
  130.5 1.5 collective-permute-start.16
  132.0 2.5 %collective-permute-done.16 = f32[8,128]{1,0:T(8,128)S(1)} collective-permute-done((f32[8,128]{1,0:T(8,128)S(1)}, f32[8,128]{1,0:T(8,128)S(1)}, u32[]{:S(2)}, u32[]{:S(2)}) %collective-permute-start.16) | collective-permute-done | bytes 4128 | tf_op jit(solution)/shard_map/cond/branch_1_fun/ppermute | solution.py:564
  134.5 2.6 %collective-permute-start.17 = (f32[8,128]{1,0:T(8,128)S(1)}, f32[8,128]{1,0:T(8,128)S(1)}, u32[]{:S(2)}, u32[]{:S(2)}) collective-permute-start(f32[8,128]{1,0:T(8,128)S(1)} %max.22), channel_id=1, source_target_pairs={{0,8},{4,12},{8,0},{12,4},{1,9},{5,13},{9,1},{13,5},{2,10},{6,14},... | collective-permute-start | bytes 12296 | tf_op jit(solution)/shard_map/cond/branch_1_fun/ppermute | solution.py:564
  137.1 7.1 %collective-permute-done.17 = f32[8,128]{1,0:T(8,128)S(1)} collective-permute-done((f32[8,128]{1,0:T(8,128)S(1)}, f32[8,128]{1,0:T(8,128)S(1)}, u32[]{:S(2)}, u32[]{:S(2)}) %collective-permute-start.17) | collective-permute-done | bytes 4128 | tf_op jit(solution)/shard_map/cond/branch_1_fun/ppermute | solution.py:564
  144.2 5.1 %branch_1_fun.11 = (bf16[8,2048,128]{2,1,0:T(8,128)(2,1)}, bf16[8,128,2048]{2,1,0:T(8,128)(2,1)}) custom-call(f32[8,128]{1,0:T(8,128)S(1)} %max.23.largest_ref, f32[8,2048,128]{2,1,0:T(8,128)S(1)} %get-tuple-element.146.down_ref, f32[8,128,2048]{2,1,0:T(8,128)S(1)} %get-tuple-element.147.up_ref), custom_call_target="tpu_custom_call" | custom-call | flops 1000000 | bytes 100000 | tf_op jit(solution)/shard_map/cond/branch_1_fun/pallas_call | solution.py:522
  149.3 4.6 %shard_map.116 = bf16[480,2048]{1,0:T(8,128)(2,1)} custom-call(bf16[480,480]{1,0:T(8,128)(2,1)S(1)} %copy-done.6, f32[480,2048]{1,0:T(8,128)S(1)} %get-tuple-element.194.frozen_ref, bf16[120,2048]{1,0:T(8,128)(2,1)} %get-tuple-element.195.rest_0_, bf16[120,2048]{1,0:T(8,128)(2,1)S(1)} %collective-permute-done.26.rest_1_, ...), custom_call_target="tpu_custom_call" | custom-call | flops 1000000 | bytes 100000 | tf_op jit(solution)/shard_map/pallas_call | solution.py:549
  (37 shorter events, 0.1 us)
Async XLA Ops:
  6.9 19.9 %collective-permute-start.19 = (bf16[480,2048]{1,0:T(8,128)(2,1)}, bf16[480,2048]{1,0:T(8,128)(2,1)}, u32[]{:S(2)}, u32[]{:S(2)}) collective-permute-start(bf16[480,2048]{1,0:T(8,128)(2,1)} %get-tuple-element.179.rest_0_), channel_id=1, source_target_pairs={{0,1},{1,0},{2,3},{3,2},{4,5},{5,4},{6,7},{7,6},{8,9},{9,8},{10,11... | collective-permute-start | bytes 5898248 | tf_op jit(solution)/shard_map/ppermute | solution.py:564
  7.4 76.7 %collective-permute-start.25 = (bf16[480,2048]{1,0:T(8,128)(2,1)}, bf16[480,2048]{1,0:T(8,128)(2,1)}, u32[]{:S(2)}, u32[]{:S(2)}) collective-permute-start(bf16[480,2048]{1,0:T(8,128)(2,1)} %get-tuple-element.179.rest_0_), channel_id=1, source_target_pairs={{0,2},{1,3},{2,0},{3,1},{4,6},{5,7},{6,4},{7,5},{8,10},{9,11},{10,... | collective-permute-start | bytes 5898248 | tf_op jit(solution)/shard_map/ppermute | solution.py:581
  9.9 16.8 %collective-permute-start.20 = (bf16[128,2048]{1,0:T(8,128)(2,1)}, bf16[128,2048]{1,0:T(8,128)(2,1)S(1)}, u32[]{:S(2)}, u32[]{:S(2)}) collective-permute-start(bf16[128,2048]{1,0:T(8,128)(2,1)} %get-tuple-element.180), channel_id=1, source_target_pairs={{0,4},{4,8},{8,12},{12,0},{1,5},{5,9},{9,13},{13,1},{2,6},{6,10},{... | collective-permute-start | bytes 1572872 | tf_op jit(solution)/shard_map/ppermute | solution.py:616
  11.5 30.4 %collective-permute-start.18 = (bf16[128,2048]{1,0:T(8,128)(2,1)}, bf16[128,2048]{1,0:T(8,128)(2,1)S(1)}, u32[]{:S(2)}, u32[]{:S(2)}) collective-permute-start(bf16[128,2048]{1,0:T(8,128)(2,1)} %get-tuple-element.178), channel_id=1, source_target_pairs={{0,12},{4,0},{8,4},{12,8},{1,13},{5,1},{9,5},{13,9},{2,14},{6,2},{... | collective-permute-start | bytes 1572872 | tf_op jit(solution)/shard_map/ppermute | solution.py:616
  13.8 62.2 %collective-permute-start.21 = (bf16[128,2048]{1,0:T(8,128)(2,1)}, bf16[128,2048]{1,0:T(8,128)(2,1)S(1)}, u32[]{:S(2)}, u32[]{:S(2)}) collective-permute-start(bf16[128,2048]{1,0:T(8,128)(2,1)} %get-tuple-element.183), channel_id=1, source_target_pairs={{0,8},{4,12},{8,0},{12,4},{1,9},{5,13},{9,1},{13,5},{2,10},{6,14},... | collective-permute-start | bytes 1572872 | tf_op jit(solution)/shard_map/ppermute | solution.py:616
  26.8 0.8 copy-start.1
  42.0 34.0 %copy-start.2 = (bf16[128,2048]{1,0:T(8,128)(2,1)S(1)}, bf16[128,2048]{1,0:T(8,128)(2,1)}, u32[]{:S(2)}) copy-start(bf16[128,2048]{1,0:T(8,128)(2,1)} %copy-done.1) | copy-start | bytes 1572868
  42.0 34.0 %copy-start.5 = (bf16[128,2048]{1,0:T(8,128)(2,1)S(1)}, bf16[128,2048]{1,0:T(8,128)(2,1)}, u32[]{:S(2)}) copy-start(bf16[128,2048]{1,0:T(8,128)(2,1)} %get-tuple-element.182.rest_0_) | copy-start | bytes 1572868
  42.0 0.8 copy-start.3
  47.9 52.7 %collective-permute-start.22 = (bf16[120,2048]{1,0:T(8,128)(2,1)}, bf16[120,2048]{1,0:T(8,128)(2,1)}, u32[]{:S(2)}, u32[]{:S(2)}) collective-permute-start(bf16[120,2048]{1,0:T(8,128)(2,1)} %get-tuple-element.186), channel_id=1, source_target_pairs={{0,4},{4,8},{8,12},{12,0},{1,5},{5,9},{9,13},{13,1},{2,6},{6,10},{... | collective-permute-start | bytes 1474568 | tf_op jit(solution)/shard_map/ppermute | solution.py:616
  71.0 31.0 %collective-permute-start.23 = (bf16[120,2048]{1,0:T(8,128)(2,1)}, bf16[120,2048]{1,0:T(8,128)(2,1)}, u32[]{:S(2)}, u32[]{:S(2)}) collective-permute-start(bf16[120,2048]{1,0:T(8,128)(2,1)} %get-tuple-element.187), channel_id=1, source_target_pairs={{0,8},{4,12},{8,0},{12,4},{1,9},{5,13},{9,1},{13,5},{2,10},{6,14},... | collective-permute-start | bytes 1474568 | tf_op jit(solution)/shard_map/ppermute | solution.py:616
  73.1 28.9 %collective-permute-start.24 = (bf16[120,2048]{1,0:T(8,128)(2,1)}, bf16[120,2048]{1,0:T(8,128)(2,1)}, u32[]{:S(2)}, u32[]{:S(2)}) collective-permute-start(bf16[120,2048]{1,0:T(8,128)(2,1)} %get-tuple-element.188), channel_id=1, source_target_pairs={{0,12},{4,0},{8,4},{12,8},{1,13},{5,1},{9,5},{13,9},{2,14},{6,2},{... | collective-permute-start | bytes 1474568 | tf_op jit(solution)/shard_map/ppermute | solution.py:616
  76.0 2.2 %copy-start = (bf16[8,128,2048]{2,1,0:T(8,128)(2,1)S(1)}, bf16[8,128,2048]{2,1,0:T(8,128)(2,1)}, u32[]{:S(2)}) copy-start(bf16[8,128,2048]{2,1,0:T(8,128)(2,1)} %table_ref.1) | copy-start | bytes 12582916
  78.2 1.0 copy-start.4
  79.2 4.8 %copy-start.7 = (f32[480,2048]{1,0:T(8,128)S(1)}, f32[480,2048]{1,0:T(8,128)}, u32[]{:S(2)}) copy-start(f32[480,2048]{1,0:T(8,128)} %shard_map.113.rest_1_.rest_4_) | copy-start | bytes 11796484
  79.2 4.8 %copy-start.8 = (bf16[8,2048,128]{2,1,0:T(8,128)(2,1)S(1)}, bf16[8,2048,128]{2,1,0:T(8,128)(2,1)}, u32[]{:S(2)}) copy-start(bf16[8,2048,128]{2,1,0:T(8,128)(2,1)} %param.16) | copy-start | bytes 12582916
  84.1 1.6 %collective-permute-start.2 = (f32[480,128]{1,0:T(8,128)S(1)}, f32[480,128]{1,0:T(8,128)S(1)}, u32[]{:S(2)}, u32[]{:S(2)}) collective-permute-start(f32[480,128]{1,0:T(8,128)S(1)} %get-tuple-element.97.rest_3_), channel_id=1, source_target_pairs={{0,1},{1,0},{2,3},{3,2},{4,5},{5,4},{6,7},{7,6},{8,9},{9,8},{10,11... | collective-permute-start | bytes 737288 | tf_op jit(solution)/shard_map/cond/branch_1_fun/ppermute | solution.py:564
  85.7 9.7 %collective-permute-start.3 = (f32[480,128]{1,0:T(8,128)S(1)}, f32[480,128]{1,0:T(8,128)S(1)}, u32[]{:S(2)}, u32[]{:S(2)}) collective-permute-start(f32[480,128]{1,0:T(8,128)S(1)} %add.13.mine_ref), channel_id=1, source_target_pairs={{0,2},{1,3},{2,0},{3,1},{4,6},{5,7},{6,4},{7,5},{8,10},{9,11},{10,... | collective-permute-start | bytes 737288 | tf_op jit(solution)/shard_map/cond/branch_1_fun/ppermute | solution.py:564
  100.0 49.3 %collective-permute-start.26 = (bf16[120,2048]{1,0:T(8,128)(2,1)}, bf16[120,2048]{1,0:T(8,128)(2,1)S(1)}, u32[]{:S(2)}, u32[]{:S(2)}) collective-permute-start(bf16[120,2048]{1,0:T(8,128)(2,1)} %get-tuple-element.196), channel_id=1, source_target_pairs={{0,12},{4,0},{8,4},{12,8},{1,13},{5,1},{9,5},{13,9},{2,14},{6,2},{... | collective-permute-start | bytes 1474568 | tf_op jit(solution)/shard_map/ppermute | solution.py:616
  100.0 49.3 %collective-permute-start.27 = (bf16[120,2048]{1,0:T(8,128)(2,1)}, bf16[120,2048]{1,0:T(8,128)(2,1)S(1)}, u32[]{:S(2)}, u32[]{:S(2)}) collective-permute-start(bf16[120,2048]{1,0:T(8,128)(2,1)} %get-tuple-element.197), channel_id=1, source_target_pairs={{0,8},{4,12},{8,0},{12,4},{1,9},{5,13},{9,1},{13,5},{2,10},{6,14},... | collective-permute-start | bytes 1474568 | tf_op jit(solution)/shard_map/ppermute | solution.py:616
  100.6 48.8 %collective-permute-start.28 = (bf16[120,2048]{1,0:T(8,128)(2,1)}, bf16[120,2048]{1,0:T(8,128)(2,1)S(1)}, u32[]{:S(2)}, u32[]{:S(2)}) collective-permute-start(bf16[120,2048]{1,0:T(8,128)(2,1)} %get-tuple-element.198), channel_id=1, source_target_pairs={{0,4},{4,8},{8,12},{12,0},{1,5},{5,9},{9,13},{13,1},{2,6},{6,10},{... | collective-permute-start | bytes 1474568 | tf_op jit(solution)/shard_map/ppermute | solution.py:616
  102.0 47.3 %copy-start.6 = (bf16[480,480]{1,0:T(8,128)(2,1)S(1)}, bf16[480,480]{1,0:T(8,128)(2,1)}, u32[]{:S(2)}) copy-start(bf16[480,480]{1,0:T(8,128)(2,1)} %get-tuple-element.181.hot_ref) | copy-start | bytes 1382404
  102.2 8.8 %collective-permute-start.13 = (bf16[480,2048]{1,0:T(8,128)(2,1)}, bf16[480,2048]{1,0:T(8,128)(2,1)S(1)}, u32[]{:S(2)}, u32[]{:S(2)}) collective-permute-start(bf16[480,2048]{1,0:T(8,128)(2,1)} %get-tuple-element.142), channel_id=1, source_target_pairs={{0,1},{1,0},{2,3},{3,2},{4,5},{5,4},{6,7},{7,6},{8,9},{9,8},{10,11... | collective-permute-start | bytes 5898248 | tf_op jit(solution)/shard_map/cond/branch_1_fun/ppermute | solution.py:564
  107.7 1.7 %collective-permute-start.11 = (f32[480,128]{1,0:T(8,128)S(1)}, f32[480,128]{1,0:T(8,128)S(1)}, u32[]{:S(2)}, u32[]{:S(2)}) collective-permute-start(f32[480,128]{1,0:T(8,128)S(1)} %get-tuple-element.137.rest_3_), channel_id=1, source_target_pairs={{0,1},{1,0},{2,3},{3,2},{4,5},{5,4},{6,7},{7,6},{8,9},{9,8},{10,11... | collective-permute-start | bytes 737288 | tf_op jit(solution)/shard_map/cond/branch_1_fun/ppermute | solution.py:564
  109.5 9.4 %collective-permute-start.12 = (f32[480,128]{1,0:T(8,128)S(1)}, f32[480,128]{1,0:T(8,128)S(1)}, u32[]{:S(2)}, u32[]{:S(2)}) collective-permute-start(f32[480,128]{1,0:T(8,128)S(1)} %add.15.mine_ref), channel_id=1, source_target_pairs={{0,2},{1,3},{2,0},{3,1},{4,6},{5,7},{6,4},{7,5},{8,10},{9,11},{10,... | collective-permute-start | bytes 737288 | tf_op jit(solution)/shard_map/cond/branch_1_fun/ppermute | solution.py:564
  111.0 7.9 %copy-start.12 = (bf16[480,2048]{1,0:T(8,128)(2,1)S(1)}, bf16[480,2048]{1,0:T(8,128)(2,1)}, u32[]{:S(2)}) copy-start(bf16[480,2048]{1,0:T(8,128)(2,1)} %get-tuple-element.140.masked_ref) | copy-start | bytes 5898244 | tf_op jit(solution)/shard_map/cond
  118.9 6.8 %copy-start.9 = (f32[480,2048]{1,0:T(8,128)}, f32[480,2048]{1,0:T(8,128)S(1)}, u32[]{:S(2)}) copy-start(f32[480,2048]{1,0:T(8,128)S(1)} %branch_1_fun.9.rest_0_) | copy-start | bytes 11796484 | tf_op jit(solution)/shard_map/cond
  125.7 1.2 collective-permute-start.14
  126.9 3.6 %collective-permute-start.15 = (f32[8,128]{1,0:T(8,128)S(1)}, f32[8,128]{1,0:T(8,128)S(1)}, u32[]{:S(2)}, u32[]{:S(2)}) collective-permute-start(f32[8,128]{1,0:T(8,128)S(1)} %max.20), channel_id=1, source_target_pairs={{0,2},{1,3},{2,0},{3,1},{4,6},{5,7},{6,4},{7,5},{8,10},{9,11},{10,... | collective-permute-start | bytes 12296 | tf_op jit(solution)/shard_map/cond/branch_1_fun/ppermute | solution.py:564
  130.5 3.9 %collective-permute-start.16 = (f32[8,128]{1,0:T(8,128)S(1)}, f32[8,128]{1,0:T(8,128)S(1)}, u32[]{:S(2)}, u32[]{:S(2)}) collective-permute-start(f32[8,128]{1,0:T(8,128)S(1)} %max.21), channel_id=1, source_target_pairs={{0,4},{4,0},{8,12},{12,8},{1,5},{5,1},{9,13},{13,9},{2,6},{6,2},{1... | collective-permute-start | bytes 12296 | tf_op jit(solution)/shard_map/cond/branch_1_fun/ppermute | solution.py:564
  134.5 9.7 %collective-permute-start.17 = (f32[8,128]{1,0:T(8,128)S(1)}, f32[8,128]{1,0:T(8,128)S(1)}, u32[]{:S(2)}, u32[]{:S(2)}) collective-permute-start(f32[8,128]{1,0:T(8,128)S(1)} %max.22), channel_id=1, source_target_pairs={{0,8},{4,12},{8,0},{12,4},{1,9},{5,13},{9,1},{13,5},{2,10},{6,14},... | collective-permute-start | bytes 12296 | tf_op jit(solution)/shard_map/cond/branch_1_fun/ppermute | solution.py:564
  144.2 5.1 %copy-start.10 = (f32[480,2048]{1,0:T(8,128)S(1)}, f32[480,2048]{1,0:T(8,128)}, u32[]{:S(2)}) copy-start(f32[480,2048]{1,0:T(8,128)} %copy-done.9) | copy-start | bytes 11796484 | tf_op jit(solution)/shard_map/cond

commit v5 on v4

--- a/solution.py
+++ b/solution.py
@@ -149,7 +149,7 @@
     piece = native // (micro * windows)
     rows = groups * micro * WINDOWS_PER_OWNER * piece
     sent = rows // groups + NOTES
-    fb = feature_block(features)
+    fb = feature_block(features, 1024)
     far = pl.BlockSpec(memory_space=pltpu.MemorySpace.HBM)
     return pl.pallas_call(
         functools.partial(route_body, groups, slots, piece),
@@ -216,7 +216,7 @@
 def pack(x, hot, groups, *after):
     native, features = x.shape
     rows = hot.shape[0]
-    fb = feature_block(features)
+    fb = feature_block(features, 1024)
     return pl.pallas_call(
         functools.partial(pack_body, groups),
         grid=(features // fb,),
@@ -352,6 +352,21 @@
     )(table, *sent, *after)
 
 
+def gate_body(*refs):
+    pass
+
+
+def gate(blocks, *after):
+    return pl.pallas_call(
+        gate_body,
+        out_shape=[jax.ShapeDtypeStruct(x.shape, x.dtype) for x in blocks],
+        in_specs=[ANY] * (len(blocks) + len(after)),
+        out_specs=[ANY] * len(blocks),
+        input_output_aliases={i: i for i in range(len(blocks))},
+        cost_estimate=SMALL,
+    )(*blocks, *after)
+
+
 def project_body(groups, pick_ref, table_ref, *rest):
     out_ref, rows_ref, wide_ref, total_ref = rest[-4:]
     slots = table_ref.shape[0]
@@ -375,7 +390,7 @@
     count, top = pick.shape
     groups = len(blocks)
     slots, features = table.shape[:2]
-    fb = feature_block(features)
+    fb = feature_block(features, 1024)
     return pl.pallas_call(
         functools.partial(project_body, groups),
         grid=(features // fb,),
@@ -424,7 +439,7 @@
 def back(mine, other, lane, pick, down, groups, *after):
     rows, top = pick.shape
     slots, features, _ = down.shape
-    fb = feature_block(features)
+    fb = feature_block(features, 1024)
     each = rows // groups
     return pl.pallas_call(
         functools.partial(back_body, groups),
@@ -484,7 +499,7 @@
 def grads(mine, other, lane, pick, low, acts, masked, slots, *after):
     rows, top = pick.shape
     features = acts.shape[1]
-    fb = feature_block(features)
+    fb = feature_block(features, 1024)
     return pl.pallas_call(
         functools.partial(grads_body, slots),
         grid=(features // fb,),
@@ -517,18 +532,18 @@
 
 def scaled(largest, down, up):
     slots, features, top = down.shape
-    down_spec = pl.BlockSpec((1, features, top), lambda e: (e, 0, 0))
-    up_spec = pl.BlockSpec((1, top, features), lambda e: (e, 0, 0))
+    down_spec = pl.BlockSpec((2, features, top), lambda e: (e, 0, 0))
+    up_spec = pl.BlockSpec((2, top, features), lambda e: (e, 0, 0))
     return pl.pallas_call(
         scaled_body,
-        grid=(slots,),
+        grid=(slots // 2,),
         out_shape=[
             jax.ShapeDtypeStruct(down.shape, BF16),
             jax.ShapeDtypeStruct(up.shape, BF16),
         ],
         in_specs=[WHOLE, down_spec, up_spec],
         out_specs=[down_spec, up_spec],
-        compiler_params=params(16),
+        compiler_params=params(32),
         cost_estimate=SMALL,
     )(largest, down, up)
 
@@ -545,7 +560,7 @@
     groups = len(returned)
     native, features = frozen.shape
     each = returned[0].shape[0]
-    fb = feature_block(features)
+    fb = feature_block(features, 1024)
     return pl.pallas_call(
         functools.partial(finish_body, groups),
         grid=(features // fb,),
@@ -635,20 +650,18 @@
         masked_sent, adapter_up_weights, micro * WINDOWS_PER_OWNER, piece, frozen
     )
 
-    def lower(near_first, low_part, pick, lane, table, far, weights, frozen):
+    def lower(near_first, low_part, pick, lane, table):
         low_mine, low_other = all_but_last_sum(near_first, low_part, "tp")
-        if far:
-            frozen = frozen_product(*far, weights, frozen, low_part)
-        *backs, low = back(low_mine, low_other, lane, pick, table, groups, frozen)
-        return backs, low, frozen
+        *backs, low = back(low_mine, low_other, lane, pick, table, groups)
+        return backs, low
 
     def lift(near_first, acts_sent, low, pick, lane, masked, table, far, weights, frozen):
         lift_part, acts = project(acts_sent, pick, table, low)
         lift_mine, lift_other = all_but_last_sum(near_first, lift_part, "tp")
         if far:
-            sources, blocks = far
-            blocks = [partner(x, "tp", 1) for x in blocks]
-            frozen = frozen_product(sources ^ 1, blocks, weights, frozen, lift_part)
+            sources = jnp.concatenate([far[0], far[0] ^ 1])
+            blocks = far[1] + [partner(x, "tp", 1) for x in far[1]]
+            frozen = frozen_product(sources, blocks, weights, frozen, lift_part)
         down_sum, up_sum, largest = grads(
             lift_mine, lift_other, lane, pick, low, acts, masked, slots, frozen
         )
@@ -656,7 +669,7 @@
         return scaled(largest, down_sum, up_sum), frozen
 
     early = window_live_rows[0, 0] <= piece
-    backs, low, frozen = lax.cond(
+    backs, low = lax.cond(
         early,
         functools.partial(lower, True),
         functools.partial(lower, False),
@@ -664,11 +677,8 @@
         pick,
         lane,
         adapter_down_weights,
-        far,
-        frozen_weight_matrix,
-        frozen,
-    )
-    returned = across(backs, -1)
+    )
+    returned = across(gate(backs, acts_sent[2]), -1)
     (grad_down, grad_up), frozen = lax.cond(
         early,
         functools.partial(lift, True),

time: 155 us -> 152 us (0.981)
  Pallas kernels: 73.9 us -> 65.5 us
  local copies, waits for them, and re-layouts: 6.05 us -> 8.97 us
  waiting for transfers between devices: 28 us -> 30.3 us
    pallas_call x3 -> x2, Pallas kernels: 31.4 us -> 27.4 us  [frozen_product(): pl.pallas_call(functools.partial(frozen_body, parts, so_far is not None),...]
    unnamed x18 -> x22, local copies, waits for them, and re-layouts: 4.82 us -> 7.7 us
    ppermute x10, waiting for transfers between devices: 16.4 us -> 18.7 us  [partner(): return lax.ppermute(x, axis, [(i, i ^ bit) for i in range(count)])]
    pallas_call x1 -> x2, Pallas kernels: 5.11 us -> 4.31 us  [the longest x1 4.31 us: scaled(): pl.pallas_call(scaled_body, grid=(slots // 2,), out_shape=[jax.ShapeDtype...]
  transfers between devices with their start and end apart: 20 -> 20, of which waited for: 7 -> 8; matrix products, arithmetic and copies ran while one was open for 1% -> 1% of each run, Pallas kernels for 41% -> 37%
where the time goes in v5:
time: 152 us
  Pallas kernels  65.5 us (43%)
  starting transfers between devices  44.1 us (29%)
  waiting for transfers between devices  30.3 us (20%)
  local copies, waits for them, and re-layouts  8.97 us (6%)
    ppermute x9, starting transfers between devices, across(): lax.ppermute(blocks[s], 'grp', [(i, (i + sign * s) % groups) for i in ran...  33 us
    pallas_call x2, Pallas kernels, frozen_product(): pl.pallas_call(functools.partial(frozen_body, parts, so_far is not None),...  27.4 us
    ppermute x10, waiting for transfers between devices, partner(): return lax.ppermute(x, axis, [(i, i ^ bit) for i in range(count)])  18.7 us
    ppermute x9, waiting for transfers between devices, across(): lax.ppermute(blocks[s], 'grp', [(i, (i + sign * s) % groups) for i in ran...  11.6 us
    ppermute x10, starting transfers between devices, partner(): return lax.ppermute(x, axis, [(i, i ^ bit) for i in range(count)])  8.54 us
    unnamed x22, local copies, waits for them, and re-layouts  7.7 us
    pallas_call x1, Pallas kernels, grads(): pl.pallas_call(functools.partial(grads_body, slots), grid=(features // fb...  6.42 us
    pallas_call x1, Pallas kernels, route(): pl.pallas_call(functools.partial(route_body, groups, slots, piece), grid=...  5.55 us
  transfers between devices with their start and end apart: 20, of which 8 were waited for; matrix products, arithmetic and copies ran while one was open for 1% of the time, Pallas kernels for 37%

profile of v5, /device:TPU:0, one launch (start us, length us, event | category | flops | bytes accessed | tf_op | source)
XLA Modules:
  0.0 151.6 jit_solution(2217695451112642080)
XLA Ops:
  0.6 5.5 %shard_map.112 = (bf16[128,2048]{1,0:T(8,128)(2,1)}, bf16[128,2048]{1,0:T(8,128)(2,1)}, bf16[128,2048]{1,0:T(8,128)(2,1)}, bf16[128,2048]{1,0:T(8,128)(2,1)}, bf...) custom-call(s32[3,8]{1,0:T(4,128)} %adapter_in.1, s32[32]{0:T(128)} %slot_in.1, s32[32]{0:T(128)} %rank_in.1, ...), custom_call_target="tpu_custom_call" | custom-call | flops 1000000 | bytes 100000 | tf_op jit(solution)/shard_map/pallas_call | solution.py:154
  6.2 0.5 collective-permute-start.19
  6.7 2.6 %collective-permute-start.25 = (bf16[480,2048]{1,0:T(8,128)(2,1)}, bf16[480,2048]{1,0:T(8,128)(2,1)}, u32[]{:S(2)}, u32[]{:S(2)}) collective-permute-start(bf16[480,2048]{1,0:T(8,128)(2,1)} %get-tuple-element.148.rest_0_), channel_id=1, source_target_pairs={{0,2},{1,3},{2,0},{3,1},{4,6},{5,7},{6,4},{7,5},{8,10},{9,11},{10,... | collective-permute-start | bytes 5898248 | tf_op jit(solution)/shard_map/ppermute | solution.py:596
  9.3 1.6 %collective-permute-start.20 = (bf16[128,2048]{1,0:T(8,128)(2,1)}, bf16[128,2048]{1,0:T(8,128)(2,1)S(1)}, u32[]{:S(2)}, u32[]{:S(2)}) collective-permute-start(bf16[128,2048]{1,0:T(8,128)(2,1)} %get-tuple-element.149), channel_id=1, source_target_pairs={{0,4},{4,8},{8,12},{12,0},{1,5},{5,9},{9,13},{13,1},{2,6},{6,10},{... | collective-permute-start | bytes 1572872 | tf_op jit(solution)/shard_map/ppermute | solution.py:631
  10.8 2.3 %collective-permute-start.18 = (bf16[128,2048]{1,0:T(8,128)(2,1)}, bf16[128,2048]{1,0:T(8,128)(2,1)S(1)}, u32[]{:S(2)}, u32[]{:S(2)}) collective-permute-start(bf16[128,2048]{1,0:T(8,128)(2,1)} %get-tuple-element.147), channel_id=1, source_target_pairs={{0,12},{4,0},{8,4},{12,8},{1,13},{5,1},{9,5},{13,9},{2,14},{6,2},{... | collective-permute-start | bytes 1572872 | tf_op jit(solution)/shard_map/ppermute | solution.py:631
  13.1 0.8 collective-permute-start.21
  13.9 0.6 pad_add_fusion.2.source_ref
  14.5 11.6 %collective-permute-done.20.rest_4_.rest_1_ = bf16[128,2048]{1,0:T(8,128)(2,1)S(1)} collective-permute-done((bf16[128,2048]{1,0:T(8,128)(2,1)}, bf16[128,2048]{1,0:T(8,128)(2,1)S(1)}, u32[]{:S(2)}, u32[]{:S(2)}) %collective-permute-start.20) | collective-permute-done | bytes 524320 | tf_op jit(solution)/shard_map/ppermute | solution.py:631
  26.1 0.8 copy-done.1
  26.9 1.3 copy-done.15
  28.2 14.5 %shard_map.113.rest_1_.rest_4_ = f32[480,2048]{1,0:T(8,128)} custom-call(s32[2]{0:T(128)} %pad_add_fusion.2.source_ref, bf16[480,2048]{1,0:T(8,128)(2,1)} %get-tuple-element.148.rest_0_, bf16[480,2048]{1,0:T(8,128)(2,1)} %copy-done.15, bf16[2048,8192]{1,0:T(8,128)(2,1)} %rest_3_.1, bf16[2048,8192]{1,0:T(8,128)(2,1)} %rest_3_.1, bf16[128,2048]{1,0:T(8,128)(2,1)} %copy-done.1), custom_call_target="tpu_custom_call" | custom-call | flops 1000000 | bytes 100000 | tf_op jit(solution)/shard_map/pallas_call | solution.py:258
  42.8 0.8 copy-done.3
  43.5 4.3 %shard_map.114 = (bf16[120,2048]{1,0:T(8,128)(2,1)}, bf16[120,2048]{1,0:T(8,128)(2,1)}, bf16[120,2048]{1,0:T(8,128)(2,1)}, bf16[120,2048]{1,0:T(8,128)(2,1)}, bf16[480,480]{1,0:T(8,128)(2,1)}) custom-call(bf16[480,480]{1,0:T(8,128)(2,1)} %get-tuple-element.146.hot_ref, bf16[480,2048]{1,0:T(8,128)(2,1)} %bitcast.14, bf16[128,2048]{1,0:T(8,128)(2,1)} %copy-done.3, ...), custom_call_target="tpu_custom_call" | custom-call | flops 1000000 | bytes 100000 | tf_op jit(solution)/shard_map/pallas_call | solution.py:220
  47.9 23.2 %collective-permute-start.23 = (bf16[120,2048]{1,0:T(8,128)(2,1)}, bf16[120,2048]{1,0:T(8,128)(2,1)}, u32[]{:S(2)}, u32[]{:S(2)}) collective-permute-start(bf16[120,2048]{1,0:T(8,128)(2,1)} %get-tuple-element.156), channel_id=1, source_target_pairs={{0,8},{4,12},{8,0},{12,4},{1,9},{5,13},{9,1},{13,5},{2,10},{6,14},... | collective-permute-start | bytes 1474568 | tf_op jit(solution)/shard_map/ppermute | solution.py:631
  71.1 1.3 slice.3
  73.0 0.1 collective-permute-start.22
  73.1 3.8 %collective-permute-start.24 = (bf16[120,2048]{1,0:T(8,128)(2,1)}, bf16[120,2048]{1,0:T(8,128)(2,1)}, u32[]{:S(2)}, u32[]{:S(2)}) collective-permute-start(bf16[120,2048]{1,0:T(8,128)(2,1)} %get-tuple-element.157), channel_id=1, source_target_pairs={{0,12},{4,0},{8,4},{12,8},{1,13},{5,1},{9,5},{13,9},{2,14},{6,2},{... | collective-permute-start | bytes 1474568 | tf_op jit(solution)/shard_map/ppermute | solution.py:631
  76.9 2.2 %copy-done = bf16[8,128,2048]{2,1,0:T(8,128)(2,1)S(1)} copy-done((bf16[8,128,2048]{2,1,0:T(8,128)(2,1)S(1)}, bf16[8,128,2048]{2,1,0:T(8,128)(2,1)}, u32[]{:S(2)}) %copy-start) | copy-done | bytes 4194328
  79.1 1.0 copy-done.4
  80.2 4.8 %shard_map.115 = (f32[480,128]{1,0:T(8,128)S(1)}, f32[480,128]{1,0:T(8,128)S(1)}, f32[480,128]{1,0:T(8,128)S(1)}, bf16[480,2048]{1,0:T(8,128)(2,1)}) custom-call(bf16[8,128,2048]{2,1,0:T(8,128)(2,1)S(1)} %copy-done, bf16[128,2048]{1,0:T(8,128)(2,1)S(1)} %copy-done.5, bf16[128,2048]{1,0:T(8,128)(2,1)S(1)} %copy-done.2, ...), custom_call_target="tpu_custom_call" | custom-call | flops 1000000 | bytes 100000 | tf_op jit(solution)/shard_map/pallas_call | solution.py:335
  85.0 13.8 %conditional.2 = ((bf16[120,2048]{1,0:T(8,128)(2,1)S(1)}, bf16[120,2048]{1,0:T(8,128)(2,1)}, bf16[120,2048]{1,0:T(8,128)(2,1)}, bf16[120,2048]{1,0:T(8,128)(2,1)S(1)}, bf16[480,1024]{1,0:T(8,128)(2,1)S(1)})) conditional(s32[]{:T(128)} %bitcast.6, (f32[480,128]{1,0:T(8,128)S(1)}, f32[480,128]{1,0:T(8,128)S(1)}, f32[480,128]{1,0:T(8,128)S(1)}, ...), branch_computations={%region_0.1_spmd, %region_1.2_spmd} | conditional | flops 1061440 | bytes 2803448 | solution.py:672
  85.0 1.5 collective-permute-done.2
  86.5 0.6 collective-permute-start.3
  87.1 7.5 %collective-permute-done.3.other_ref = f32[480,128]{1,0:T(8,128)S(1)} collective-permute-done((f32[480,128]{1,0:T(8,128)S(1)}, f32[480,128]{1,0:T(8,128)S(1)}, u32[]{:S(2)}, u32[]{:S(2)}) %collective-permute-start.3) | collective-permute-done | bytes 245792 | tf_op jit(solution)/shard_map/cond/branch_1_fun/ppermute | solution.py:579
  94.6 4.2 %branch_1_fun.5 = (bf16[120,2048]{1,0:T(8,128)(2,1)S(1)}, bf16[120,2048]{1,0:T(8,128)(2,1)}, bf16[120,2048]{1,0:T(8,128)(2,1)}, bf16[120,2048]{1,0:T(8,128)(2,1)S(1)}, bf16[480,1024]{1,0:T(8,128)(2,1)S(1)}) custom-call(f32[480,128]{1,0:T(8,128)S(1)} %add.13.mine_ref, f32[480,128]{1,0:T(8,128)S(1)} %collective-permute-done.3.other_ref, ...), custom_call_target="tpu_custom_call" | custom-call | flops 1000000 | bytes 100000 | tf_op jit(solution)/shard_map/cond/branch_1_fun/pallas_call | solution.py:444
  98.8 0.8 copy-done.14
  99.6 0.0 collective-permute-start.26
  99.6 0.8 copy-done.16
  100.4 1.3 collective-permute-start.28
  101.7 46.2 %conditional.3 = (bf16[8,2048,128]{2,1,0:T(8,128)(2,1)}, bf16[8,128,2048]{2,1,0:T(8,128)(2,1)}, f32[480,2048]{1,0:T(8,128)S(1)}) conditional(s32[]{:T(128)} %bitcast.6, (f32[480,128]{1,0:T(8,128)S(1)}, bf16[8,2048,128]{2,1,0:T(8,128)(2,1)}, bf16[120,2048]{1,0:T(8,128)(2,1)}, bf16[120,2048]{1,0:T(8,128)(2,1)}, bf16[120,2048]{1,0:T(8,128)(2,1)}, ...), branch_computations={%region_2.3_spmd, %region_3.4_spmd} | conditional | flops 4065539 | bytes 66133052 | solution.py:682
  102.1 0.1 collective-permute-start.13
  102.2 4.9 %branch_1_fun.6 = (f32[480,128]{1,0:T(8,128)S(1)}, bf16[480,2048]{1,0:T(8,128)(2,1)S(1)}) custom-call(f32[480,128]{1,0:T(8,128)S(1)} %get-tuple-element.96.pick_ref, bf16[8,2048,128]{2,1,0:T(8,128)(2,1)} %get-tuple-element.97.table_ref, bf16[120,2048]{1,0:T(8,128)(2,1)} %get-tuple-element.98.rest_0_, bf16[120,2048]{1,0:T(8,128)(2,1)} %get-tuple-element.99.rest_1_, ...), custom_call_target="tpu_custom_call" | custom-call | flops 1000000 | bytes 100000 | tf_op jit(solution)/shard_map/cond/branch_1_fun/pallas_call | solution.py:394
  107.1 0.5 collective-permute-start.11
  107.6 1.1 collective-permute-done.11
  108.8 0.6 collective-permute-start.12
  109.4 0.1 pad_add_fusion.1.source_ref
  109.5 12.8 %branch_1_fun.7.rest_0_ = f32[480,2048]{1,0:T(8,128)S(1)} custom-call(s32[2]{0:T(128)S(1)} %pad_add_fusion.1.source_ref, bf16[480,2048]{1,0:T(8,128)(2,1)} %get-tuple-element.108.rest_0_, bf16[480,2048]{1,0:T(8,128)(2,1)S(1)} %collective-permute-done.13.rest_1_, bf16[2048,8192]{1,0:T(8,128)(2,1)} %get-tuple-element.109.rest_2_.rest_3_, ...), custom_call_target="tpu_custom_call" | custom-call | flops 1000000 | bytes 100000 | tf_op jit(solution)/shard_map/cond/branch_1_fun/pallas_call | solution.py:258
  122.4 6.4 %branch_1_fun.8 = (f32[8,2048,128]{2,1,0:T(8,128)S(1)}, f32[8,128,2048]{2,1,0:T(8,128)S(1)}, f32[8,128]{1,0:T(8,128)S(1)}) custom-call(f32[480,128]{1,0:T(8,128)S(1)} %add.15.mine_ref, f32[480,128]{1,0:T(8,128)S(1)} %collective-permute-done.12.other_ref, f32[480,128]{1,0:T(8,128)S(1)} %get-tuple-element.104.lane_ref, ...), custom_call_target="tpu_custom_call" | custom-call | flops 1000000 | bytes 100000 | tf_op jit(solution)/shard_map/cond/branch_1_fun/pallas_call | solution.py:503
  128.8 0.1 collective-permute-start.14
  129.0 1.1 collective-permute-done.14
  130.1 1.5 collective-permute-start.15
  131.6 2.1 %collective-permute-done.15 = f32[8,128]{1,0:T(8,128)S(1)} collective-permute-done((f32[8,128]{1,0:T(8,128)S(1)}, f32[8,128]{1,0:T(8,128)S(1)}, u32[]{:S(2)}, u32[]{:S(2)}) %collective-permute-start.15) | collective-permute-done | bytes 4128 | tf_op jit(solution)/shard_map/cond/branch_1_fun/ppermute | solution.py:579
  133.7 2.2 %collective-permute-start.16 = (f32[8,128]{1,0:T(8,128)S(1)}, f32[8,128]{1,0:T(8,128)S(1)}, u32[]{:S(2)}, u32[]{:S(2)}) collective-permute-start(f32[8,128]{1,0:T(8,128)S(1)} %max.21), channel_id=1, source_target_pairs={{0,4},{4,0},{8,12},{12,8},{1,5},{5,1},{9,13},{13,9},{2,6},{6,2},{1... | collective-permute-start | bytes 12296 | tf_op jit(solution)/shard_map/cond/branch_1_fun/ppermute | solution.py:579
  135.9 1.9 %collective-permute-done.16 = f32[8,128]{1,0:T(8,128)S(1)} collective-permute-done((f32[8,128]{1,0:T(8,128)S(1)}, f32[8,128]{1,0:T(8,128)S(1)}, u32[]{:S(2)}, u32[]{:S(2)}) %collective-permute-start.16) | collective-permute-done | bytes 4128 | tf_op jit(solution)/shard_map/cond/branch_1_fun/ppermute | solution.py:579
  137.8 2.4 %collective-permute-start.17 = (f32[8,128]{1,0:T(8,128)S(1)}, f32[8,128]{1,0:T(8,128)S(1)}, u32[]{:S(2)}, u32[]{:S(2)}) collective-permute-start(f32[8,128]{1,0:T(8,128)S(1)} %max.22), channel_id=1, source_target_pairs={{0,8},{4,12},{8,0},{12,4},{1,9},{5,13},{9,1},{13,5},{2,10},{6,14},... | collective-permute-start | bytes 12296 | tf_op jit(solution)/shard_map/cond/branch_1_fun/ppermute | solution.py:579
  140.2 3.4 %collective-permute-done.17 = f32[8,128]{1,0:T(8,128)S(1)} collective-permute-done((f32[8,128]{1,0:T(8,128)S(1)}, f32[8,128]{1,0:T(8,128)S(1)}, u32[]{:S(2)}, u32[]{:S(2)}) %collective-permute-start.17) | collective-permute-done | bytes 4128 | tf_op jit(solution)/shard_map/cond/branch_1_fun/ppermute | solution.py:579
  143.6 4.3 %branch_1_fun.9 = (bf16[8,2048,128]{2,1,0:T(8,128)(2,1)}, bf16[8,128,2048]{2,1,0:T(8,128)(2,1)}) custom-call(f32[8,128]{1,0:T(8,128)S(1)} %max.23.largest_ref, f32[8,2048,128]{2,1,0:T(8,128)S(1)} %get-tuple-element.112.down_ref, f32[8,128,2048]{2,1,0:T(8,128)S(1)} %get-tuple-element.113.up_ref), custom_call_target="tpu_custom_call" | custom-call | flops 1000000 | bytes 100000 | tf_op jit(solution)/shard_map/cond/branch_1_fun/pallas_call | solution.py:537
  148.0 3.6 %shard_map.117 = bf16[480,2048]{1,0:T(8,128)(2,1)} custom-call(bf16[480,480]{1,0:T(8,128)(2,1)S(1)} %copy-done.6, f32[480,2048]{1,0:T(8,128)S(1)} %get-tuple-element.162.frozen_ref, bf16[120,2048]{1,0:T(8,128)(2,1)} %copy-done.14, bf16[120,2048]{1,0:T(8,128)(2,1)S(1)} %collective-permute-done.26.rest_1_, ...), custom_call_target="tpu_custom_call" | custom-call | flops 1000000 | bytes 100000 | tf_op jit(solution)/shard_map/pallas_call | solution.py:564
  (44 shorter events, 0.2 us)
Async XLA Ops:
  6.2 19.9 %collective-permute-start.19 = (bf16[480,2048]{1,0:T(8,128)(2,1)}, bf16[480,2048]{1,0:T(8,128)(2,1)S(1)}, u32[]{:S(2)}, u32[]{:S(2)}) collective-permute-start(bf16[480,2048]{1,0:T(8,128)(2,1)} %get-tuple-element.148.rest_0_), channel_id=1, source_target_pairs={{0,1},{1,0},{2,3},{3,2},{4,5},{5,4},{6,7},{7,6},{8,9},{9,8},{10,11... | collective-permute-start | bytes 5898248 | tf_op jit(solution)/shard_map/ppermute | solution.py:579
  6.7 93.7 %collective-permute-start.25 = (bf16[480,2048]{1,0:T(8,128)(2,1)}, bf16[480,2048]{1,0:T(8,128)(2,1)}, u32[]{:S(2)}, u32[]{:S(2)}) collective-permute-start(bf16[480,2048]{1,0:T(8,128)(2,1)} %get-tuple-element.148.rest_0_), channel_id=1, source_target_pairs={{0,2},{1,3},{2,0},{3,1},{4,6},{5,7},{6,4},{7,5},{8,10},{9,11},{10,... | collective-permute-start | bytes 5898248 | tf_op jit(solution)/shard_map/ppermute | solution.py:596
  9.3 16.8 %collective-permute-start.20 = (bf16[128,2048]{1,0:T(8,128)(2,1)}, bf16[128,2048]{1,0:T(8,128)(2,1)S(1)}, u32[]{:S(2)}, u32[]{:S(2)}) collective-permute-start(bf16[128,2048]{1,0:T(8,128)(2,1)} %get-tuple-element.149), channel_id=1, source_target_pairs={{0,4},{4,8},{8,12},{12,0},{1,5},{5,9},{9,13},{13,1},{2,6},{6,10},{... | collective-permute-start | bytes 1572872 | tf_op jit(solution)/shard_map/ppermute | solution.py:631
  10.8 31.9 %collective-permute-start.18 = (bf16[128,2048]{1,0:T(8,128)(2,1)}, bf16[128,2048]{1,0:T(8,128)(2,1)S(1)}, u32[]{:S(2)}, u32[]{:S(2)}) collective-permute-start(bf16[128,2048]{1,0:T(8,128)(2,1)} %get-tuple-element.147), channel_id=1, source_target_pairs={{0,12},{4,0},{8,4},{12,8},{1,13},{5,1},{9,5},{13,9},{2,14},{6,2},{... | collective-permute-start | bytes 1572872 | tf_op jit(solution)/shard_map/ppermute | solution.py:631
  13.1 63.8 %collective-permute-start.21 = (bf16[128,2048]{1,0:T(8,128)(2,1)}, bf16[128,2048]{1,0:T(8,128)(2,1)S(1)}, u32[]{:S(2)}, u32[]{:S(2)}) collective-permute-start(bf16[128,2048]{1,0:T(8,128)(2,1)} %get-tuple-element.152), channel_id=1, source_target_pairs={{0,8},{4,12},{8,0},{12,4},{1,9},{5,13},{9,1},{13,5},{2,10},{6,14},... | collective-permute-start | bytes 1572872 | tf_op jit(solution)/shard_map/ppermute | solution.py:631
  26.1 0.8 copy-start.1
  26.9 1.3 copy-start.15
  42.7 34.2 %copy-start.2 = (bf16[128,2048]{1,0:T(8,128)(2,1)S(1)}, bf16[128,2048]{1,0:T(8,128)(2,1)}, u32[]{:S(2)}) copy-start(bf16[128,2048]{1,0:T(8,128)(2,1)} %copy-done.1) | copy-start | bytes 1572868
  42.7 34.2 %copy-start.5 = (bf16[128,2048]{1,0:T(8,128)(2,1)S(1)}, bf16[128,2048]{1,0:T(8,128)(2,1)}, u32[]{:S(2)}) copy-start(bf16[128,2048]{1,0:T(8,128)(2,1)} %get-tuple-element.151.rest_0_) | copy-start | bytes 1572868
  42.7 0.8 copy-start.3
  47.9 50.9 %collective-permute-start.23 = (bf16[120,2048]{1,0:T(8,128)(2,1)}, bf16[120,2048]{1,0:T(8,128)(2,1)}, u32[]{:S(2)}, u32[]{:S(2)}) collective-permute-start(bf16[120,2048]{1,0:T(8,128)(2,1)} %get-tuple-element.156), channel_id=1, source_target_pairs={{0,8},{4,12},{8,0},{12,4},{1,9},{5,13},{9,1},{13,5},{2,10},{6,14},... | collective-permute-start | bytes 1474568 | tf_op jit(solution)/shard_map/ppermute | solution.py:631
  73.0 28.6 %collective-permute-start.22 = (bf16[120,2048]{1,0:T(8,128)(2,1)}, bf16[120,2048]{1,0:T(8,128)(2,1)}, u32[]{:S(2)}, u32[]{:S(2)}) collective-permute-start(bf16[120,2048]{1,0:T(8,128)(2,1)} %get-tuple-element.155), channel_id=1, source_target_pairs={{0,4},{4,8},{8,12},{12,0},{1,5},{5,9},{9,13},{13,1},{2,6},{6,10},{... | collective-permute-start | bytes 1474568 | tf_op jit(solution)/shard_map/ppermute | solution.py:631
  73.1 28.6 %collective-permute-start.24 = (bf16[120,2048]{1,0:T(8,128)(2,1)}, bf16[120,2048]{1,0:T(8,128)(2,1)}, u32[]{:S(2)}, u32[]{:S(2)}) collective-permute-start(bf16[120,2048]{1,0:T(8,128)(2,1)} %get-tuple-element.157), channel_id=1, source_target_pairs={{0,12},{4,0},{8,4},{12,8},{1,13},{5,1},{9,5},{13,9},{2,14},{6,2},{... | collective-permute-start | bytes 1474568 | tf_op jit(solution)/shard_map/ppermute | solution.py:631
  76.9 2.2 %copy-start = (bf16[8,128,2048]{2,1,0:T(8,128)(2,1)S(1)}, bf16[8,128,2048]{2,1,0:T(8,128)(2,1)}, u32[]{:S(2)}) copy-start(bf16[8,128,2048]{2,1,0:T(8,128)(2,1)} %table_ref.1) | copy-start | bytes 12582916
  79.1 1.0 copy-start.4
  80.2 4.8 %copy-start.9 = (bf16[8,2048,128]{2,1,0:T(8,128)(2,1)S(1)}, bf16[8,2048,128]{2,1,0:T(8,128)(2,1)}, u32[]{:S(2)}) copy-start(bf16[8,2048,128]{2,1,0:T(8,128)(2,1)} %param.16) | copy-start | bytes 12582916
  85.0 1.5 collective-permute-start.2
  86.5 8.1 %collective-permute-start.3 = (f32[480,128]{1,0:T(8,128)S(1)}, f32[480,128]{1,0:T(8,128)S(1)}, u32[]{:S(2)}, u32[]{:S(2)}) collective-permute-start(f32[480,128]{1,0:T(8,128)S(1)} %add.13.mine_ref), channel_id=1, source_target_pairs={{0,2},{1,3},{2,0},{3,1},{4,6},{5,7},{6,4},{7,5},{8,10},{9,11},{10,... | collective-permute-start | bytes 737288 | tf_op jit(solution)/shard_map/cond/branch_1_fun/ppermute | solution.py:579
  98.8 0.8 copy-start.14
  99.6 0.8 copy-start.16
  99.6 48.3 %collective-permute-start.26 = (bf16[120,2048]{1,0:T(8,128)(2,1)}, bf16[120,2048]{1,0:T(8,128)(2,1)S(1)}, u32[]{:S(2)}, u32[]{:S(2)}) collective-permute-start(bf16[120,2048]{1,0:T(8,128)(2,1)} %get-tuple-element.168), channel_id=1, source_target_pairs={{0,12},{4,0},{8,4},{12,8},{1,13},{5,1},{9,5},{13,9},{2,14},{6,2},{... | collective-permute-start | bytes 1474568 | tf_op jit(solution)/shard_map/ppermute | solution.py:631
  100.4 47.6 %collective-permute-start.27 = (bf16[120,2048]{1,0:T(8,128)(2,1)}, bf16[120,2048]{1,0:T(8,128)(2,1)S(1)}, u32[]{:S(2)}, u32[]{:S(2)}) collective-permute-start(bf16[120,2048]{1,0:T(8,128)(2,1)} %get-tuple-element.169), channel_id=1, source_target_pairs={{0,8},{4,12},{8,0},{12,4},{1,9},{5,13},{9,1},{13,5},{2,10},{6,14},... | collective-permute-start | bytes 1474568 | tf_op jit(solution)/shard_map/ppermute | solution.py:631
  100.4 47.6 %collective-permute-start.28 = (bf16[120,2048]{1,0:T(8,128)(2,1)}, bf16[120,2048]{1,0:T(8,128)(2,1)S(1)}, u32[]{:S(2)}, u32[]{:S(2)}) collective-permute-start(bf16[120,2048]{1,0:T(8,128)(2,1)} %copy-done.16), channel_id=1, source_target_pairs={{0,4},{4,8},{8,12},{12,0},{1,5},{5,9},{9,13},{13,1},{2,6},{6,10},{... | collective-permute-start | bytes 1474568 | tf_op jit(solution)/shard_map/ppermute | solution.py:631
  101.7 46.3 %copy-start.6 = (bf16[480,480]{1,0:T(8,128)(2,1)S(1)}, bf16[480,480]{1,0:T(8,128)(2,1)}, u32[]{:S(2)}) copy-start(bf16[480,480]{1,0:T(8,128)(2,1)} %get-tuple-element.150.hot_ref) | copy-start | bytes 1382404
  102.1 7.4 %collective-permute-start.13 = (bf16[480,2048]{1,0:T(8,128)(2,1)}, bf16[480,2048]{1,0:T(8,128)(2,1)S(1)}, u32[]{:S(2)}, u32[]{:S(2)}) collective-permute-start(bf16[480,2048]{1,0:T(8,128)(2,1)} %get-tuple-element.108.rest_0_), channel_id=1, source_target_pairs={{0,1},{1,0},{2,3},{3,2},{4,5},{5,4},{6,7},{7,6},{8,9},{9,8},{10,11... | collective-permute-start | bytes 5898248 | tf_op jit(solution)/shard_map/cond/branch_1_fun/ppermute | solution.py:579
  102.2 7.3 %copy-start.8 = (f32[480,2048]{1,0:T(8,128)S(1)}, f32[480,2048]{1,0:T(8,128)}, u32[]{:S(2)}) copy-start(f32[480,2048]{1,0:T(8,128)} %get-tuple-element.110.rest_4_) | copy-start | bytes 11796484 | tf_op jit(solution)/shard_map/cond
  107.1 1.7 %collective-permute-start.11 = (f32[480,128]{1,0:T(8,128)S(1)}, f32[480,128]{1,0:T(8,128)S(1)}, u32[]{:S(2)}, u32[]{:S(2)}) collective-permute-start(f32[480,128]{1,0:T(8,128)S(1)} %get-tuple-element.103.rest_5_), channel_id=1, source_target_pairs={{0,1},{1,0},{2,3},{3,2},{4,5},{5,4},{6,7},{7,6},{8,9},{9,8},{10,11... | collective-permute-start | bytes 737288 | tf_op jit(solution)/shard_map/cond/branch_1_fun/ppermute | solution.py:579
  108.8 13.6 %collective-permute-start.12 = (f32[480,128]{1,0:T(8,128)S(1)}, f32[480,128]{1,0:T(8,128)S(1)}, u32[]{:S(2)}, u32[]{:S(2)}) collective-permute-start(f32[480,128]{1,0:T(8,128)S(1)} %add.15.mine_ref), channel_id=1, source_target_pairs={{0,2},{1,3},{2,0},{3,1},{4,6},{5,7},{6,4},{7,5},{8,10},{9,11},{10,... | collective-permute-start | bytes 737288 | tf_op jit(solution)/shard_map/cond/branch_1_fun/ppermute | solution.py:579
  109.5 12.9 %copy-start.13 = (bf16[480,2048]{1,0:T(8,128)(2,1)S(1)}, bf16[480,2048]{1,0:T(8,128)(2,1)}, u32[]{:S(2)}) copy-start(bf16[480,2048]{1,0:T(8,128)(2,1)} %get-tuple-element.106.masked_ref) | copy-start | bytes 5898244 | tf_op jit(solution)/shard_map/cond
  122.4 6.5 %copy-start.10 = (f32[480,2048]{1,0:T(8,128)}, f32[480,2048]{1,0:T(8,128)S(1)}, u32[]{:S(2)}) copy-start(f32[480,2048]{1,0:T(8,128)S(1)} %branch_1_fun.7.rest_0_) | copy-start | bytes 11796484 | tf_op jit(solution)/shard_map/cond
  128.8 1.2 collective-permute-start.14
  130.1 3.6 %collective-permute-start.15 = (f32[8,128]{1,0:T(8,128)S(1)}, f32[8,128]{1,0:T(8,128)S(1)}, u32[]{:S(2)}, u32[]{:S(2)}) collective-permute-start(f32[8,128]{1,0:T(8,128)S(1)} %max.20), channel_id=1, source_target_pairs={{0,2},{1,3},{2,0},{3,1},{4,6},{5,7},{6,4},{7,5},{8,10},{9,11},{10,... | collective-permute-start | bytes 12296 | tf_op jit(solution)/shard_map/cond/branch_1_fun/ppermute | solution.py:579
  133.7 4.1 %collective-permute-start.16 = (f32[8,128]{1,0:T(8,128)S(1)}, f32[8,128]{1,0:T(8,128)S(1)}, u32[]{:S(2)}, u32[]{:S(2)}) collective-permute-start(f32[8,128]{1,0:T(8,128)S(1)} %max.21), channel_id=1, source_target_pairs={{0,4},{4,0},{8,12},{12,8},{1,5},{5,1},{9,13},{13,9},{2,6},{6,2},{1... | collective-permute-start | bytes 12296 | tf_op jit(solution)/shard_map/cond/branch_1_fun/ppermute | solution.py:579
  137.8 5.8 %collective-permute-start.17 = (f32[8,128]{1,0:T(8,128)S(1)}, f32[8,128]{1,0:T(8,128)S(1)}, u32[]{:S(2)}, u32[]{:S(2)}) collective-permute-start(f32[8,128]{1,0:T(8,128)S(1)} %max.22), channel_id=1, source_target_pairs={{0,8},{4,12},{8,0},{12,4},{1,9},{5,13},{9,1},{13,5},{2,10},{6,14},... | collective-permute-start | bytes 12296 | tf_op jit(solution)/shard_map/cond/branch_1_fun/ppermute | solution.py:579
  143.6 4.3 %copy-start.11 = (f32[480,2048]{1,0:T(8,128)S(1)}, f32[480,2048]{1,0:T(8,128)}, u32[]{:S(2)}) copy-start(f32[480,2048]{1,0:T(8,128)} %copy-done.10) | copy-start | bytes 11796484 | tf_op jit(solution)/shard_map/cond

commit v6 on v5

--- a/solution.py
+++ b/solution.py
@@ -330,7 +330,7 @@
     slots, top, features = table.shape
     count = windows * piece
     rows = groups * count
-    fb = feature_block(features)
+    fb = feature_block(features, 1024)
     fixed = pl.BlockSpec((rows, top), lambda f: (0, 0))
     return pl.pallas_call(
         functools.partial(receive_body, groups, windows, piece),
@@ -627,10 +627,12 @@
         return x.transpose(0, 2, 1, 3).reshape(micro * piece * windows, features)
 
     def across(blocks, sign):
-        return [blocks[0]] + [
-            lax.ppermute(blocks[s], "grp", [(i, (i + sign * s) % groups) for i in range(groups)])
-            for s in range(1, groups)
-        ]
+        order = sorted(range(1, groups), key=lambda s: abs(2 * s - groups), reverse=sign > 0)
+        moved = {0: blocks[0]}
+        for s in order:
+            pairs = [(i, (i + sign * s) % groups) for i in range(groups)]
+            moved[s] = lax.ppermute(blocks[s], "grp", pairs)
+        return [moved[s] for s in range(groups)]
 
     *masked_out, masked_flat, hot = route(
         native(cotangent),

time: 152 us -> 152 us (level)
  no operation moved by 1% of the time
where the time goes in v6:
time: 152 us
  Pallas kernels  65.2 us (43%)
  starting transfers between devices  44.2 us (29%)
  waiting for transfers between devices  30.6 us (20%)
  local copies, waits for them, and re-layouts  8.95 us (6%)
    ppermute x9, starting transfers between devices, across(): moved[s] = lax.ppermute(blocks[s], 'grp', pairs)  33 us
    pallas_call x2, Pallas kernels, frozen_product(): pl.pallas_call(functools.partial(frozen_body, parts, so_far is not None),...  27.4 us
    ppermute x10, waiting for transfers between devices, partner(): return lax.ppermute(x, axis, [(i, i ^ bit) for i in range(count)])  19 us
    ppermute x9, waiting for transfers between devices, across(): moved[s] = lax.ppermute(blocks[s], 'grp', pairs)  11.6 us
    ppermute x10, starting transfers between devices, partner(): return lax.ppermute(x, axis, [(i, i ^ bit) for i in range(count)])  8.55 us
    unnamed x22, local copies, waits for them, and re-layouts  7.68 us
    pallas_call x1, Pallas kernels, grads(): pl.pallas_call(functools.partial(grads_body, slots), grid=(features // fb...  6.42 us
    pallas_call x1, Pallas kernels, route(): pl.pallas_call(functools.partial(route_body, groups, slots, piece), grid=...  5.55 us
  transfers between devices with their start and end apart: 20, of which 8 were waited for; matrix products, arithmetic and copies ran while one was open for 1% of the time, Pallas kernels for 37%

profile of v6, /device:TPU:0, one launch (start us, length us, event | category | flops | bytes accessed | tf_op | source)
XLA Modules:
  0.0 151.6 jit_solution(6896478212469920174)
XLA Ops:
  0.6 5.5 %shard_map.112 = (bf16[128,2048]{1,0:T(8,128)(2,1)}, bf16[128,2048]{1,0:T(8,128)(2,1)}, bf16[128,2048]{1,0:T(8,128)(2,1)}, bf16[128,2048]{1,0:T(8,128)(2,1)}, bf...) custom-call(s32[3,8]{1,0:T(4,128)} %adapter_in.1, s32[32]{0:T(128)} %slot_in.1, s32[32]{0:T(128)} %rank_in.1, ...), custom_call_target="tpu_custom_call" | custom-call | flops 1000000 | bytes 100000 | tf_op jit(solution)/shard_map/pallas_call | solution.py:154
  6.2 0.5 collective-permute-start.19
  6.7 2.6 %collective-permute-start.25 = (bf16[480,2048]{1,0:T(8,128)(2,1)}, bf16[480,2048]{1,0:T(8,128)(2,1)}, u32[]{:S(2)}, u32[]{:S(2)}) collective-permute-start(bf16[480,2048]{1,0:T(8,128)(2,1)} %get-tuple-element.148.rest_0_), channel_id=1, source_target_pairs={{0,2},{1,3},{2,0},{3,1},{4,6},{5,7},{6,4},{7,5},{8,10},{9,11},{10,... | collective-permute-start | bytes 5898248 | tf_op jit(solution)/shard_map/ppermute | solution.py:596
  9.3 1.6 %collective-permute-start.20 = (bf16[128,2048]{1,0:T(8,128)(2,1)}, bf16[128,2048]{1,0:T(8,128)(2,1)S(1)}, u32[]{:S(2)}, u32[]{:S(2)}) collective-permute-start(bf16[128,2048]{1,0:T(8,128)(2,1)} %get-tuple-element.149), channel_id=1, source_target_pairs={{0,4},{4,8},{8,12},{12,0},{1,5},{5,9},{9,13},{13,1},{2,6},{6,10},{... | collective-permute-start | bytes 1572872 | tf_op jit(solution)/shard_map/ppermute | solution.py:634
  10.8 2.3 %collective-permute-start.18 = (bf16[128,2048]{1,0:T(8,128)(2,1)}, bf16[128,2048]{1,0:T(8,128)(2,1)S(1)}, u32[]{:S(2)}, u32[]{:S(2)}) collective-permute-start(bf16[128,2048]{1,0:T(8,128)(2,1)} %get-tuple-element.147), channel_id=1, source_target_pairs={{0,12},{4,0},{8,4},{12,8},{1,13},{5,1},{9,5},{13,9},{2,14},{6,2},{... | collective-permute-start | bytes 1572872 | tf_op jit(solution)/shard_map/ppermute | solution.py:634
  13.1 0.8 collective-permute-start.21
  13.9 0.6 pad_add_fusion.2.source_ref
  14.5 11.6 %collective-permute-done.20.rest_4_.rest_1_ = bf16[128,2048]{1,0:T(8,128)(2,1)S(1)} collective-permute-done((bf16[128,2048]{1,0:T(8,128)(2,1)}, bf16[128,2048]{1,0:T(8,128)(2,1)S(1)}, u32[]{:S(2)}, u32[]{:S(2)}) %collective-permute-start.20) | collective-permute-done | bytes 524320 | tf_op jit(solution)/shard_map/ppermute | solution.py:634
  26.1 0.8 copy-done.1
  26.9 1.3 copy-done.15
  28.2 14.5 %shard_map.113.rest_1_.rest_4_ = f32[480,2048]{1,0:T(8,128)} custom-call(s32[2]{0:T(128)} %pad_add_fusion.2.source_ref, bf16[480,2048]{1,0:T(8,128)(2,1)} %get-tuple-element.148.rest_0_, bf16[480,2048]{1,0:T(8,128)(2,1)} %copy-done.15, bf16[2048,8192]{1,0:T(8,128)(2,1)} %rest_3_.1, bf16[2048,8192]{1,0:T(8,128)(2,1)} %rest_3_.1, bf16[128,2048]{1,0:T(8,128)(2,1)} %copy-done.1), custom_call_target="tpu_custom_call" | custom-call | flops 1000000 | bytes 100000 | tf_op jit(solution)/shard_map/pallas_call | solution.py:258
  42.8 0.8 copy-done.3
  43.5 4.3 %shard_map.114 = (bf16[120,2048]{1,0:T(8,128)(2,1)}, bf16[120,2048]{1,0:T(8,128)(2,1)}, bf16[120,2048]{1,0:T(8,128)(2,1)}, bf16[120,2048]{1,0:T(8,128)(2,1)}, bf16[480,480]{1,0:T(8,128)(2,1)}) custom-call(bf16[480,480]{1,0:T(8,128)(2,1)} %get-tuple-element.146.hot_ref, bf16[480,2048]{1,0:T(8,128)(2,1)} %bitcast.14, bf16[128,2048]{1,0:T(8,128)(2,1)} %copy-done.3, ...), custom_call_target="tpu_custom_call" | custom-call | flops 1000000 | bytes 100000 | tf_op jit(solution)/shard_map/pallas_call | solution.py:220
  47.9 23.2 %collective-permute-start.23 = (bf16[120,2048]{1,0:T(8,128)(2,1)}, bf16[120,2048]{1,0:T(8,128)(2,1)}, u32[]{:S(2)}, u32[]{:S(2)}) collective-permute-start(bf16[120,2048]{1,0:T(8,128)(2,1)} %get-tuple-element.156), channel_id=1, source_target_pairs={{0,8},{4,12},{8,0},{12,4},{1,9},{5,13},{9,1},{13,5},{2,10},{6,14},... | collective-permute-start | bytes 1474568 | tf_op jit(solution)/shard_map/ppermute | solution.py:634
  71.1 1.3 slice.3
  73.0 0.1 collective-permute-start.22
  73.1 3.8 %collective-permute-start.24 = (bf16[120,2048]{1,0:T(8,128)(2,1)}, bf16[120,2048]{1,0:T(8,128)(2,1)}, u32[]{:S(2)}, u32[]{:S(2)}) collective-permute-start(bf16[120,2048]{1,0:T(8,128)(2,1)} %get-tuple-element.157), channel_id=1, source_target_pairs={{0,12},{4,0},{8,4},{12,8},{1,13},{5,1},{9,5},{13,9},{2,14},{6,2},{... | collective-permute-start | bytes 1474568 | tf_op jit(solution)/shard_map/ppermute | solution.py:634
  76.9 2.2 %copy-done = bf16[8,128,2048]{2,1,0:T(8,128)(2,1)S(1)} copy-done((bf16[8,128,2048]{2,1,0:T(8,128)(2,1)S(1)}, bf16[8,128,2048]{2,1,0:T(8,128)(2,1)}, u32[]{:S(2)}) %copy-start) | copy-done | bytes 4194328
  79.1 1.0 copy-done.4
  80.2 4.5 %shard_map.115 = (f32[480,128]{1,0:T(8,128)S(1)}, f32[480,128]{1,0:T(8,128)S(1)}, f32[480,128]{1,0:T(8,128)S(1)}, bf16[480,2048]{1,0:T(8,128)(2,1)}) custom-call(bf16[8,128,2048]{2,1,0:T(8,128)(2,1)S(1)} %copy-done, bf16[128,2048]{1,0:T(8,128)(2,1)S(1)} %copy-done.5, bf16[128,2048]{1,0:T(8,128)(2,1)S(1)} %copy-done.2, ...), custom_call_target="tpu_custom_call" | custom-call | flops 1000000 | bytes 100000 | tf_op jit(solution)/shard_map/pallas_call | solution.py:335
  84.7 13.8 %conditional.2 = ((bf16[120,2048]{1,0:T(8,128)(2,1)S(1)}, bf16[120,2048]{1,0:T(8,128)(2,1)}, bf16[120,2048]{1,0:T(8,128)(2,1)}, bf16[120,2048]{1,0:T(8,128)(2,1)S(1)}, bf16[480,1024]{1,0:T(8,128)(2,1)S(1)})) conditional(s32[]{:T(128)} %bitcast.6, (f32[480,128]{1,0:T(8,128)S(1)}, f32[480,128]{1,0:T(8,128)S(1)}, f32[480,128]{1,0:T(8,128)S(1)}, ...), branch_computations={%region_0.1_spmd, %region_1.2_spmd} | conditional | flops 1061440 | bytes 2803448 | solution.py:674
  84.7 1.5 collective-permute-done.2
  86.2 0.6 collective-permute-start.3
  86.8 7.5 %collective-permute-done.3.other_ref = f32[480,128]{1,0:T(8,128)S(1)} collective-permute-done((f32[480,128]{1,0:T(8,128)S(1)}, f32[480,128]{1,0:T(8,128)S(1)}, u32[]{:S(2)}, u32[]{:S(2)}) %collective-permute-start.3) | collective-permute-done | bytes 245792 | tf_op jit(solution)/shard_map/cond/branch_1_fun/ppermute | solution.py:579
  94.3 4.2 %branch_1_fun.5 = (bf16[120,2048]{1,0:T(8,128)(2,1)S(1)}, bf16[120,2048]{1,0:T(8,128)(2,1)}, bf16[120,2048]{1,0:T(8,128)(2,1)}, bf16[120,2048]{1,0:T(8,128)(2,1)S(1)}, bf16[480,1024]{1,0:T(8,128)(2,1)S(1)}) custom-call(f32[480,128]{1,0:T(8,128)S(1)} %add.13.mine_ref, f32[480,128]{1,0:T(8,128)S(1)} %collective-permute-done.3.other_ref, ...), custom_call_target="tpu_custom_call" | custom-call | flops 1000000 | bytes 100000 | tf_op jit(solution)/shard_map/cond/branch_1_fun/pallas_call | solution.py:444
  98.5 0.8 copy-done.14
  99.3 0.0 collective-permute-start.26
  99.3 0.7 copy-done.16
  100.1 1.3 collective-permute-start.28
  101.4 46.5 %conditional.3 = (bf16[8,2048,128]{2,1,0:T(8,128)(2,1)}, bf16[8,128,2048]{2,1,0:T(8,128)(2,1)}, f32[480,2048]{1,0:T(8,128)S(1)}) conditional(s32[]{:T(128)} %bitcast.6, (f32[480,128]{1,0:T(8,128)S(1)}, bf16[8,2048,128]{2,1,0:T(8,128)(2,1)}, bf16[120,2048]{1,0:T(8,128)(2,1)}, bf16[120,2048]{1,0:T(8,128)(2,1)}, bf16[120,2048]{1,0:T(8,128)(2,1)}, ...), branch_computations={%region_2.3_spmd, %region_3.4_spmd} | conditional | flops 4065539 | bytes 66133052 | solution.py:684
  101.8 0.1 collective-permute-start.13
  101.9 4.9 %branch_1_fun.6 = (f32[480,128]{1,0:T(8,128)S(1)}, bf16[480,2048]{1,0:T(8,128)(2,1)S(1)}) custom-call(f32[480,128]{1,0:T(8,128)S(1)} %get-tuple-element.96.pick_ref, bf16[8,2048,128]{2,1,0:T(8,128)(2,1)} %get-tuple-element.97.table_ref, bf16[120,2048]{1,0:T(8,128)(2,1)} %get-tuple-element.98.rest_0_, bf16[120,2048]{1,0:T(8,128)(2,1)} %get-tuple-element.99.rest_1_, ...), custom_call_target="tpu_custom_call" | custom-call | flops 1000000 | bytes 100000 | tf_op jit(solution)/shard_map/cond/branch_1_fun/pallas_call | solution.py:394
  106.8 0.5 collective-permute-start.11
  107.3 1.1 collective-permute-done.11
  108.5 0.6 collective-permute-start.12
  109.1 0.1 pad_add_fusion.1.source_ref
  109.2 12.8 %branch_1_fun.7.rest_0_ = f32[480,2048]{1,0:T(8,128)S(1)} custom-call(s32[2]{0:T(128)S(1)} %pad_add_fusion.1.source_ref, bf16[480,2048]{1,0:T(8,128)(2,1)} %get-tuple-element.108.rest_0_, bf16[480,2048]{1,0:T(8,128)(2,1)S(1)} %collective-permute-done.13.rest_1_, bf16[2048,8192]{1,0:T(8,128)(2,1)} %get-tuple-element.109.rest_2_.rest_3_, ...), custom_call_target="tpu_custom_call" | custom-call | flops 1000000 | bytes 100000 | tf_op jit(solution)/shard_map/cond/branch_1_fun/pallas_call | solution.py:258
  122.1 6.4 %branch_1_fun.8 = (f32[8,2048,128]{2,1,0:T(8,128)S(1)}, f32[8,128,2048]{2,1,0:T(8,128)S(1)}, f32[8,128]{1,0:T(8,128)S(1)}) custom-call(f32[480,128]{1,0:T(8,128)S(1)} %add.15.mine_ref, f32[480,128]{1,0:T(8,128)S(1)} %collective-permute-done.12.other_ref, f32[480,128]{1,0:T(8,128)S(1)} %get-tuple-element.104.lane_ref, ...), custom_call_target="tpu_custom_call" | custom-call | flops 1000000 | bytes 100000 | tf_op jit(solution)/shard_map/cond/branch_1_fun/pallas_call | solution.py:503
  128.5 0.1 collective-permute-start.14
  128.7 1.1 collective-permute-done.14
  129.8 1.5 collective-permute-start.15
  131.3 2.1 %collective-permute-done.15 = f32[8,128]{1,0:T(8,128)S(1)} collective-permute-done((f32[8,128]{1,0:T(8,128)S(1)}, f32[8,128]{1,0:T(8,128)S(1)}, u32[]{:S(2)}, u32[]{:S(2)}) %collective-permute-start.15) | collective-permute-done | bytes 4128 | tf_op jit(solution)/shard_map/cond/branch_1_fun/ppermute | solution.py:579
  133.4 2.2 %collective-permute-start.16 = (f32[8,128]{1,0:T(8,128)S(1)}, f32[8,128]{1,0:T(8,128)S(1)}, u32[]{:S(2)}, u32[]{:S(2)}) collective-permute-start(f32[8,128]{1,0:T(8,128)S(1)} %max.21), channel_id=1, source_target_pairs={{0,4},{4,0},{8,12},{12,8},{1,5},{5,1},{9,13},{13,9},{2,6},{6,2},{1... | collective-permute-start | bytes 12296 | tf_op jit(solution)/shard_map/cond/branch_1_fun/ppermute | solution.py:579
  135.6 1.9 %collective-permute-done.16 = f32[8,128]{1,0:T(8,128)S(1)} collective-permute-done((f32[8,128]{1,0:T(8,128)S(1)}, f32[8,128]{1,0:T(8,128)S(1)}, u32[]{:S(2)}, u32[]{:S(2)}) %collective-permute-start.16) | collective-permute-done | bytes 4128 | tf_op jit(solution)/shard_map/cond/branch_1_fun/ppermute | solution.py:579
  137.5 2.4 %collective-permute-start.17 = (f32[8,128]{1,0:T(8,128)S(1)}, f32[8,128]{1,0:T(8,128)S(1)}, u32[]{:S(2)}, u32[]{:S(2)}) collective-permute-start(f32[8,128]{1,0:T(8,128)S(1)} %max.22), channel_id=1, source_target_pairs={{0,8},{4,12},{8,0},{12,4},{1,9},{5,13},{9,1},{13,5},{2,10},{6,14},... | collective-permute-start | bytes 12296 | tf_op jit(solution)/shard_map/cond/branch_1_fun/ppermute | solution.py:579
  139.9 3.7 %collective-permute-done.17 = f32[8,128]{1,0:T(8,128)S(1)} collective-permute-done((f32[8,128]{1,0:T(8,128)S(1)}, f32[8,128]{1,0:T(8,128)S(1)}, u32[]{:S(2)}, u32[]{:S(2)}) %collective-permute-start.17) | collective-permute-done | bytes 4128 | tf_op jit(solution)/shard_map/cond/branch_1_fun/ppermute | solution.py:579
  143.6 4.3 %branch_1_fun.9 = (bf16[8,2048,128]{2,1,0:T(8,128)(2,1)}, bf16[8,128,2048]{2,1,0:T(8,128)(2,1)}) custom-call(f32[8,128]{1,0:T(8,128)S(1)} %max.23.largest_ref, f32[8,2048,128]{2,1,0:T(8,128)S(1)} %get-tuple-element.112.down_ref, f32[8,128,2048]{2,1,0:T(8,128)S(1)} %get-tuple-element.113.up_ref), custom_call_target="tpu_custom_call" | custom-call | flops 1000000 | bytes 100000 | tf_op jit(solution)/shard_map/cond/branch_1_fun/pallas_call | solution.py:537
  148.0 3.6 %shard_map.117 = bf16[480,2048]{1,0:T(8,128)(2,1)} custom-call(bf16[480,480]{1,0:T(8,128)(2,1)S(1)} %copy-done.6, f32[480,2048]{1,0:T(8,128)S(1)} %get-tuple-element.162.frozen_ref, bf16[120,2048]{1,0:T(8,128)(2,1)} %copy-done.14, bf16[120,2048]{1,0:T(8,128)(2,1)S(1)} %collective-permute-done.26.rest_1_, ...), custom_call_target="tpu_custom_call" | custom-call | flops 1000000 | bytes 100000 | tf_op jit(solution)/shard_map/pallas_call | solution.py:564
  (44 shorter events, 0.2 us)
Async XLA Ops:
  6.2 19.9 %collective-permute-start.19 = (bf16[480,2048]{1,0:T(8,128)(2,1)}, bf16[480,2048]{1,0:T(8,128)(2,1)S(1)}, u32[]{:S(2)}, u32[]{:S(2)}) collective-permute-start(bf16[480,2048]{1,0:T(8,128)(2,1)} %get-tuple-element.148.rest_0_), channel_id=1, source_target_pairs={{0,1},{1,0},{2,3},{3,2},{4,5},{5,4},{6,7},{7,6},{8,9},{9,8},{10,11... | collective-permute-start | bytes 5898248 | tf_op jit(solution)/shard_map/ppermute | solution.py:579
  6.7 93.3 %collective-permute-start.25 = (bf16[480,2048]{1,0:T(8,128)(2,1)}, bf16[480,2048]{1,0:T(8,128)(2,1)}, u32[]{:S(2)}, u32[]{:S(2)}) collective-permute-start(bf16[480,2048]{1,0:T(8,128)(2,1)} %get-tuple-element.148.rest_0_), channel_id=1, source_target_pairs={{0,2},{1,3},{2,0},{3,1},{4,6},{5,7},{6,4},{7,5},{8,10},{9,11},{10,... | collective-permute-start | bytes 5898248 | tf_op jit(solution)/shard_map/ppermute | solution.py:596
  9.3 16.8 %collective-permute-start.20 = (bf16[128,2048]{1,0:T(8,128)(2,1)}, bf16[128,2048]{1,0:T(8,128)(2,1)S(1)}, u32[]{:S(2)}, u32[]{:S(2)}) collective-permute-start(bf16[128,2048]{1,0:T(8,128)(2,1)} %get-tuple-element.149), channel_id=1, source_target_pairs={{0,4},{4,8},{8,12},{12,0},{1,5},{5,9},{9,13},{13,1},{2,6},{6,10},{... | collective-permute-start | bytes 1572872 | tf_op jit(solution)/shard_map/ppermute | solution.py:634
  10.8 31.9 %collective-permute-start.18 = (bf16[128,2048]{1,0:T(8,128)(2,1)}, bf16[128,2048]{1,0:T(8,128)(2,1)S(1)}, u32[]{:S(2)}, u32[]{:S(2)}) collective-permute-start(bf16[128,2048]{1,0:T(8,128)(2,1)} %get-tuple-element.147), channel_id=1, source_target_pairs={{0,12},{4,0},{8,4},{12,8},{1,13},{5,1},{9,5},{13,9},{2,14},{6,2},{... | collective-permute-start | bytes 1572872 | tf_op jit(solution)/shard_map/ppermute | solution.py:634
  13.1 63.8 %collective-permute-start.21 = (bf16[128,2048]{1,0:T(8,128)(2,1)}, bf16[128,2048]{1,0:T(8,128)(2,1)S(1)}, u32[]{:S(2)}, u32[]{:S(2)}) collective-permute-start(bf16[128,2048]{1,0:T(8,128)(2,1)} %get-tuple-element.152), channel_id=1, source_target_pairs={{0,8},{4,12},{8,0},{12,4},{1,9},{5,13},{9,1},{13,5},{2,10},{6,14},... | collective-permute-start | bytes 1572872 | tf_op jit(solution)/shard_map/ppermute | solution.py:634
  26.1 0.8 copy-start.1
  26.9 1.3 copy-start.15
  42.7 34.2 %copy-start.2 = (bf16[128,2048]{1,0:T(8,128)(2,1)S(1)}, bf16[128,2048]{1,0:T(8,128)(2,1)}, u32[]{:S(2)}) copy-start(bf16[128,2048]{1,0:T(8,128)(2,1)} %copy-done.1) | copy-start | bytes 1572868
  42.7 34.2 %copy-start.5 = (bf16[128,2048]{1,0:T(8,128)(2,1)S(1)}, bf16[128,2048]{1,0:T(8,128)(2,1)}, u32[]{:S(2)}) copy-start(bf16[128,2048]{1,0:T(8,128)(2,1)} %get-tuple-element.151.rest_0_) | copy-start | bytes 1572868
  42.7 0.8 copy-start.3
  47.9 50.6 %collective-permute-start.23 = (bf16[120,2048]{1,0:T(8,128)(2,1)}, bf16[120,2048]{1,0:T(8,128)(2,1)}, u32[]{:S(2)}, u32[]{:S(2)}) collective-permute-start(bf16[120,2048]{1,0:T(8,128)(2,1)} %get-tuple-element.156), channel_id=1, source_target_pairs={{0,8},{4,12},{8,0},{12,4},{1,9},{5,13},{9,1},{13,5},{2,10},{6,14},... | collective-permute-start | bytes 1474568 | tf_op jit(solution)/shard_map/ppermute | solution.py:634
  73.0 28.3 %collective-permute-start.22 = (bf16[120,2048]{1,0:T(8,128)(2,1)}, bf16[120,2048]{1,0:T(8,128)(2,1)}, u32[]{:S(2)}, u32[]{:S(2)}) collective-permute-start(bf16[120,2048]{1,0:T(8,128)(2,1)} %get-tuple-element.155), channel_id=1, source_target_pairs={{0,4},{4,8},{8,12},{12,0},{1,5},{5,9},{9,13},{13,1},{2,6},{6,10},{... | collective-permute-start | bytes 1474568 | tf_op jit(solution)/shard_map/ppermute | solution.py:634
  73.1 28.3 %collective-permute-start.24 = (bf16[120,2048]{1,0:T(8,128)(2,1)}, bf16[120,2048]{1,0:T(8,128)(2,1)}, u32[]{:S(2)}, u32[]{:S(2)}) collective-permute-start(bf16[120,2048]{1,0:T(8,128)(2,1)} %get-tuple-element.157), channel_id=1, source_target_pairs={{0,12},{4,0},{8,4},{12,8},{1,13},{5,1},{9,5},{13,9},{2,14},{6,2},{... | collective-permute-start | bytes 1474568 | tf_op jit(solution)/shard_map/ppermute | solution.py:634
  76.9 2.2 %copy-start = (bf16[8,128,2048]{2,1,0:T(8,128)(2,1)S(1)}, bf16[8,128,2048]{2,1,0:T(8,128)(2,1)}, u32[]{:S(2)}) copy-start(bf16[8,128,2048]{2,1,0:T(8,128)(2,1)} %table_ref.1) | copy-start | bytes 12582916
  79.1 1.0 copy-start.4
  80.2 4.5 %copy-start.9 = (bf16[8,2048,128]{2,1,0:T(8,128)(2,1)S(1)}, bf16[8,2048,128]{2,1,0:T(8,128)(2,1)}, u32[]{:S(2)}) copy-start(bf16[8,2048,128]{2,1,0:T(8,128)(2,1)} %param.16) | copy-start | bytes 12582916
  84.7 1.5 collective-permute-start.2
  86.2 8.1 %collective-permute-start.3 = (f32[480,128]{1,0:T(8,128)S(1)}, f32[480,128]{1,0:T(8,128)S(1)}, u32[]{:S(2)}, u32[]{:S(2)}) collective-permute-start(f32[480,128]{1,0:T(8,128)S(1)} %add.13.mine_ref), channel_id=1, source_target_pairs={{0,2},{1,3},{2,0},{3,1},{4,6},{5,7},{6,4},{7,5},{8,10},{9,11},{10,... | collective-permute-start | bytes 737288 | tf_op jit(solution)/shard_map/cond/branch_1_fun/ppermute | solution.py:579
  98.5 0.8 copy-start.14
  99.3 0.8 copy-start.16
  99.3 48.6 %collective-permute-start.26 = (bf16[120,2048]{1,0:T(8,128)(2,1)}, bf16[120,2048]{1,0:T(8,128)(2,1)S(1)}, u32[]{:S(2)}, u32[]{:S(2)}) collective-permute-start(bf16[120,2048]{1,0:T(8,128)(2,1)} %get-tuple-element.168), channel_id=1, source_target_pairs={{0,12},{4,0},{8,4},{12,8},{1,13},{5,1},{9,5},{13,9},{2,14},{6,2},{... | collective-permute-start | bytes 1474568 | tf_op jit(solution)/shard_map/ppermute | solution.py:634
  100.1 47.9 %collective-permute-start.27 = (bf16[120,2048]{1,0:T(8,128)(2,1)}, bf16[120,2048]{1,0:T(8,128)(2,1)S(1)}, u32[]{:S(2)}, u32[]{:S(2)}) collective-permute-start(bf16[120,2048]{1,0:T(8,128)(2,1)} %get-tuple-element.169), channel_id=1, source_target_pairs={{0,8},{4,12},{8,0},{12,4},{1,9},{5,13},{9,1},{13,5},{2,10},{6,14},... | collective-permute-start | bytes 1474568 | tf_op jit(solution)/shard_map/ppermute | solution.py:634
  100.1 47.9 %collective-permute-start.28 = (bf16[120,2048]{1,0:T(8,128)(2,1)}, bf16[120,2048]{1,0:T(8,128)(2,1)S(1)}, u32[]{:S(2)}, u32[]{:S(2)}) collective-permute-start(bf16[120,2048]{1,0:T(8,128)(2,1)} %copy-done.16), channel_id=1, source_target_pairs={{0,4},{4,8},{8,12},{12,0},{1,5},{5,9},{9,13},{13,1},{2,6},{6,10},{... | collective-permute-start | bytes 1474568 | tf_op jit(solution)/shard_map/ppermute | solution.py:634
  101.4 46.6 %copy-start.6 = (bf16[480,480]{1,0:T(8,128)(2,1)S(1)}, bf16[480,480]{1,0:T(8,128)(2,1)}, u32[]{:S(2)}) copy-start(bf16[480,480]{1,0:T(8,128)(2,1)} %get-tuple-element.150.hot_ref) | copy-start | bytes 1382404
  101.8 7.4 %collective-permute-start.13 = (bf16[480,2048]{1,0:T(8,128)(2,1)}, bf16[480,2048]{1,0:T(8,128)(2,1)S(1)}, u32[]{:S(2)}, u32[]{:S(2)}) collective-permute-start(bf16[480,2048]{1,0:T(8,128)(2,1)} %get-tuple-element.108.rest_0_), channel_id=1, source_target_pairs={{0,1},{1,0},{2,3},{3,2},{4,5},{5,4},{6,7},{7,6},{8,9},{9,8},{10,11... | collective-permute-start | bytes 5898248 | tf_op jit(solution)/shard_map/cond/branch_1_fun/ppermute | solution.py:579
  101.9 7.3 %copy-start.8 = (f32[480,2048]{1,0:T(8,128)S(1)}, f32[480,2048]{1,0:T(8,128)}, u32[]{:S(2)}) copy-start(f32[480,2048]{1,0:T(8,128)} %get-tuple-element.110.rest_4_) | copy-start | bytes 11796484 | tf_op jit(solution)/shard_map/cond
  106.8 1.7 %collective-permute-start.11 = (f32[480,128]{1,0:T(8,128)S(1)}, f32[480,128]{1,0:T(8,128)S(1)}, u32[]{:S(2)}, u32[]{:S(2)}) collective-permute-start(f32[480,128]{1,0:T(8,128)S(1)} %get-tuple-element.103.rest_5_), channel_id=1, source_target_pairs={{0,1},{1,0},{2,3},{3,2},{4,5},{5,4},{6,7},{7,6},{8,9},{9,8},{10,11... | collective-permute-start | bytes 737288 | tf_op jit(solution)/shard_map/cond/branch_1_fun/ppermute | solution.py:579
  108.5 13.6 %collective-permute-start.12 = (f32[480,128]{1,0:T(8,128)S(1)}, f32[480,128]{1,0:T(8,128)S(1)}, u32[]{:S(2)}, u32[]{:S(2)}) collective-permute-start(f32[480,128]{1,0:T(8,128)S(1)} %add.15.mine_ref), channel_id=1, source_target_pairs={{0,2},{1,3},{2,0},{3,1},{4,6},{5,7},{6,4},{7,5},{8,10},{9,11},{10,... | collective-permute-start | bytes 737288 | tf_op jit(solution)/shard_map/cond/branch_1_fun/ppermute | solution.py:579
  109.2 12.9 %copy-start.13 = (bf16[480,2048]{1,0:T(8,128)(2,1)S(1)}, bf16[480,2048]{1,0:T(8,128)(2,1)}, u32[]{:S(2)}) copy-start(bf16[480,2048]{1,0:T(8,128)(2,1)} %get-tuple-element.106.masked_ref) | copy-start | bytes 5898244 | tf_op jit(solution)/shard_map/cond
  122.1 6.5 %copy-start.10 = (f32[480,2048]{1,0:T(8,128)}, f32[480,2048]{1,0:T(8,128)S(1)}, u32[]{:S(2)}) copy-start(f32[480,2048]{1,0:T(8,128)S(1)} %branch_1_fun.7.rest_0_) | copy-start | bytes 11796484 | tf_op jit(solution)/shard_map/cond
  128.5 1.2 collective-permute-start.14
  129.8 3.6 %collective-permute-start.15 = (f32[8,128]{1,0:T(8,128)S(1)}, f32[8,128]{1,0:T(8,128)S(1)}, u32[]{:S(2)}, u32[]{:S(2)}) collective-permute-start(f32[8,128]{1,0:T(8,128)S(1)} %max.20), channel_id=1, source_target_pairs={{0,2},{1,3},{2,0},{3,1},{4,6},{5,7},{6,4},{7,5},{8,10},{9,11},{10,... | collective-permute-start | bytes 12296 | tf_op jit(solution)/shard_map/cond/branch_1_fun/ppermute | solution.py:579
  133.4 4.1 %collective-permute-start.16 = (f32[8,128]{1,0:T(8,128)S(1)}, f32[8,128]{1,0:T(8,128)S(1)}, u32[]{:S(2)}, u32[]{:S(2)}) collective-permute-start(f32[8,128]{1,0:T(8,128)S(1)} %max.21), channel_id=1, source_target_pairs={{0,4},{4,0},{8,12},{12,8},{1,5},{5,1},{9,13},{13,9},{2,6},{6,2},{1... | collective-permute-start | bytes 12296 | tf_op jit(solution)/shard_map/cond/branch_1_fun/ppermute | solution.py:579
  137.5 6.1 %collective-permute-start.17 = (f32[8,128]{1,0:T(8,128)S(1)}, f32[8,128]{1,0:T(8,128)S(1)}, u32[]{:S(2)}, u32[]{:S(2)}) collective-permute-start(f32[8,128]{1,0:T(8,128)S(1)} %max.22), channel_id=1, source_target_pairs={{0,8},{4,12},{8,0},{12,4},{1,9},{5,13},{9,1},{13,5},{2,10},{6,14},... | collective-permute-start | bytes 12296 | tf_op jit(solution)/shard_map/cond/branch_1_fun/ppermute | solution.py:579
  143.6 4.3 %copy-start.11 = (f32[480,2048]{1,0:T(8,128)S(1)}, f32[480,2048]{1,0:T(8,128)}, u32[]{:S(2)}) copy-start(f32[480,2048]{1,0:T(8,128)} %copy-done.10) | copy-start | bytes 11796484 | tf_op jit(solution)/shard_map/cond
